TPU v7x, 256 devices: a whole 4x4x8 slice. The times are simulated.
256 devices in a mesh: fluid: 64 (over z, x, core), sect: 4 (over y).
Axes of the slice: x: 4, y: 4, z: 8, core: 2. Of those that a mesh axis runs over, the one named last changes fastest.
Arguments:
- density: float32 [256, 256, 128], P('fluid', 'sect'), may hold values from 0.6 to 1.8
- velocity: float32 [3, 256, 256, 128], P(None, 'fluid', 'sect'), may hold values from -3 to 3
- pressure: float32 [256, 256, 128], P('fluid', 'sect'), may hold values from 0.6 to 3
- deck_disp: float32 [4096, 512], P('fluid', 'sect'), may hold values from -4 to 4
- deck_prev: float32 [4096, 512], P('fluid', 'sect'), may hold values from -4 to 4
- stay_stiff: float32 [168], replicated, may hold values from 0.5 to 4
- stay_tension: float32 [168], replicated, may hold values from 1 to 4
- anchor_node: int32 [168], replicated, may hold values from 0 to 2097151, as said below
- failed_stay: int32 [1], replicated, may hold values from 0 to 167
- facet_cells: int32 [32768, 128], P(('fluid', 'sect')), may hold values from 0 to 255
- facet_owner: int32 [32768, 1], P(('fluid', 'sect')), may hold values from 0 to 63; in each aligned block of 128 rows (0 to 127, 128 to 255, ...) at most 2 rows name the same one
- facet_row: int32 [32768], P(('fluid', 'sect')), may hold values from 0 to 63
- facet_count: int32 [256], P(('fluid', 'sect')), may hold values from 1 to 128, 13107 in all
Outputs:
- fields: float32 [5, 256, 256, 128], P(None, 'fluid', 'sect')
- deck_next: float32 [4096, 512], P('fluid', 'sect')
- facet_disp: float32 [32768, 128], P(('fluid', 'sect'))
Inputs may be any that keep to these rules, and one draw needn't show every extreme that they name: `facet_owner`: among the 128 slots of one device every owner index appears exactly 2 times. `facet_count`: the slots below a device's count are live; the counts of all devices sum to 13107. `anchor_node`: distinct deck nodes, numbered row by row over the 4096 x 512 deck.
All inputs are finite; a program needn't handle non-finite values.
Results may differ from a plain program's by a relative error of at most 0.000071.
Values sent between devices are 32-bit elements; how exact they have to be, the bound alone decides.
No kernel may reach another device: no remote copies, remote signals or barrier semaphores. Data moves between devices by JAX's collectives and lax.ppermute only.
A program may use at most 64 MiB of HBM per device.

v0:
```python
import jax
import jax.numpy as jnp
from jax import lax
from jax.experimental import pallas as pl
from jax.experimental.pallas import tpu as pltpu
from jax.sharding import PartitionSpec as P

SSTEPS = 2


STEP_FLUID = 0.045
STEP_DECK = 0.06
GAMMA_LESS = 0.4
AMBIENT = 1.0
SLOT_GROUP = 16


def with_halo(cells, sides, width, closed):
    for axis, dim in sides:
        count = lax.axis_size(axis)
        ends = count if closed else count - 1
        head = lax.slice_in_dim(cells, 0, width, axis=dim)
        tail = lax.slice_in_dim(cells, cells.shape[dim] - width, cells.shape[dim], axis=dim)
        cells = jnp.concatenate(
            [
                lax.ppermute(tail, axis, [(i, (i + 1) % count) for i in range(ends)]),
                cells,
                lax.ppermute(head, axis, [((i + 1) % count, i) for i in range(ends)]),
            ],
            axis=dim,
        )
    return cells


YOFF = 8
YROWS = 80
KFL = 0.5 * STEP_FLUID


def euler_prims(rho, m1, m2, m3, en):
    inv = 1.0 / rho
    v1, v2, v3 = m1 * inv, m2 * inv, m3 * inv
    p = GAMMA_LESS * (en - 0.5 * (m1 * v1 + m2 * v2 + m3 * v3))
    return v1, v2, v3, p, jnp.sqrt(1.4 * p * inv)


def from_raw(rho, v1, v2, v3, p):
    en = p * (1.0 / GAMMA_LESS) + 0.5 * rho * (v1 * v1 + v2 * v2 + v3 * v3)
    return (rho, rho * v1, rho * v2, rho * v3, en), (v1, v2, v3, p, jnp.sqrt(1.4 * p / rho))


def flux(state, prim, d):
    rho, m1, m2, m3, en = state
    v, p = prim[d], prim[3]
    out = [state[1 + d], m1 * v, m2 * v, m3 * v, (en + p) * v]
    out[1 + d] = out[1 + d] + p
    return out


def add_direction(acc, here, prim, up, uprim, down, dprim, d):
    fu, fd = flux(up, uprim, d), flux(down, dprim, d)
    s0 = jnp.abs(prim[d]) + prim[4]
    lu = jnp.maximum(s0, jnp.abs(uprim[d]) + uprim[4])
    ld = jnp.maximum(s0, jnp.abs(dprim[d]) + dprim[4])
    out = []
    for c in range(5):
        term = (fu[c] - fd[c]) - lu * (up[c] - here[c]) + ld * (here[c] - down[c])
        out.append(term if acc is None else acc[c] + term)
    return out


def bulk_kernel(rho_ref, vel_ref, pre_ref, xlo_ref, xhi_ref, ylo_ref, yhi_ref, out_ref, ua, pa, ub, pb):
    lane = lax.broadcasted_iota(jnp.int32, (8, 128), 1)
    first, last = lane == 0, lane == 127

    def put(planes, rows, raw):
        state, prim = from_raw(*raw)
        for c in range(5):
            ua[c, planes, rows, :] = state[c]
            pa[c, planes, rows, :] = prim[c]

    def own(i, _):
        for r in range(0, 64, 8):
            rows = pl.ds(r, 8)
            put(i + 2, pl.ds(r + YOFF, 8), (rho_ref[i, rows, :], vel_ref[0, i, rows, :], vel_ref[1, i, rows, :], vel_ref[2, i, rows, :], pre_ref[i, rows, :]))
        put(i + 2, pl.ds(YOFF - 2, 2), [ylo_ref[c, i] for c in range(5)])
        put(i + 2, pl.ds(YOFF + 64, 2), [yhi_ref[c, i] for c in range(5)])
        return 0

    lax.fori_loop(0, 4, own, 0)

    def halo(i, _):
        for ref, base in ((xlo_ref, 0), (xhi_ref, 6)):
            for r in range(0, 64, 8):
                put(base + i, pl.ds(r + YOFF, 8), [ref[c, i, pl.ds(r, 8), :] for c in range(5)])
            put(base + i, pl.ds(YOFF + 64, 2), [ref[c, i, pl.ds(64, 2), :] for c in range(5)])
            put(base + i, pl.ds(YOFF - 2, 2), [ref[c, i, pl.ds(66, 2), :] for c in range(5)])
        return 0

    lax.fori_loop(0, 2, halo, 0)

    def update(u, q, i, r, n):
        def load(plane, row):
            rows = pl.ds(row, n)
            return [u[c, plane, rows, :] for c in range(5)], [q[c, plane, rows, :] for c in range(5)]

        here, prim = load(i, r)
        acc = None
        for d, (up, down) in enumerate((((i + 1, r), (i - 1, r)), ((i, r + 1), (i, r - 1)))):
            uu, uq = load(*up)
            du, dq = load(*down)
            acc = add_direction(acc, here, prim, uu, uq, du, dq, d)

        def shifted(x, sign, step, edge):
            return jnp.where(edge[:n], sign * x if sign < 0 else x, pltpu.roll(x, step, 1))

        signs = (1, 1, 1, -1, 1)
        qsigns = (None, None, -1, 1, 1)
        zu = [shifted(here[c], signs[c], 127, last) for c in range(5)]
        zd = [shifted(here[c], signs[c], 1, first) for c in range(5)]
        zuq = [None if qsigns[c] is None else shifted(prim[c], qsigns[c], 127, last) for c in range(5)]
        zdq = [None if qsigns[c] is None else shifted(prim[c], qsigns[c], 1, first) for c in range(5)]
        acc = add_direction(acc, here, prim, zu, zuq, zd, zdq, 2)
        return [here[c] - KFL * acc[c] for c in range(5)]

    def step_one(i, _):
        for r, n in [(YOFF - 8, 8)] + [(YOFF + k, 8) for k in range(0, 72, 8)]:
            if r == YOFF - 8:
                r, n = YOFF - 1, 1
            if r == YOFF + 64:
                n = 1
            new = update(ua, pa, i, r, n)
            prim = euler_prims(*new)
            for c in range(5):
                ub[c, i, pl.ds(r, n), :] = new[c]
                pb[c, i, pl.ds(r, n), :] = prim[c]
        return 0

    lax.fori_loop(1, 7, step_one, 0)

    def step_two(i, _):
        for r in range(0, 64, 8):
            new = update(ub, pb, i + 2, r + YOFF, 8)
            for c in range(5):
                out_ref[c, i, pl.ds(r, 8), :] = new[c]
        return 0

    lax.fori_loop(0, 4, step_two, 0)


def bulk_euler(density, velocity, pressure, xlo, xhi, ylo, yhi):
    vm = pl.BlockSpec(memory_space=pltpu.VMEM)
    return pl.pallas_call(
        bulk_kernel,
        out_shape=jax.ShapeDtypeStruct((5, 4, 64, 128), jnp.float32),
        in_specs=[vm] * 7,
        out_specs=vm,
        scratch_shapes=[pltpu.VMEM((5, 8, YROWS, 128), jnp.float32)] * 4,
        compiler_params=pltpu.CompilerParams(vmem_limit_bytes=32 * 1024 * 1024),
        cost_estimate=pl.CostEstimate(flops=60_000_000, bytes_accessed=3_000_000, transcendentals=100_000),
        name="bulk_euler",
    )(density, velocity, pressure, xlo, xhi, ylo, yhi)


def pressure_of(fields):
    kinetic = (
        0.5 * (fields[1] * fields[1] + fields[2] * fields[2] + fields[3] * fields[3]) / fields[0]
    )
    return GAMMA_LESS * (fields[4] - kinetic)


def laplace(field):
    return (
        field[2:, 1:-1]
        + field[:-2, 1:-1]
        + field[1:-1, 2:]
        + field[1:-1, :-2]
        - 4.0 * field[1:-1, 1:-1]
    )


def pick_rows(selector, table):
    return jnp.dot(selector, table, precision=lax.Precision.HIGHEST)


def body(
    density,
    velocity,
    pressure,
    deck_disp,
    deck_prev,
    stay_stiff,
    stay_tension,
    anchor_node,
    failed_stay,
    facet_cells,
    facet_owner,
    facet_row,
    facet_count,
):
    raw = jnp.concatenate([density[None], velocity, pressure[None]], axis=0)
    around = [(i, (i + 1) % 4) for i in range(4)]
    back = [(i, (i - 1) % 4) for i in range(4)]
    ylo = lax.ppermute(raw[:, :, 62:], "sect", around)
    yhi = lax.ppermute(raw[:, :, :2], "sect", back)
    wide = jnp.concatenate([raw, yhi, ylo, jnp.ones((5, 4, 4, 128), jnp.float32)], axis=2)
    count = lax.axis_size("fluid")
    xlo = lax.ppermute(wide[:, 2:], "fluid", [(i, (i + 1) % count) for i in range(count)])
    xhi = lax.ppermute(wide[:, :2], "fluid", [(i, (i - 1) % count) for i in range(count)])
    fields = bulk_euler(density, velocity, pressure, xlo, xhi, ylo, yhi)
    pressure_flat = pressure_of(fields[:, :, :, 0]).reshape(-1)
    cell_ids = jnp.arange(pressure_flat.shape[0], dtype=jnp.int32)
    slot_count, block_width = facet_cells.shape
    fluid_count = lax.axis_size("fluid")
    capacity = slot_count // fluid_count

    def sample_group(group_cells):
        flat_ids = group_cells.reshape(-1)
        picker = (flat_ids[:, None] == cell_ids[None, :]).astype(jnp.float32)
        return pick_rows(picker, pressure_flat).reshape(group_cells.shape)

    grouped = facet_cells.reshape(slot_count // SLOT_GROUP, SLOT_GROUP, block_width)
    samples = lax.map(sample_group, grouped).reshape(slot_count, block_width)
    alive_slot = jnp.arange(slot_count, dtype=jnp.int32) < facet_count[0]
    values = jnp.where(alive_slot[:, None], samples - AMBIENT, jnp.zeros_like(samples))
    owners = facet_owner[:, 0]
    matches = (owners[:, None] == jnp.arange(fluid_count, dtype=jnp.int32)[None, :]).astype(
        jnp.int32
    )
    earlier = jnp.cumsum(matches, axis=0) - matches
    within = jnp.sum(earlier * matches, axis=1)
    position = owners * capacity + within
    placement = (position[:, None] == jnp.arange(slot_count, dtype=jnp.int32)[None, :]).astype(
        jnp.float32
    )
    packed = pick_rows(placement.T, values).reshape(fluid_count, capacity, block_width)
    row_packed = pick_rows(placement.T, facet_row.astype(jnp.float32)).reshape(
        fluid_count, capacity, 1
    )
    got_values, got_rows = (
        lax.all_to_all(packed, "fluid", split_axis=0, concat_axis=0, tiled=True),
        lax.all_to_all(row_packed, "fluid", split_axis=0, concat_axis=0, tiled=True),
    )
    rows_tile, width_tile = deck_disp.shape
    got_index = got_rows.reshape(-1).astype(jnp.int32)
    selector_rows = (got_index[:, None] == jnp.arange(rows_tile, dtype=jnp.int32)[None, :]).astype(
        jnp.float32
    )
    deck_load = pick_rows(selector_rows.T, got_values.reshape(-1, block_width))
    fluid_index = lax.axis_index("fluid")
    sect_index = lax.axis_index("sect")
    deck_width = width_tile * lax.axis_size("sect")
    anchor_row = anchor_node // deck_width
    anchor_col = anchor_node % deck_width
    inside = (anchor_row // rows_tile == fluid_index) & (anchor_col // width_tile == sect_index)
    local_node = (anchor_row - fluid_index * rows_tile) * width_tile + (
        anchor_col - sect_index * width_tile
    )
    node_ids = jnp.arange(rows_tile * width_tile, dtype=jnp.int32)
    selector_stay = ((local_node[:, None] == node_ids[None, :]) & inside[:, None]).astype(
        jnp.float32
    )
    alive_stay = (jnp.arange(stay_stiff.shape[0], dtype=jnp.int32) != failed_stay[0]).astype(
        jnp.float32
    )
    current = deck_disp
    previous = deck_prev
    for substep in range(SSTEPS):
        padded_deck = with_halo(current, (("fluid", 0), ("sect", 1)), 2, False)
        bending = laplace(laplace(padded_deck))
        anchored = pick_rows(selector_stay, current.reshape(-1))
        stay_force = alive_stay * (stay_tension - stay_stiff * anchored)
        force_field = pick_rows(stay_force, selector_stay).reshape(rows_tile, width_tile)
        following = 2.0 * current - previous + STEP_DECK * (deck_load + force_field - bending)
        previous = current
        current = following
    outgoing = pick_rows(selector_rows, current).reshape(fluid_count, capacity, block_width)
    incoming = lax.all_to_all(outgoing, "fluid", split_axis=0, concat_axis=0, tiled=True)
    returned = pick_rows(placement, incoming.reshape(slot_count, block_width))
    facet_disp = jnp.where(alive_slot[:, None], returned, jnp.zeros_like(returned))
    return (fields, current, facet_disp)


def solution(mesh):
    return jax.shard_map(
        body,
        mesh=mesh,
        in_specs=(
            P("fluid", "sect", None),
            P(None, "fluid", "sect", None),
            P("fluid", "sect", None),
            P("fluid", "sect"),
            P("fluid", "sect"),
            P(),
            P(),
            P(),
            P(),
            P(("fluid", "sect"), None),
            P(("fluid", "sect"), None),
            P(("fluid", "sect")),
            P(("fluid", "sect")),
        ),
        out_specs=(P(None, "fluid", "sect", None), P("fluid", "sect"), P(("fluid", "sect"), None)),
        check_vma=False,
    )
```

profile of v0, /device:TPU:1, one launch (start us, length us, event | category | flops | bytes accessed | tf_op | source)
XLA Modules:
  0.0 122.2 jit_solution(12503526018386891205)
XLA Ops:
  0.7 0.9 pad_maximum_fusion.18
  1.6 2.2 %collective-permute-start.1 = (f32[5,4,2,128]{3,2,1,0:T(2,128)S(1)}, f32[5,4,2,128]{3,2,1,0:T(2,128)S(1)}, u32[]{:S(2)}, u32[]{:S(2)}) collective-permute-start(f32[5,4,2,128]{3,2,1,0:T(2,128)S(1)} %get-tuple-element.54), channel_id=1, source_target_pairs={{0,1},{1,2},{2,3},{3,0},{4,5},{5,6},{6,7},{7,4},{8,9},{9,10},{10,1... | collective-permute-start | bytes 61448 | tf_op jit(solution)/shard_map/ppermute | solution.py:204
  3.8 1.5 %collective-permute-start = (f32[5,4,2,128]{3,2,1,0:T(2,128)S(1)}, f32[5,4,2,128]{3,2,1,0:T(2,128)S(1)}, u32[]{:S(2)}, u32[]{:S(2)}) collective-permute-start(f32[5,4,2,128]{3,2,1,0:T(2,128)S(1)} %get-tuple-element.53), channel_id=1, source_target_pairs={{0,3},{1,0},{2,1},{3,2},{4,7},{5,4},{6,5},{7,6},{8,11},{9,8},{10,9... | collective-permute-start | bytes 61448 | tf_op jit(solution)/shard_map/ppermute | solution.py:205
  5.3 0.7 fusion.59
  6.0 4.7 %collective-permute-start.5 = (f32[2,128]{1,0:T(2,128)S(1)}, f32[2,128]{1,0:T(2,128)S(1)}, u32[]{:S(2)}, u32[]{:S(2)}) collective-permute-start(f32[2,128]{1,0:T(2,128)S(1)} %get-tuple-element.62), channel_id=1, source_target_pairs={{4,0},{8,4},{12,8},{16,12},{20,16},{24,20},{28,24},{32,28},{36,32}... | collective-permute-start | bytes 3080 | tf_op jit(solution)/shard_map/ppermute | solution.py:28
  10.7 1.9 %collective-permute-start.4 = (f32[2,128]{1,0:T(2,128)S(1)}, f32[2,128]{1,0:T(2,128)S(1)}, u32[]{:S(2)}, u32[]{:S(2)}) collective-permute-start(f32[2,128]{1,0:T(2,128)S(1)} %get-tuple-element.61), channel_id=1, source_target_pairs={{0,4},{4,8},{8,12},{12,16},{16,20},{20,24},{24,28},{28,32},{32,36}... | collective-permute-start | bytes 3080 | tf_op jit(solution)/shard_map/ppermute | solution.py:26
  12.7 0.7 fusion.35
  13.9 0.8 reshape.103
  14.7 12.4 %all-to-all-start = ((f32[64,2,1]{1,2,0:T(1,128)}), f32[64,2,1]{1,2,0:T(1,128)S(1)}, u32[]{:S(2)}, u32[]{:S(2)}) async-start(f32[64,2,1]{1,2,0:T(1,128)} %bitcast.7), calls=%async_computation | async-start | bytes 65536 | tf_op jit(solution)/shard_map/all_to_all | solution.py:242
  27.9 2.8 %fusion.11 = f32[1,168]{1,0:T(1,128)S(1)} fusion(f32[8192,1]{0,1:T(1,128)S(1)} %bitcast.75, s32[168]{0:T(256)S(1)} %subtract_add_fusion, pred[168]{0:T(512)(128)(4,1)S(1)} %get-tuple-element.49), kind=kOutput, calls=%fused_computation.11 | convolution fusion | flops 19267584 | bytes 34280 | tf_op jit(solution)/shard_map/dot_general | solution.py:183
  30.7 2.0 %fusion.9 = f32[1,8192]{1,0:T(1,128)S(1)} fusion(f32[168,1]{0,1:T(1,128)S(1)} %bitcast.88, s32[168]{0:T(256)S(1)} %subtract_add_fusion, pred[168]{0:T(512)(128)(4,1)S(1)} %get-tuple-element.49), kind=kOutput, calls=%fused_computation.10 | convolution fusion | flops 19267584 | bytes 34280 | tf_op jit(solution)/shard_map/dot_general | solution.py:183
  33.8 1.7 %collective-permute-start.2 = (f32[5,2,72,128]{3,2,1,0:T(8,128)S(1)}, f32[5,2,72,128]{3,2,1,0:T(8,128)S(1)}, u32[]{:S(2)}, u32[]{:S(2)}) collective-permute-start(f32[5,2,72,128]{3,2,1,0:T(8,128)S(1)} %get-tuple-element.52), channel_id=1, source_target_pairs={{0,4},{4,8},{8,12},{12,16},{16,20},{20,24},{24,28},{28,32},{32,36}... | collective-permute-start | bytes 1105928 | tf_op jit(solution)/shard_map/ppermute | solution.py:208
  35.6 1.3 %collective-permute-start.7 = (f32[68,2]{1,0:T(8,128)S(1)}, f32[68,2]{1,0:T(8,128)S(1)}, u32[]{:S(2)}, u32[]{:S(2)}) collective-permute-start(f32[68,2]{1,0:T(8,128)S(1)} %get-tuple-element.58), channel_id=1, source_target_pairs={{1,0},{2,1},{3,2},{5,4},{6,5},{7,6},{9,8},{10,9},{11,10},{13,12},{... | collective-permute-start | bytes 1640 | tf_op jit(solution)/shard_map/ppermute | solution.py:28
  36.9 4.0 %collective-permute-start.6 = (f32[68,2]{1,0:T(8,128)S(1)}, f32[68,2]{1,0:T(8,128)S(1)}, u32[]{:S(2)}, u32[]{:S(2)}) collective-permute-start(f32[68,2]{1,0:T(8,128)S(1)} %get-tuple-element.57), channel_id=1, source_target_pairs={{0,1},{1,2},{2,3},{4,5},{5,6},{6,7},{8,9},{9,10},{10,11},{12,13},{... | collective-permute-start | bytes 1640 | tf_op jit(solution)/shard_map/ppermute | solution.py:26
  41.1 0.8 collective-permute-done.6
  42.0 0.7 collective-permute-done.3.xhi_ref
  42.7 4.4 %bulk_euler.1 = f32[5,4,64,128]{3,2,1,0:T(8,128)} custom-call(f32[4,64,128]{2,1,0:T(8,128)S(1)} %copy-done.1, f32[3,4,64,128]{3,2,1,0:T(8,128)S(1)} %copy-done, f32[4,64,128]{2,1,0:T(8,128)S(1)} %copy-done.2, f32[5,2,72,128]{3,2,1,0:T(8,128)S(1)} %collective-permute-done.2.xlo_ref, f32[5,2,72,128]{3,2,1,0:T(8,128)S(1)} %collective-permute-done.3.xhi_ref, ...), custom_call_target="tpu_custom_call" | custom-call | flops 60000000 | bytes 3000000 | tf_op jit(solution)/shard_map/bulk_euler/pallas_call | solution.py:153
  47.1 1.3 %fusion.26 = f32[4,64]{1,0:T(4,128)S(1)} fusion(f32[5,4,64,128]{3,2,1,0:T(8,128)} %bulk_euler.1), kind=kLoop, calls=%fused_computation.32 | loop fusion | flops 2304 | bytes 6144 | tf_op jit(solution)/shard_map/mul | solution.py:169
  48.5 14.1 %while.12 = (s32[]{:T(128)}, f32[8,16,128]{2,1,0:T(8,128)S(1)}, s32[8,16,128]{2,1,0:T(8,128)}, f32[256]{0:T(256)S(1)}) while((s32[]{:T(128)}, f32[8,16,128]{2,1,0:T(8,128)S(1)}, s32[8,16,128]{2,1,0:T(8,128)}, f32[256]{0:T(256)S(1)}) %tuple.39), condition=%wide.region_3.4_spmd.clone.clone, body=%wide.region_2.3_spmd.clone.sunk.clone | while | flops 6815746 | bytes 50245 | solution.py:223
  48.5 0.7 dynamic-slice_bitcast_fusion.3
  49.2 1.0 fusion.74
  50.2 0.7 dynamic-slice_bitcast_fusion.3
  51.0 1.0 fusion.74
  52.0 0.7 dynamic-slice_bitcast_fusion.3
  52.7 1.0 fusion.74
  53.8 0.7 dynamic-slice_bitcast_fusion.3
  54.5 1.0 fusion.74
  55.5 0.7 dynamic-slice_bitcast_fusion.3
  56.3 1.0 fusion.74
  57.3 0.7 dynamic-slice_bitcast_fusion.3
  58.0 1.0 fusion.74
  59.1 0.7 dynamic-slice_bitcast_fusion.3
  59.8 1.0 fusion.74
  60.9 0.7 dynamic-slice_bitcast_fusion.3
  61.6 1.0 fusion.74
  63.0 0.7 copy.20
  63.7 11.7 %all-to-all-start.1 = ((f32[64,2,128]{2,1,0:T(2,128)}), f32[64,2,128]{2,1,0:T(2,128)S(1)}, u32[]{:S(2)}, u32[]{:S(2)}) async-start(f32[64,2,128]{2,1,0:T(2,128)} %copy.20), calls=%async_computation.1 | async-start | bytes 131072 | tf_op jit(solution)/shard_map/all_to_all | solution.py:241
  75.6 9.9 %all-to-all-done.1 = f32[64,2,128]{2,1,0:T(2,128)S(1)} async-done(((f32[64,2,128]{2,1,0:T(2,128)}), f32[64,2,128]{2,1,0:T(2,128)S(1)}, u32[]{:S(2)}, u32[]{:S(2)}) %all-to-all-start.1) | async-done | bytes 65568 | tf_op jit(solution)/shard_map/all_to_all | solution.py:241
  85.8 2.3 %collective-permute-start.9 = (f32[2,128]{1,0:T(2,128)S(1)}, f32[2,128]{1,0:T(2,128)S(1)}, u32[]{:S(2)}, u32[]{:S(2)}) collective-permute-start(f32[2,128]{1,0:T(2,128)S(1)} %get-tuple-element.60), channel_id=1, source_target_pairs={{4,0},{8,4},{12,8},{16,12},{20,16},{24,20},{28,24},{32,28},{36,32}... | collective-permute-start | bytes 3080 | tf_op jit(solution)/shard_map/ppermute | solution.py:28
  88.1 3.3 %collective-permute-start.8 = (f32[2,128]{1,0:T(2,128)S(1)}, f32[2,128]{1,0:T(2,128)S(1)}, u32[]{:S(2)}, u32[]{:S(2)}) collective-permute-start(f32[2,128]{1,0:T(2,128)S(1)} %get-tuple-element.59), channel_id=1, source_target_pairs={{0,4},{4,8},{8,12},{12,16},{16,20},{20,24},{24,28},{28,32},{32,36}... | collective-permute-start | bytes 3080 | tf_op jit(solution)/shard_map/ppermute | solution.py:26
  91.4 2.8 %fusion.7 = f32[1,168]{1,0:T(1,128)S(1)} fusion(f32[8192,1]{0,1:T(1,128)S(1)} %bitcast.76, s32[168]{0:T(256)S(1)} %subtract_add_fusion, pred[168]{0:T(512)(128)(4,1)S(1)} %get-tuple-element.49), kind=kOutput, calls=%fused_computation.9 | convolution fusion | flops 19267584 | bytes 34280 | tf_op jit(solution)/shard_map/dot_general | solution.py:183
  94.3 1.3 %collective-permute-start.11 = (f32[68,2]{1,0:T(8,128)S(1)}, f32[68,2]{1,0:T(8,128)S(1)}, u32[]{:S(2)}, u32[]{:S(2)}) collective-permute-start(f32[68,2]{1,0:T(8,128)S(1)} %get-tuple-element.56), channel_id=1, source_target_pairs={{1,0},{2,1},{3,2},{5,4},{6,5},{7,6},{9,8},{10,9},{11,10},{13,12},{... | collective-permute-start | bytes 1640 | tf_op jit(solution)/shard_map/ppermute | solution.py:28
  95.6 4.6 %collective-permute-start.10 = (f32[68,2]{1,0:T(8,128)S(1)}, f32[68,2]{1,0:T(8,128)S(1)}, u32[]{:S(2)}, u32[]{:S(2)}) collective-permute-start(f32[68,2]{1,0:T(8,128)S(1)} %get-tuple-element.55), channel_id=1, source_target_pairs={{0,1},{1,2},{2,3},{4,5},{5,6},{6,7},{8,9},{9,10},{10,11},{12,13},{... | collective-permute-start | bytes 1640 | tf_op jit(solution)/shard_map/ppermute | solution.py:26
  100.2 2.0 %fusion.5 = f32[1,8192]{1,0:T(1,128)S(1)} fusion(f32[168,1]{0,1:T(1,128)S(1)} %bitcast.87, s32[168]{0:T(256)S(1)} %subtract_add_fusion, pred[168]{0:T(512)(128)(4,1)S(1)} %get-tuple-element.49), kind=kOutput, calls=%fused_computation.8 | convolution fusion | flops 19267584 | bytes 34280 | tf_op jit(solution)/shard_map/dot_general | solution.py:183
  102.6 0.9 fusion.33
  103.5 7.8 %all-to-all-start.2 = ((f32[64,2,128]{2,1,0:T(2,128)}), f32[64,2,128]{2,1,0:T(2,128)S(1)}, u32[]{:S(2)}, u32[]{:S(2)}) async-start(f32[64,2,128]{2,1,0:T(2,128)} %bitcast.26), calls=%async_computation.2 | async-start | bytes 131072 | tf_op jit(solution)/shard_map/all_to_all | solution.py:278
  111.3 10.1 %all-to-all-done.2 = f32[64,2,128]{2,1,0:T(2,128)S(1)} async-done(((f32[64,2,128]{2,1,0:T(2,128)}), f32[64,2,128]{2,1,0:T(2,128)S(1)}, u32[]{:S(2)}, u32[]{:S(2)}) %all-to-all-start.2) | async-done | bytes 65568 | tf_op jit(solution)/shard_map/all_to_all | solution.py:278
  121.4 0.9 convolution_select_fusion
  (74 shorter events, 2.7 us)
Async XLA Ops:
  0.6 27.2 %copy-start.3 = (f32[64,128]{1,0:T(8,128)S(1)}, f32[64,128]{1,0:T(8,128)}, u32[]{:S(2)}) copy-start(f32[64,128]{1,0:T(8,128)} %param.18) | copy-start | bytes 98308
  0.6 12.9 %copy-start.9 = (s32[128,1]{0,1:T(1,128)S(1)}, s32[128,1]{0,1:T(1,128)}, u32[]{:S(2)}) copy-start(s32[128,1]{0,1:T(1,128)} %param.25) | copy-start | bytes 1540
  0.7 13.1 %copy-start.10 = (s32[128]{0:T(128)S(1)}, s32[128]{0:T(128)}, u32[]{:S(2)}) copy-start(s32[128]{0:T(128)} %param.26) | copy-start | bytes 1540
  0.7 26.5 %copy-start.6 = (s32[168]{0:T(256)S(1)}, s32[168]{0:T(256)}, u32[]{:S(2)}) copy-start(s32[168]{0:T(256)} %param.22) | copy-start | bytes 2020
  1.6 32.0 %collective-permute-start.1 = (f32[5,4,2,128]{3,2,1,0:T(2,128)S(1)}, f32[5,4,2,128]{3,2,1,0:T(2,128)S(1)}, u32[]{:S(2)}, u32[]{:S(2)}) collective-permute-start(f32[5,4,2,128]{3,2,1,0:T(2,128)S(1)} %get-tuple-element.54), channel_id=1, source_target_pairs={{0,1},{1,2},{2,3},{3,0},{4,5},{5,6},{6,7},{7,4},{8,9},{9,10},{10,1... | collective-permute-start | bytes 61448 | tf_op jit(solution)/shard_map/ppermute | solution.py:204
  3.8 29.8 %collective-permute-start = (f32[5,4,2,128]{3,2,1,0:T(2,128)S(1)}, f32[5,4,2,128]{3,2,1,0:T(2,128)S(1)}, u32[]{:S(2)}, u32[]{:S(2)}) collective-permute-start(f32[5,4,2,128]{3,2,1,0:T(2,128)S(1)} %get-tuple-element.53), channel_id=1, source_target_pairs={{0,3},{1,0},{2,1},{3,2},{4,7},{5,4},{6,5},{7,6},{8,11},{9,8},{10,9... | collective-permute-start | bytes 61448 | tf_op jit(solution)/shard_map/ppermute | solution.py:205
  6.0 27.5 %collective-permute-start.5 = (f32[2,128]{1,0:T(2,128)S(1)}, f32[2,128]{1,0:T(2,128)S(1)}, u32[]{:S(2)}, u32[]{:S(2)}) collective-permute-start(f32[2,128]{1,0:T(2,128)S(1)} %get-tuple-element.62), channel_id=1, source_target_pairs={{4,0},{8,4},{12,8},{16,12},{20,16},{24,20},{28,24},{32,28},{36,32}... | collective-permute-start | bytes 3080 | tf_op jit(solution)/shard_map/ppermute | solution.py:28
  10.7 22.8 %collective-permute-start.4 = (f32[2,128]{1,0:T(2,128)S(1)}, f32[2,128]{1,0:T(2,128)S(1)}, u32[]{:S(2)}, u32[]{:S(2)}) collective-permute-start(f32[2,128]{1,0:T(2,128)S(1)} %get-tuple-element.61), channel_id=1, source_target_pairs={{0,4},{4,8},{8,12},{12,16},{16,20},{20,24},{24,28},{28,32},{32,36}... | collective-permute-start | bytes 3080 | tf_op jit(solution)/shard_map/ppermute | solution.py:26
  14.7 26.1 %all-to-all-start = ((f32[64,2,1]{1,2,0:T(1,128)}), f32[64,2,1]{1,2,0:T(1,128)S(1)}, u32[]{:S(2)}, u32[]{:S(2)}) async-start(f32[64,2,1]{1,2,0:T(1,128)} %bitcast.7), calls=%async_computation | async-start | bytes 65536 | tf_op jit(solution)/shard_map/all_to_all | solution.py:242
  27.8 2.8 %copy-start.7 = (f32[168]{0:T(256)S(1)}, f32[168]{0:T(256)}, u32[]{:S(2)}) copy-start(f32[168]{0:T(256)} %param.21) | copy-start | bytes 2020
  27.8 2.8 %copy-start.8 = (f32[168]{0:T(256)S(1)}, f32[168]{0:T(256)}, u32[]{:S(2)}) copy-start(f32[168]{0:T(256)} %param.20) | copy-start | bytes 2020
  30.7 2.9 %copy-start = (f32[3,4,64,128]{3,2,1,0:T(8,128)S(1)}, f32[3,4,64,128]{3,2,1,0:T(8,128)}, u32[]{:S(2)}) copy-start(f32[3,4,64,128]{3,2,1,0:T(8,128)} %vel_ref.1) | copy-start | bytes 1179652
  30.7 2.9 %copy-start.1 = (f32[4,64,128]{2,1,0:T(8,128)S(1)}, f32[4,64,128]{2,1,0:T(8,128)}, u32[]{:S(2)}) copy-start(f32[4,64,128]{2,1,0:T(8,128)} %rho_ref.1) | copy-start | bytes 393220
  30.7 2.9 %copy-start.2 = (f32[4,64,128]{2,1,0:T(8,128)S(1)}, f32[4,64,128]{2,1,0:T(8,128)}, u32[]{:S(2)}) copy-start(f32[4,64,128]{2,1,0:T(8,128)} %pre_ref.1) | copy-start | bytes 393220
  33.8 8.2 %collective-permute-start.2 = (f32[5,2,72,128]{3,2,1,0:T(8,128)S(1)}, f32[5,2,72,128]{3,2,1,0:T(8,128)S(1)}, u32[]{:S(2)}, u32[]{:S(2)}) collective-permute-start(f32[5,2,72,128]{3,2,1,0:T(8,128)S(1)} %get-tuple-element.52), channel_id=1, source_target_pairs={{0,4},{4,8},{8,12},{12,16},{16,20},{20,24},{24,28},{28,32},{32,36}... | collective-permute-start | bytes 1105928 | tf_op jit(solution)/shard_map/ppermute | solution.py:208
  35.5 7.2 %collective-permute-start.3 = (f32[5,2,72,128]{3,2,1,0:T(8,128)S(1)}, f32[5,2,72,128]{3,2,1,0:T(8,128)S(1)}, u32[]{:S(2)}, u32[]{:S(2)}) collective-permute-start(f32[5,2,72,128]{3,2,1,0:T(8,128)S(1)} %get-tuple-element.51), channel_id=1, source_target_pairs={{0,252},{4,0},{8,4},{12,8},{16,12},{20,16},{24,20},{28,24},{32,28}... | collective-permute-start | bytes 1105928 | tf_op jit(solution)/shard_map/ppermute | solution.py:209
  35.6 5.5 %collective-permute-start.7 = (f32[68,2]{1,0:T(8,128)S(1)}, f32[68,2]{1,0:T(8,128)S(1)}, u32[]{:S(2)}, u32[]{:S(2)}) collective-permute-start(f32[68,2]{1,0:T(8,128)S(1)} %get-tuple-element.58), channel_id=1, source_target_pairs={{1,0},{2,1},{3,2},{5,4},{6,5},{7,6},{9,8},{10,9},{11,10},{13,12},{... | collective-permute-start | bytes 1640 | tf_op jit(solution)/shard_map/ppermute | solution.py:28
  36.9 5.0 %collective-permute-start.6 = (f32[68,2]{1,0:T(8,128)S(1)}, f32[68,2]{1,0:T(8,128)S(1)}, u32[]{:S(2)}, u32[]{:S(2)}) collective-permute-start(f32[68,2]{1,0:T(8,128)S(1)} %get-tuple-element.57), channel_id=1, source_target_pairs={{0,1},{1,2},{2,3},{4,5},{5,6},{6,7},{8,9},{9,10},{10,11},{12,13},{... | collective-permute-start | bytes 1640 | tf_op jit(solution)/shard_map/ppermute | solution.py:26
  62.6 22.9 %copy-start.5 = (f32[64,128]{1,0:T(8,128)S(1)}, f32[64,128]{1,0:T(8,128)}, u32[]{:S(2)}) copy-start(f32[64,128]{1,0:T(8,128)} %param.19) | copy-start | bytes 98308
  63.7 21.8 %all-to-all-start.1 = ((f32[64,2,128]{2,1,0:T(2,128)}), f32[64,2,128]{2,1,0:T(2,128)S(1)}, u32[]{:S(2)}, u32[]{:S(2)}) async-start(f32[64,2,128]{2,1,0:T(2,128)} %copy.20), calls=%async_computation.1 | async-start | bytes 131072 | tf_op jit(solution)/shard_map/all_to_all | solution.py:241
  85.8 8.4 %collective-permute-start.9 = (f32[2,128]{1,0:T(2,128)S(1)}, f32[2,128]{1,0:T(2,128)S(1)}, u32[]{:S(2)}, u32[]{:S(2)}) collective-permute-start(f32[2,128]{1,0:T(2,128)S(1)} %get-tuple-element.60), channel_id=1, source_target_pairs={{4,0},{8,4},{12,8},{16,12},{20,16},{24,20},{28,24},{32,28},{36,32}... | collective-permute-start | bytes 3080 | tf_op jit(solution)/shard_map/ppermute | solution.py:28
  88.1 6.1 %collective-permute-start.8 = (f32[2,128]{1,0:T(2,128)S(1)}, f32[2,128]{1,0:T(2,128)S(1)}, u32[]{:S(2)}, u32[]{:S(2)}) collective-permute-start(f32[2,128]{1,0:T(2,128)S(1)} %get-tuple-element.59), channel_id=1, source_target_pairs={{0,4},{4,8},{8,12},{12,16},{16,20},{20,24},{24,28},{28,32},{32,36}... | collective-permute-start | bytes 3080 | tf_op jit(solution)/shard_map/ppermute | solution.py:26
  94.3 7.9 %collective-permute-start.11 = (f32[68,2]{1,0:T(8,128)S(1)}, f32[68,2]{1,0:T(8,128)S(1)}, u32[]{:S(2)}, u32[]{:S(2)}) collective-permute-start(f32[68,2]{1,0:T(8,128)S(1)} %get-tuple-element.56), channel_id=1, source_target_pairs={{1,0},{2,1},{3,2},{5,4},{6,5},{7,6},{9,8},{10,9},{11,10},{13,12},{... | collective-permute-start | bytes 1640 | tf_op jit(solution)/shard_map/ppermute | solution.py:28
  95.6 6.6 %collective-permute-start.10 = (f32[68,2]{1,0:T(8,128)S(1)}, f32[68,2]{1,0:T(8,128)S(1)}, u32[]{:S(2)}, u32[]{:S(2)}) collective-permute-start(f32[68,2]{1,0:T(8,128)S(1)} %get-tuple-element.55), channel_id=1, source_target_pairs={{0,1},{1,2},{2,3},{4,5},{5,6},{6,7},{8,9},{9,10},{10,11},{12,13},{... | collective-permute-start | bytes 1640 | tf_op jit(solution)/shard_map/ppermute | solution.py:26
  102.6 19.6 %copy-start.4 = (f32[64,128]{1,0:T(8,128)}, f32[64,128]{1,0:T(8,128)S(1)}, u32[]{:S(2)}) copy-start(f32[64,128]{1,0:T(8,128)S(1)} %fusion.41) | copy-start | bytes 98308
  103.5 17.9 %all-to-all-start.2 = ((f32[64,2,128]{2,1,0:T(2,128)}), f32[64,2,128]{2,1,0:T(2,128)S(1)}, u32[]{:S(2)}, u32[]{:S(2)}) async-start(f32[64,2,128]{2,1,0:T(2,128)} %bitcast.26), calls=%async_computation.2 | async-start | bytes 131072 | tf_op jit(solution)/shard_map/all_to_all | solution.py:278
where the time goes:
time: 123 us; the launch traced here: 122 us
  starting transfers between devices  60.6 us (49%)
  waiting for transfers between devices  21.5 us (17%)
  matrix products  20.4 us (17%)
  local copies, waits for them, and re-layouts  8.56 us (7%)
  Pallas kernels  4.38 us (4%)
  other arithmetic  4.29 us (3%)
  between operations  2.45 us (2%)
    dot_general x17, matrix products, pick_rows(): return jnp.dot(selector, table, precision=lax.Precision.HIGHEST)  20.4 us
    ppermute x4, starting transfers between devices, with_halo(): lax.ppermute(tail, axis, [(i, (i + 1) % count) for i in range(ends)])  13.7 us
    all_to_all x1, starting transfers between devices, body(): lax.all_to_all(row_packed, 'fluid', split_axis=0, concat_axis=0, tiled=True)  12.4 us
    all_to_all x1, starting transfers between devices, body(): lax.all_to_all(packed, 'fluid', split_axis=0, concat_axis=0, tiled=True)  11.7 us
    all_to_all x1, waiting for transfers between devices, body(): lax.all_to_all(outgoing, 'fluid', split_axis=0, concat_axis=0, tiled=True)  10.1 us
    all_to_all x1, waiting for transfers between devices, body(): lax.all_to_all(packed, 'fluid', split_axis=0, concat_axis=0, tiled=True)  9.92 us
    ppermute x4, starting transfers between devices, with_halo(): lax.ppermute(head, axis, [((i + 1) % count, i) for i in range(ends)])  9.59 us
    all_to_all x1, starting transfers between devices, body(): lax.all_to_all(outgoing, 'fluid', split_axis=0, concat_axis=0, tiled=True)  7.76 us
  transfers between devices with their start and end apart: 15, of which 4 were waited for; matrix products, arithmetic and copies ran while one was open for 11% of the time, Pallas kernels for 0%

commit v1 on v0

v1 whole, which is shorter than its diff:
```python
import jax
import jax.numpy as jnp
from jax import lax
from jax.experimental import pallas as pl
from jax.experimental.pallas import tpu as pltpu
from jax.sharding import PartitionSpec as P

STEP_FLUID = 0.045
STEP_DECK = 0.06
GAMMA_LESS = 0.4
AMBIENT = 1.0

THIN = 0
TABLE = 64
DECK = 72
EDGES = 88
NT = (((1,), (1,)), ((), ()))
NN = (((1,), (0,)), ((), ()))


def vmem(count):
    return [pl.BlockSpec(memory_space=pltpu.VMEM)] * count


def local_call(kernel, shapes, name, args, scratch=(), flops=1_000_000, smem=()):
    single = not isinstance(shapes, list)
    outs = [s if isinstance(s, jax.ShapeDtypeStruct) else jax.ShapeDtypeStruct(s, jnp.float32) for s in ([shapes] if single else shapes)]
    specs = [pl.BlockSpec(memory_space=pltpu.SMEM if i in smem else pltpu.VMEM) for i in range(len(args))]
    result = pl.pallas_call(
        kernel,
        out_shape=outs,
        in_specs=specs,
        out_specs=vmem(len(outs)),
        scratch_shapes=list(scratch),
        compiler_params=pltpu.CompilerParams(vmem_limit_bytes=32 * 1024 * 1024),
        cost_estimate=pl.CostEstimate(flops=flops, bytes_accessed=1_000_000, transcendentals=0),
        name=name,
    )(*args)
    return result[0] if single else result


def iota(shape, axis):
    return lax.broadcasted_iota(jnp.int32, shape, axis)


def split3(x):
    high = x.astype(jnp.bfloat16)
    rest = x - high.astype(jnp.float32)
    middle = rest.astype(jnp.bfloat16)
    low = (rest - middle.astype(jnp.float32)).astype(jnp.bfloat16)
    return high, middle, low


def pick(onehot, table, dims=NN):
    onehot = onehot.astype(jnp.float32).astype(jnp.bfloat16)
    total = None
    for part in split3(table):
        term = lax.dot_general(onehot, part, dims, preferred_element_type=jnp.float32)
        total = term if total is None else total + term
    return total


def side_rows():
    sect = lax.axis_index("sect")
    left, right = lax.rem(sect + 3, 4), lax.rem(sect + 1, 4)
    return pl.multiple_of(left * 128, 128), pl.multiple_of(right * 128, 128)


YOFF = 8
YROWS = 80
KFL = 0.5 * STEP_FLUID


def euler_prims(rho, m1, m2, m3, en):
    inv = 1.0 / rho
    v1, v2, v3 = m1 * inv, m2 * inv, m3 * inv
    p = GAMMA_LESS * (en - 0.5 * (m1 * v1 + m2 * v2 + m3 * v3))
    return v1, v2, v3, p, jnp.sqrt(1.4 * p * inv)


def from_raw(rho, v1, v2, v3, p):
    en = p * (1.0 / GAMMA_LESS) + 0.5 * rho * (v1 * v1 + v2 * v2 + v3 * v3)
    return (rho, rho * v1, rho * v2, rho * v3, en), (v1, v2, v3, p, jnp.sqrt(1.4 * p / rho))


def flux(state, prim, d):
    rho, m1, m2, m3, en = state
    v, p = prim[d], prim[3]
    out = [state[1 + d], m1 * v, m2 * v, m3 * v, (en + p) * v]
    out[1 + d] = out[1 + d] + p
    return out


def add_direction(acc, here, prim, up, uprim, down, dprim, d):
    fu, fd = flux(up, uprim, d), flux(down, dprim, d)
    s0 = jnp.abs(prim[d]) + prim[4]
    lu = jnp.maximum(s0, jnp.abs(uprim[d]) + uprim[4])
    ld = jnp.maximum(s0, jnp.abs(dprim[d]) + dprim[4])
    out = []
    for c in range(5):
        term = (fu[c] - fd[c]) - lu * (up[c] - here[c]) + ld * (here[c] - down[c])
        out.append(term if acc is None else acc[c] + term)
    return out


def prep_kernel(rho_ref, vel_ref, pre_ref, w_ref, u_ref, ext_ref, cor_ref, own_ref, edge_ref):
    core = lax.axis_index("fluid") % 2
    chooser = iota((16, 128), 0) == iota((16, 128), 1)
    raw = [rho_ref, vel_ref.at[0], vel_ref.at[1], vel_ref.at[2], pre_ref]
    own_ref[15:16, :] = jnp.zeros((1, 256), jnp.float32)
    for c in range(5):
        own_ref[3 * c : 3 * c + 3, :] = pick(chooser, raw[c][...].reshape(256, 128), NT)[0:3]
        for side, y in ((0, 0), (1, 62)):
            for i in range(4):
                edge_ref[pl.ds(40 * side + 8 * c + 2 * i, 2), :] = raw[c][i, pl.ds(y, 2), :]
    first, last = own_ref[:, 0:128], own_ref[:, 128:256]
    even = core == 0
    ext_ref[0:16, :] = jnp.where(even, first, last)
    cor_ref[0:16, :] = jnp.where(even, last, first)
    wf, wl, uf, ul = w_ref[0:4, :], w_ref[60:64, :], u_ref[0:2, :], u_ref[62:64, :]
    ext_ref[16:20, :] = jnp.where(even, wf, wl)
    cor_ref[16:20, :] = jnp.where(even, wl, wf)
    ext_ref[20:22, :] = jnp.where(even, uf, ul)
    cor_ref[20:22, :] = jnp.where(even, ul, uf)
    ext_ref[22:24, :] = jnp.zeros((2, 128), jnp.float32)
    cor_ref[22:24, :] = jnp.zeros((2, 128), jnp.float32)


def table_kernel(cells_ref, owner_ref, row_ref, count_ref, tab_ref, pos_ref, place_ref):
    owner = jnp.broadcast_to(owner_ref[...].astype(jnp.float32), (128, 128))
    owner_row = owner.T
    same = owner == owner_row
    down, along = iota((128, 128), 0), iota((128, 128), 1)
    within = jnp.sum(jnp.where(same & (along < down), 1.0, 0.0), axis=1, keepdims=True)
    within_row = jnp.sum(jnp.where(same & (down < along), 1.0, 0.0), axis=0, keepdims=True)
    position = (2.0 * owner[:, 0:1] + within).astype(jnp.int32)
    pos_ref[...] = jnp.broadcast_to(2.0 * owner_row[0:1, :] + within_row, (8, 128))
    place = jnp.where(position == along, 1.0, 0.0).astype(jnp.bfloat16)
    place_ref[...] = place
    r, c = iota((16, 128), 0), iota((16, 128), 1)
    columns = jnp.where(((r < 2) & (c == r)) | ((r >= 2) & (r < 4) & (c == r + 124)), 1.0, 0.0).astype(jnp.bfloat16)
    cells = cells_ref[...].astype(jnp.float32).astype(jnp.bfloat16)
    picked = lax.dot_general(columns, cells, NT, preferred_element_type=jnp.float32)
    live = iota((1, 128), 1) < count_ref[0]
    code = jnp.where(live, row_ref[...] + 128, 0).astype(jnp.float32)
    stacked = jnp.where(r == 4, jnp.broadcast_to(code, (16, 128)), picked).astype(jnp.bfloat16)
    tab_ref[...] = lax.dot_general(stacked, place, NN, preferred_element_type=jnp.float32)[0:8]


def middle_kernel(ext_ref, cor_ref, own_ref, w_ref, u_ref, tab_ref, edge_ref, out_ref, deck_ref, wide):
    fluid, sect = lax.axis_index("fluid"), lax.axis_index("sect")
    even = fluid % 2 == 0
    ext, cor = ext_ref[...], cor_ref[...]
    low, high = jnp.where(even, ext, cor), jnp.where(even, cor, ext)
    low_deck = jnp.where(fluid == 0, 0.0, low[16:24])
    high_deck = jnp.where(fluid == 63, 0.0, high[16:24])
    wide[...] = jnp.zeros((2, 128, 128), jnp.float32)
    wide[0, 0:4, :] = low_deck[0:4]
    wide[0, 4:68, :] = w_ref[...]
    wide[0, 68:72, :] = high_deck[0:4]
    wide[1, 2:4, :] = low_deck[4:6]
    wide[1, 4:68, :] = u_ref[...]
    wide[1, 68:70, :] = high_deck[4:6]
    deck_ref[...] = wide[:, 0:72, :]
    w_columns, u_columns = wide[0].T, wide[1].T
    pieces = [low[0:16], own_ref[:, 0:128], own_ref[:, 128:256], high[0:16], tab_ref[...], w_columns[0:4], w_columns[124:128], u_columns[0:2], u_columns[126:128], jnp.zeros((4, 128), jnp.float32)]
    block = jnp.concatenate(pieces, axis=0)
    for t in range(4):
        out_ref[t, 0:EDGES, :] = block
        out_ref[t, EDGES:128, :] = edge_ref[0:40, :]
    out_ref[lax.rem(sect + 1, 4), EDGES:128, :] = edge_ref[40:80, :]


def wall_press(around_ref):
    lane = iota((8, 128), 1)
    low_half, y = lane < 64, lane & 63

    def get(t, c, z):
        part = around_ref[pl.ds(THIN + 16 * t + 3 * c + z, 4, stride=128), :]
        return jnp.concatenate([part, part], axis=0)

    def x_around(tiles):
        turned = [pltpu.roll(x, 64, 1) for x in tiles]
        after, before = turned[1:] + turned[-1:], turned[:1] + turned[:-1]
        ups = [jnp.where(low_half, a, b) for a, b in zip(turned, after)]
        downs = [jnp.where(low_half, b, a) for a, b in zip(turned, before)]
        return ups, downs

    def y_up(x):
        return jnp.where(y == 63, pltpu.roll(pltpu.roll(x, 7, 0), 63, 1), pltpu.roll(x, 127, 1))

    def y_down(x):
        return jnp.where(y == 0, pltpu.roll(pltpu.roll(x, 1, 0), 65, 1), pltpu.roll(x, 1, 1))

    def mirrored(state, prim):
        return [state[0], state[1], state[2], -state[3], state[4]], [prim[0], prim[1], -prim[2], prim[3], prim[4]]

    def advance(states, prims, layer, tiles):
        here, q = states[layer], prims[layer]
        xu = [x_around([here[t][c] for t in range(4)]) for c in range(5)]
        xq = {c: x_around([q[t][c] for t in range(4)]) for c in (0, 3, 4)}
        result = []
        for t in tiles:
            pack = [None] * 5
            up, down = [xu[c][0][t] for c in range(5)], [xu[c][1][t] for c in range(5)]
            upq, downq = list(pack), list(pack)
            for c in (0, 3, 4):
                upq[c], downq[c] = xq[c][0][t], xq[c][1][t]
            acc = add_direction(None, here[t], q[t], up, upq, down, downq, 0)
            up, down = [y_up(here[t][c]) for c in range(5)], [y_down(here[t][c]) for c in range(5)]
            upq, downq = list(pack), list(pack)
            for c in (1, 3, 4):
                upq[c], downq[c] = y_up(q[t][c]), y_down(q[t][c])
            acc = add_direction(acc, here[t], q[t], up, upq, down, downq, 1)
            down, downq = mirrored(here[t], q[t]) if layer == 0 else (states[layer - 1][t], prims[layer - 1][t])
            acc = add_direction(acc, here[t], q[t], states[layer + 1][t], prims[layer + 1][t], down, downq, 2)
            result.append([here[t][c] - KFL * acc[c] for c in range(5)])
        return result

    states, prims = [], []
    for z in range(3):
        both = [from_raw(*[get(t, c, z) for c in range(5)]) for t in range(4)]
        states.append([b[0] for b in both])
        prims.append([b[1] for b in both])
    after = [advance(states, prims, z, range(4)) for z in range(2)]
    after_prims = [[euler_prims(*after[z][t]) for t in range(4)] for z in range(2)]
    final = advance(after, after_prims, 0, (1, 2))
    return [euler_prims(*final[i])[3] for i in range(2)]


def gather_lanes(tables, cells):
    index = cells & 127
    low = jnp.take_along_axis(jnp.broadcast_to(tables[0], cells.shape), index, axis=1, mode="promise_in_bounds")
    high = jnp.take_along_axis(jnp.broadcast_to(tables[1], cells.shape), index, axis=1, mode="promise_in_bounds")
    return jnp.where(cells < 128, low, high) - AMBIENT


def facet_kernel(around_ref, cells_ref, tab_ref, pos_ref, out_ref, press):
    fluid, sect = lax.axis_index("fluid"), lax.axis_index("sect")
    left, right = side_rows()
    first, second = wall_press(around_ref)
    press[0:8, :] = first
    press[8:16, :] = second

    def tables(s):
        return press[pl.ds(s, 1), :], press[pl.ds(s + 8, 1), :]

    values = gather_lanes(tables(sect), cells_ref[...])
    r = iota((512, 128), 0)
    wanted = 2 * (r >> 3) + (r & 7) - 2
    chooser = (pos_ref[0:1, :].astype(jnp.int32) == wanted) & ((r & 7) < 6)
    out_ref[...] = pick(chooser, values)
    left_tab = around_ref[pl.ds(left + TABLE, 8), :]
    right_tab = around_ref[pl.ds(right + TABLE, 8), :]
    left_values = gather_lanes(tables(lax.rem(sect + 3, 4)), left_tab.astype(jnp.int32))
    right_values = gather_lanes(tables(lax.rem(sect + 1, 4)), right_tab.astype(jnp.int32))
    left_code = jnp.where(sect == 0, 0.0, left_tab[4:5])
    right_code = jnp.where(sect == 3, 0.0, right_tab[4:5])
    rows = [tab_ref[4:5, :], left_code, left_values[2:3], left_values[3:4], right_code, right_values[0:1], right_values[1:2]]
    spread = jnp.concatenate([jnp.broadcast_to(x, (8, 128)) for x in rows] + [jnp.zeros((72, 128), jnp.float32)], axis=0)
    place = iota((128, 128), 0) & 7
    weights = jnp.concatenate([jnp.where(place == 2, spread, 0.0), jnp.where(place == 3, spread, 0.0)], axis=1)
    o, p = iota((64, 256), 0), iota((64, 256), 1)
    base = pick(2 * o + (p >> 7) == (p & 127), weights, NT)
    owner = iota((64, 128), 0)
    before = jnp.where(owner == 0, 0.0, pltpu.roll(base, 1, 0))
    after = jnp.where(owner == 63, 0.0, pltpu.roll(base, 63, 0))
    meta = base + pltpu.roll(before, 126, 1) + pltpu.roll(after, 2, 1)
    out_ref[pl.ds(7, 64, stride=8), :] = meta


def bending_of(w):
    def laplace(x):
        rows, lanes = x.shape
        return pltpu.roll(x, 1, 0) + pltpu.roll(x, rows - 1, 0) + pltpu.roll(x, 1, 1) + pltpu.roll(x, lanes - 1, 1) - 4.0 * x

    return laplace(laplace(w))


def early_kernel(around_ref, deck_ref, stiff_ref, tension_ref, anchor_ref, failed_ref, out_ref, turn):
    fluid, sect = lax.axis_index("fluid"), lax.axis_index("sect")
    left, right = side_rows()
    turn[...] = jnp.zeros((2, 128, 128), jnp.float32)
    turn[0, 0:4, :] = jnp.where(sect == 3, 0.0, around_ref[pl.ds(right + DECK, 4), :])
    turn[0, 124:128, :] = jnp.where(sect == 0, 0.0, around_ref[pl.ds(left + DECK + 4, 4), :])
    turn[1, 0:2, :] = jnp.where(sect == 3, 0.0, around_ref[pl.ds(right + DECK + 8, 2), :])
    turn[1, 126:128, :] = jnp.where(sect == 0, 0.0, around_ref[pl.ds(left + DECK + 10, 2), :])
    w = jnp.concatenate([deck_ref[0], turn[0].T[0:72]], axis=1)
    u = jnp.concatenate([deck_ref[1], turn[1].T[0:72]], axis=1)
    anchor = anchor_ref[...]
    count = anchor.shape[1]
    alive = iota((1, count), 1) != failed_ref[0]
    row = (anchor >> 9) - 64 * fluid + 4
    column = (anchor & 511) - 128 * sect
    lane = jnp.where((column >= -4) & (column < 132) & alive, column & 255, -1)
    rows = iota((72, count), 0) == row
    columns = iota((256, count), 0) == lane
    alpha = pick(rows, jnp.where(columns, stiff_ref[...], 0.0), NT)
    beta = pick(rows, jnp.where(columns, tension_ref[...], 0.0), NT)
    first = 2.0 * w - u + STEP_DECK * (beta - alpha * w - bending_of(w))
    r, c = iota((72, 256), 0) - 4 + 64 * fluid, iota((72, 256), 1)
    c = jnp.where(c < 132, c, c - 256) + 128 * sect
    inside = (r >= 0) & (r < 4096) & (c >= 0) & (c < 512) & (c >= 128 * sect - 4)
    out_ref[0] = w
    out_ref[1] = jnp.where(inside, first, 0.0)
    out_ref[2] = alpha
    out_ref[3] = beta


def deck_kernel(got_ref, early_ref, deck_ref, ret_ref, spread):
    meta = got_ref[pl.ds(7, 64, stride=8), :]
    for j in range(8):
        spread[pl.ds(j, 64, stride=8), :] = meta
    r, c = iota((512, 128), 0), iota((512, 128), 1)
    own = jnp.where((c & 7) == (r & 7), spread[...], 0.0)
    kinds = pick((iota((16, 128), 1) >> 3) == iota((16, 128), 0), own, NT)
    k = iota((1, 512), 1)
    offset = 64 * ((k & 7) >> 1) - 64 + 4 - 128

    def rows_of(kind):
        code = kinds[kind : kind + 1].astype(jnp.int32)
        local = jnp.where((code > 0) & ((k & 7) < 6), code + offset, -1)
        return iota((72, 512), 0) == local

    centre = pick(rows_of(0), got_ref[...])
    lanes = iota((128, 512), 0)
    from_left = jnp.where(lanes == 126, kinds[2:3], jnp.where(lanes == 127, kinds[3:4], 0.0))
    from_right = jnp.where(lanes == 0, kinds[5:6], jnp.where(lanes == 1, kinds[6:7], 0.0))
    sides = pick(rows_of(1), from_left, NT) + pick(rows_of(4), from_right, NT)
    load = jnp.concatenate([centre, sides], axis=1)
    first = early_ref[1] + STEP_DECK * load
    second = 2.0 * first - early_ref[0] + STEP_DECK * (load + early_ref[3] - early_ref[2] * first - bending_of(first))
    tile = second[4:68, 0:128]
    deck_ref[...] = tile
    for i in range(2):
        row = meta[:, 2 + i : 3 + i].astype(jnp.int32) - 128
        ret_ref[:, i, :] = pick(iota((64, 64), 1) == row, tile)


def final_kernel(got_ref, place_ref, out_ref):
    out_ref[...] = pick(place_ref[...], got_ref[...])


def pack_kernel(rho_ref, vel_ref, pre_ref, around_ref, ext_ref, cor_ref):
    core = lax.axis_index("fluid") % 2
    left, right = side_rows()
    raw = [rho_ref, vel_ref.at[0], vel_ref.at[1], vel_ref.at[2], pre_ref]
    for ref, start in ((ext_ref, 2 * core), (cor_ref, 2 - 2 * core)):
        for c in range(5):
            for i in range(2):
                ref[c, i, 0:64, :] = raw[c][start + i]
                ref[c, i, 64:66, :] = around_ref[pl.ds(right + EDGES + 8 * c + 2 * (start + i), 2), :]
                ref[c, i, 66:68, :] = around_ref[pl.ds(left + EDGES + 8 * c + 2 * (start + i), 2), :]
                ref[c, i, 68:72, :] = jnp.ones((4, 128), jnp.float32)


def bulk_kernel(rho_ref, vel_ref, pre_ref, ext_ref, cor_ref, around_ref, out_ref, ua, pa, ub, pb):
    core = lax.axis_index("fluid") % 2
    left, right = side_rows()
    lane = lax.broadcasted_iota(jnp.int32, (8, 128), 1)
    first, last = lane == 0, lane == 127

    def put(planes, rows, raw):
        state, prim = from_raw(*raw)
        for c in range(5):
            ua[c, planes, rows, :] = state[c]
            pa[c, planes, rows, :] = prim[c]

    def own(i, _):
        for r in range(0, 64, 8):
            rows = pl.ds(r, 8)
            put(i + 2, pl.ds(r + YOFF, 8), (rho_ref[i, rows, :], vel_ref[0, i, rows, :], vel_ref[1, i, rows, :], vel_ref[2, i, rows, :], pre_ref[i, rows, :]))
        put(i + 2, pl.ds(YOFF - 2, 2), [around_ref[pl.ds(left + EDGES + 8 * c + 2 * i, 2), :] for c in range(5)])
        put(i + 2, pl.ds(YOFF + 64, 2), [around_ref[pl.ds(right + EDGES + 8 * c + 2 * i, 2), :] for c in range(5)])
        return 0

    lax.fori_loop(0, 4, own, 0)

    def halo(i, _):
        for ref, base in ((ext_ref, 6 * core), (cor_ref, 6 - 6 * core)):
            for r in range(0, 64, 8):
                put(base + i, pl.ds(r + YOFF, 8), [ref[c, i, pl.ds(r, 8), :] for c in range(5)])
            put(base + i, pl.ds(YOFF + 64, 2), [ref[c, i, pl.ds(64, 2), :] for c in range(5)])
            put(base + i, pl.ds(YOFF - 2, 2), [ref[c, i, pl.ds(66, 2), :] for c in range(5)])
        return 0

    lax.fori_loop(0, 2, halo, 0)

    def update(u, q, i, r, n):
        def load(plane, row):
            rows = pl.ds(row, n)
            return [u[c, plane, rows, :] for c in range(5)], [q[c, plane, rows, :] for c in range(5)]

        here, prim = load(i, r)
        acc = None
        for d, (up, down) in enumerate((((i + 1, r), (i - 1, r)), ((i, r + 1), (i, r - 1)))):
            uu, uq = load(*up)
            du, dq = load(*down)
            acc = add_direction(acc, here, prim, uu, uq, du, dq, d)

        def shifted(x, sign, step, edge):
            return jnp.where(edge[:n], sign * x if sign < 0 else x, pltpu.roll(x, step, 1))

        signs = (1, 1, 1, -1, 1)
        qsigns = (None, None, -1, 1, 1)
        zu = [shifted(here[c], signs[c], 127, last) for c in range(5)]
        zd = [shifted(here[c], signs[c], 1, first) for c in range(5)]
        zuq = [None if qsigns[c] is None else shifted(prim[c], qsigns[c], 127, last) for c in range(5)]
        zdq = [None if qsigns[c] is None else shifted(prim[c], qsigns[c], 1, first) for c in range(5)]
        acc = add_direction(acc, here, prim, zu, zuq, zd, zdq, 2)
        return [here[c] - KFL * acc[c] for c in range(5)]

    def step_one(i, _):
        for r, n in [(YOFF - 8, 8)] + [(YOFF + k, 8) for k in range(0, 72, 8)]:
            if r == YOFF - 8:
                r, n = YOFF - 1, 1
            if r == YOFF + 64:
                n = 1
            new = update(ua, pa, i, r, n)
            prim = euler_prims(*new)
            for c in range(5):
                ub[c, i, pl.ds(r, n), :] = new[c]
                pb[c, i, pl.ds(r, n), :] = prim[c]
        return 0

    lax.fori_loop(1, 7, step_one, 0)

    def step_two(i, _):
        for r in range(0, 64, 8):
            new = update(ub, pb, i + 2, r + YOFF, 8)
            for c in range(5):
                out_ref[c, i, pl.ds(r, 8), :] = new[c]
        return 0

    lax.fori_loop(0, 4, step_two, 0)


def bulk_euler(density, velocity, pressure, ext, cor, around):
    return local_call(
        bulk_kernel,
        (5, 4, 64, 128),
        "bulk_euler",
        (density, velocity, pressure, ext, cor, around),
        scratch=[pltpu.VMEM((5, 8, YROWS, 128), jnp.float32)] * 4,
        flops=60_000_000,
    )


def body(
    density,
    velocity,
    pressure,
    deck_disp,
    deck_prev,
    stay_stiff,
    stay_tension,
    anchor_node,
    failed_stay,
    facet_cells,
    facet_owner,
    facet_row,
    facet_count,
):
    count = lax.axis_size("fluid")
    outward = [(i, (i + 1) % count if i % 2 else (i - 1) % count) for i in range(count)]
    inward = [(i, i ^ 1) for i in range(count)]
    ext, cor, own, edge = local_call(
        prep_kernel, [(24, 128), (24, 128), (16, 256), (80, 128)], "prep", (density, velocity, pressure, deck_disp, deck_prev)
    )
    ext = lax.ppermute(ext, "fluid", outward)
    cor = lax.ppermute(cor, "fluid", inward)
    tab, pos, place = local_call(
        table_kernel,
        [(8, 128), (8, 128), jax.ShapeDtypeStruct((128, 128), jnp.bfloat16)],
        "tables",
        (facet_cells, facet_owner, facet_row.reshape(1, -1), facet_count),
        smem=(3,),
    )
    block, deck = local_call(
        middle_kernel,
        [(4, 128, 128), (2, 72, 128)],
        "middle",
        (ext, cor, own, deck_disp, deck_prev, tab, edge),
        scratch=[pltpu.VMEM((2, 128, 128), jnp.float32)],
    )
    around = lax.all_to_all(block, "sect", split_axis=0, concat_axis=0, tiled=True).reshape(512, 128)
    facets = local_call(
        facet_kernel, (512, 128), "facets", (around, facet_cells, tab, pos), scratch=[pltpu.VMEM((16, 128), jnp.float32)], flops=4_000_000
    )
    got = lax.all_to_all(facets.reshape(64, 8, 128), "fluid", split_axis=0, concat_axis=0, tiled=True).reshape(512, 128)
    early = local_call(
        early_kernel,
        (4, 72, 256),
        "early_deck",
        (around, deck, stay_stiff.reshape(1, -1), stay_tension.reshape(1, -1), anchor_node.reshape(1, -1), failed_stay),
        scratch=[pltpu.VMEM((2, 128, 128), jnp.float32)],
        smem=(5,),
    )
    ext_planes, cor_planes = local_call(pack_kernel, [(5, 2, 72, 128), (5, 2, 72, 128)], "pack", (density, velocity, pressure, around))
    ext_planes = lax.ppermute(ext_planes, "fluid", outward)
    cor_planes = lax.ppermute(cor_planes, "fluid", inward)
    fields = bulk_euler(density, velocity, pressure, ext_planes, cor_planes, around)
    deck_next, back = local_call(
        deck_kernel, [(64, 128), (64, 2, 128)], "deck", (got, early), scratch=[pltpu.VMEM((512, 128), jnp.float32)], flops=4_000_000
    )
    back = lax.all_to_all(back, "fluid", split_axis=0, concat_axis=0, tiled=True)
    facet_disp = local_call(final_kernel, (128, 128), "final", (back.reshape(128, 128), place))
    return (fields, deck_next, facet_disp)


def solution(mesh):
    return jax.shard_map(
        body,
        mesh=mesh,
        in_specs=(
            P("fluid", "sect", None),
            P(None, "fluid", "sect", None),
            P("fluid", "sect", None),
            P("fluid", "sect"),
            P("fluid", "sect"),
            P(),
            P(),
            P(),
            P(),
            P(("fluid", "sect"), None),
            P(("fluid", "sect"), None),
            P(("fluid", "sect")),
            P(("fluid", "sect")),
        ),
        out_specs=(P(None, "fluid", "sect", None), P("fluid", "sect"), P(("fluid", "sect"), None)),
        check_vma=False,
    )
```

time: 123 us -> 66.7 us (0.54)
  starting transfers between devices: 60.6 us -> 25.8 us
  matrix products: 20.4 us -> 0 us
  blocking collectives: 0 us -> 10.5 us
  waiting for transfers between devices: 21.5 us -> 11.5 us
  Pallas kernels: 4.38 us -> 10.1 us
  other arithmetic: 4.29 us -> 0 us
  local copies, waits for them, and re-layouts: 8.56 us -> 6.09 us
    all_to_all x3 -> x2, starting transfers between devices: 31.9 us -> 11.3 us  [the longest x1 6.35 us: body(): lax.all_to_all(facets.reshape(64, 8, 128), 'fluid', split_axis=0, concat_...]
    dot_general x17 -> x0, matrix products: 20.4 us -> none  [pick_rows(): return jnp.dot(selector, table, precision=lax.Precision.HIGHEST)]
    ppermute x12 -> x4, starting transfers between devices: 28.8 us -> 14.6 us  [the longest x1 6.39 us: body(): cor = lax.ppermute(cor, 'fluid', inward)]
    all_to_all x0 -> x1, blocking collectives: none -> 10.5 us  [body(): lax.all_to_all(block, 'sect', split_axis=0, concat_axis=0, tiled=True)]
    all_to_all x3 -> x2, waiting for transfers between devices: 20 us -> 11.5 us  [the longest x1 5.75 us: body(): lax.all_to_all(facets.reshape(64, 8, 128), 'fluid', split_axis=0, concat_...]
    unnamed x22 -> x33, local copies, waits for them, and re-layouts: 0.09 us -> 6.09 us
    pallas_call x1 -> x9, Pallas kernels: 4.38 us -> 10.1 us  [local_call(): pl.pallas_call(kernel, out_shape=outs, in_specs=specs, out_specs=vmem(len...]
    eq x8 -> x0, local copies, waits for them, and re-layouts: 5.72 us -> none  [sample_group(): picker = (flat_ids[:, None] == cell_ids[None, :]).astype(jnp.float32)]
  transfers between devices with their start and end apart: 15 -> 6, of which waited for: 4 -> 2; matrix products, arithmetic and copies ran while one was open for 11% -> 0% of each run, Pallas kernels for 0% -> 11%
where the time goes in v1:
time: 66.7 us; the launch traced here: 66.1 us
  starting transfers between devices  25.8 us (39%)
  waiting for transfers between devices  11.5 us (17%)
  blocking collectives  10.5 us (16%)
  Pallas kernels  10.1 us (15%)
  local copies, waits for them, and re-layouts  6.09 us (9%)
  between operations  2.1 us (3%)
    all_to_all x1, blocking collectives, body(): lax.all_to_all(block, 'sect', split_axis=0, concat_axis=0, tiled=True)  10.5 us
    pallas_call x9, Pallas kernels, local_call(): pl.pallas_call(kernel, out_shape=outs, in_specs=specs, out_specs=vmem(len...  10.1 us
    ppermute x1, starting transfers between devices, body(): cor = lax.ppermute(cor, 'fluid', inward)  6.39 us
    all_to_all x1, starting transfers between devices, body(): lax.all_to_all(facets.reshape(64, 8, 128), 'fluid', split_axis=0, concat_...  6.35 us
    unnamed x33, local copies, waits for them, and re-layouts  6.09 us
    all_to_all x1, waiting for transfers between devices, body(): lax.all_to_all(facets.reshape(64, 8, 128), 'fluid', split_axis=0, concat_...  5.75 us
    all_to_all x1, waiting for transfers between devices, body(): lax.all_to_all(back, 'fluid', split_axis=0, concat_axis=0, tiled=True)  5.71 us
    all_to_all x1, starting transfers between devices, body(): lax.all_to_all(back, 'fluid', split_axis=0, concat_axis=0, tiled=True)  4.91 us
  transfers between devices with their start and end apart: 6, of which 2 were waited for; matrix products, arithmetic and copies ran while one was open for 0% of the time, Pallas kernels for 11%

profile of v1, /device:TPU:1, one launch (start us, length us, event | category | flops | bytes accessed | tf_op | source)
XLA Modules:
  0.0 66.1 jit_solution(13261670008834044946)
XLA Ops:
  0.6 0.0 copy-start
  0.6 1.0 %copy-done = f32[3,4,64,128]{3,2,1,0:T(8,128)S(1)} copy-done((f32[3,4,64,128]{3,2,1,0:T(8,128)S(1)}, f32[3,4,64,128]{3,2,1,0:T(8,128)}, u32[]{:S(2)}) %copy-start) | copy-done | bytes 393240
  1.6 0.0 copy-start.2
  1.6 0.9 %copy-done.2 = f32[4,64,128]{2,1,0:T(8,128)S(1)} copy-done((f32[4,64,128]{2,1,0:T(8,128)S(1)}, f32[4,64,128]{2,1,0:T(8,128)}, u32[]{:S(2)}) %copy-start.2) | copy-done | bytes 131096
  2.5 0.0 copy-start.4
  2.5 0.9 %copy-done.4 = f32[4,64,128]{2,1,0:T(8,128)S(1)} copy-done((f32[4,64,128]{2,1,0:T(8,128)S(1)}, f32[4,64,128]{2,1,0:T(8,128)}, u32[]{:S(2)}) %copy-start.4) | copy-done | bytes 131096
  3.4 0.8 %copy-done.7 = f32[64,128]{1,0:T(8,128)S(1)} copy-done((f32[64,128]{1,0:T(8,128)S(1)}, f32[64,128]{1,0:T(8,128)}, u32[]{:S(2)}) %copy-start.7) | copy-done | bytes 32792
  4.2 0.0 copy-start.9
  4.2 0.8 %copy-done.9 = f32[64,128]{1,0:T(8,128)S(1)} copy-done((f32[64,128]{1,0:T(8,128)S(1)}, f32[64,128]{1,0:T(8,128)}, u32[]{:S(2)}) %copy-start.9) | copy-done | bytes 32792
  5.0 0.0 copy-start.15
  5.0 0.4 prep.1
  5.3 0.0 copy-start.6
  5.3 2.7 %collective-permute-start = (f32[24,128]{1,0:T(8,128)S(1)}, f32[24,128]{1,0:T(8,128)S(1)}, u32[]{:S(2)}, u32[]{:S(2)}) collective-permute-start(f32[24,128]{1,0:T(8,128)S(1)} %get-tuple-element.16), channel_id=1, source_target_pairs={{0,252},{4,8},{8,4},{12,16},{16,12},{20,24},{24,20},{28,32},{32,28... | collective-permute-start | bytes 36872 | tf_op jit(solution)/shard_map/ppermute | solution.py:470
  8.0 6.4 %collective-permute-start.1 = (f32[24,128]{1,0:T(8,128)S(1)}, f32[24,128]{1,0:T(8,128)S(1)}, u32[]{:S(2)}, u32[]{:S(2)}) collective-permute-start(f32[24,128]{1,0:T(8,128)S(1)} %get-tuple-element.17), channel_id=1, source_target_pairs={{0,4},{4,0},{8,12},{12,8},{16,20},{20,16},{24,28},{28,24},{32,36},... | collective-permute-start | bytes 36872 | tf_op jit(solution)/shard_map/ppermute | solution.py:471
  15.1 0.0 copy-done.15
  15.1 0.1 copy.16.owner_ref
  15.2 0.0 copy-done.6
  15.2 0.6 copy-done.14
  15.8 0.4 tables.1
  16.3 0.0 collective-permute-done.ext_ref
  16.3 0.0 collective-permute-done.1.cor_ref
  16.3 0.3 copy-done.8
  16.6 0.0 copy-done.10
  16.6 0.1 middle.1
  16.7 10.5 %all_to_all.15 = f32[4,128,128]{2,1,0:T(8,128)S(1)} all-to-all(f32[4,128,128]{2,1,0:T(8,128)S(1)} %get-tuple-element.21), channel_id=1, replica_groups=mesh['fluid'=64,'sect'=4] {'sect'}, dimensions={0} | all-to-all | bytes 524288 | tf_op jit(solution)/shard_map/all_to_all | solution.py:486
  27.2 1.7 %facets.1 = f32[512,128]{1,0:T(8,128)} custom-call(f32[512,128]{1,0:T(8,128)S(1)} %bitcast.8, s32[128,128]{1,0:T(8,128)S(1)} %copy-done.6, f32[8,128]{1,0:T(8,128)S(1)} %get-tuple-element.19.tab_ref, f32[8,128]{1,0:T(8,128)S(1)} %get-tuple-element.24.pos_ref), custom_call_target="tpu_custom_call" | custom-call | flops 4000000 | bytes 1000000 | tf_op jit(solution)/shard_map/facets/pallas_call | solution.py:29
  28.9 6.3 %all-to-all-start.1 = ((f32[64,8,128]{2,1,0:T(8,128)}), f32[64,8,128]{2,1,0:T(8,128)S(1)}, u32[]{:S(2)}, u32[]{:S(2)}) async-start(f32[64,8,128]{2,1,0:T(8,128)} %bitcast.2), calls=%async_computation.1 | async-start | bytes 524288 | tf_op jit(solution)/shard_map/all_to_all | solution.py:490
  35.3 0.0 copy-done.5
  35.3 0.0 copy-done.1
  35.3 0.0 copy-done.3
  35.3 0.0 copy-start.12
  35.3 0.0 copy-start.13
  35.3 0.1 pack.1
  35.4 1.7 %collective-permute-start.2 = (f32[5,2,72,128]{3,2,1,0:T(8,128)S(1)}, f32[5,2,72,128]{3,2,1,0:T(8,128)S(1)}, u32[]{:S(2)}, u32[]{:S(2)}) collective-permute-start(f32[5,2,72,128]{3,2,1,0:T(8,128)S(1)} %get-tuple-element.22), channel_id=1, source_target_pairs={{0,252},{4,8},{8,4},{12,16},{16,12},{20,24},{24,20},{28,32},{32,28... | collective-permute-start | bytes 1105928 | tf_op jit(solution)/shard_map/ppermute | solution.py:500
  37.1 3.8 %collective-permute-start.3 = (f32[5,2,72,128]{3,2,1,0:T(8,128)S(1)}, f32[5,2,72,128]{3,2,1,0:T(8,128)S(1)}, u32[]{:S(2)}, u32[]{:S(2)}) collective-permute-start(f32[5,2,72,128]{3,2,1,0:T(8,128)S(1)} %get-tuple-element.23), channel_id=1, source_target_pairs={{0,4},{4,0},{8,12},{12,8},{16,20},{20,16},{24,28},{28,24},{32,36},... | collective-permute-start | bytes 1105928 | tf_op jit(solution)/shard_map/ppermute | solution.py:501
  41.6 0.0 copy-start.11
  41.6 0.0 copy-done.12
  41.6 0.0 copy-done.13
  41.6 0.7 copy-done.11
  42.3 0.5 early_deck.1.early_ref
  42.7 5.7 %all-to-all-done.1 = f32[64,8,128]{2,1,0:T(8,128)S(1)} async-done(((f32[64,8,128]{2,1,0:T(8,128)}), f32[64,8,128]{2,1,0:T(8,128)S(1)}, u32[]{:S(2)}, u32[]{:S(2)}) %all-to-all-start.1) | async-done | bytes 262176 | tf_op jit(solution)/shard_map/all_to_all | solution.py:490
  48.5 1.8 %deck.1 = (f32[64,128]{1,0:T(8,128)}, f32[64,2,128]{2,1,0:T(2,128)}) custom-call(f32[512,128]{1,0:T(8,128)S(1)} %bitcast.12, f32[4,72,256]{2,1,0:T(8,128)S(1)} %early_deck.1.early_ref), custom_call_target="tpu_custom_call" | custom-call | flops 4000000 | bytes 1000000 | tf_op jit(solution)/shard_map/deck/pallas_call | solution.py:29
  50.3 4.9 %all-to-all-start.2 = ((f32[64,2,128]{2,1,0:T(2,128)}), f32[64,2,128]{2,1,0:T(2,128)S(1)}, u32[]{:S(2)}, u32[]{:S(2)}) async-start(f32[64,2,128]{2,1,0:T(2,128)} %get-tuple-element.27), calls=%async_computation.2 | async-start | bytes 131072 | tf_op jit(solution)/shard_map/all_to_all | solution.py:506
  55.2 0.0 collective-permute-done.2.ext_ref
  55.2 0.0 collective-permute-done.3.cor_ref
  55.2 4.4 %bulk_euler.1 = f32[5,4,64,128]{3,2,1,0:T(8,128)} custom-call(f32[4,64,128]{2,1,0:T(8,128)S(1)} %copy-done.3, f32[3,4,64,128]{3,2,1,0:T(8,128)S(1)} %copy-done.1, f32[4,64,128]{2,1,0:T(8,128)S(1)} %copy-done.5, f32[5,2,72,128]{3,2,1,0:T(8,128)S(1)} %collective-permute-done.2.ext_ref, f32[5,2,72,128]{3,2,1,0:T(8,128)S(1)} %collective-permute-done.3.cor_ref, ...), custom_call_target="tpu_custom_call" | custom-call | flops 60000000 | bytes 1000000 | tf_op jit(solution)/shard_map/bulk_euler/pallas_call | solution.py:29
  59.6 5.7 %all-to-all-done.2 = f32[64,2,128]{2,1,0:T(2,128)S(1)} async-done(((f32[64,2,128]{2,1,0:T(2,128)}), f32[64,2,128]{2,1,0:T(2,128)S(1)}, u32[]{:S(2)}, u32[]{:S(2)}) %all-to-all-start.2) | async-done | bytes 65568 | tf_op jit(solution)/shard_map/all_to_all | solution.py:506
  65.3 0.8 %final.1 = f32[128,128]{1,0:T(8,128)} custom-call(f32[128,128]{1,0:T(8,128)S(1)} %bitcast.13, bf16[128,128]{1,0:T(8,128)(2,1)S(1)} %get-tuple-element.28.place_ref), custom_call_target="tpu_custom_call" | custom-call | flops 1000000 | bytes 1000000 | tf_op jit(solution)/shard_map/final/pallas_call | solution.py:29
  (7 shorter events, 0.0 us)
Async XLA Ops:
  0.6 1.0 %copy-start = (f32[3,4,64,128]{3,2,1,0:T(8,128)S(1)}, f32[3,4,64,128]{3,2,1,0:T(8,128)}, u32[]{:S(2)}) copy-start(f32[3,4,64,128]{3,2,1,0:T(8,128)} %vel_ref.5) | copy-start | bytes 1179652
  1.6 0.9 %copy-start.2 = (f32[4,64,128]{2,1,0:T(8,128)S(1)}, f32[4,64,128]{2,1,0:T(8,128)}, u32[]{:S(2)}) copy-start(f32[4,64,128]{2,1,0:T(8,128)} %rho_ref.5) | copy-start | bytes 393220
  2.5 0.9 %copy-start.4 = (f32[4,64,128]{2,1,0:T(8,128)S(1)}, f32[4,64,128]{2,1,0:T(8,128)}, u32[]{:S(2)}) copy-start(f32[4,64,128]{2,1,0:T(8,128)} %pre_ref.5) | copy-start | bytes 393220
  3.4 0.8 %copy-start.7 = (f32[64,128]{1,0:T(8,128)S(1)}, f32[64,128]{1,0:T(8,128)}, u32[]{:S(2)}) copy-start(f32[64,128]{1,0:T(8,128)} %w_ref.3) | copy-start | bytes 98308
  4.2 0.8 %copy-start.9 = (f32[64,128]{1,0:T(8,128)S(1)}, f32[64,128]{1,0:T(8,128)}, u32[]{:S(2)}) copy-start(f32[64,128]{1,0:T(8,128)} %u_ref.3) | copy-start | bytes 98308
  5.0 10.1 %copy-start.15 = (s32[128,1]{0,1:T(1,128)S(1)}, s32[128,1]{0,1:T(1,128)}, u32[]{:S(2)}) copy-start(s32[128,1]{0,1:T(1,128)} %param.23) | copy-start | bytes 1540
  5.3 9.9 %copy-start.6 = (s32[128,128]{1,0:T(8,128)S(1)}, s32[128,128]{1,0:T(8,128)}, u32[]{:S(2)}) copy-start(s32[128,128]{1,0:T(8,128)} %cells_ref.3) | copy-start | bytes 196612
  5.3 10.9 %collective-permute-start = (f32[24,128]{1,0:T(8,128)S(1)}, f32[24,128]{1,0:T(8,128)S(1)}, u32[]{:S(2)}, u32[]{:S(2)}) collective-permute-start(f32[24,128]{1,0:T(8,128)S(1)} %get-tuple-element.16), channel_id=1, source_target_pairs={{0,252},{4,8},{8,4},{12,16},{16,12},{20,24},{24,20},{28,32},{32,28... | collective-permute-start | bytes 36872 | tf_op jit(solution)/shard_map/ppermute | solution.py:470
  8.0 8.3 %collective-permute-start.1 = (f32[24,128]{1,0:T(8,128)S(1)}, f32[24,128]{1,0:T(8,128)S(1)}, u32[]{:S(2)}, u32[]{:S(2)}) collective-permute-start(f32[24,128]{1,0:T(8,128)S(1)} %get-tuple-element.17), channel_id=1, source_target_pairs={{0,4},{4,0},{8,12},{12,8},{16,20},{20,16},{24,28},{28,24},{32,36},... | collective-permute-start | bytes 36872 | tf_op jit(solution)/shard_map/ppermute | solution.py:471
  15.2 0.7 copy-start.14
  15.8 0.8 %copy-start.8 = (f32[64,128]{1,0:T(8,128)S(1)}, f32[64,128]{1,0:T(8,128)}, u32[]{:S(2)}) copy-start(f32[64,128]{1,0:T(8,128)} %w_ref.3) | copy-start | bytes 98308
  15.8 0.8 %copy-start.10 = (f32[64,128]{1,0:T(8,128)S(1)}, f32[64,128]{1,0:T(8,128)}, u32[]{:S(2)}) copy-start(f32[64,128]{1,0:T(8,128)} %u_ref.3) | copy-start | bytes 98308
  27.2 8.1 %copy-start.5 = (f32[4,64,128]{2,1,0:T(8,128)S(1)}, f32[4,64,128]{2,1,0:T(8,128)}, u32[]{:S(2)}) copy-start(f32[4,64,128]{2,1,0:T(8,128)} %pre_ref.5) | copy-start | bytes 393220
  28.9 6.4 %copy-start.1 = (f32[3,4,64,128]{3,2,1,0:T(8,128)S(1)}, f32[3,4,64,128]{3,2,1,0:T(8,128)}, u32[]{:S(2)}) copy-start(f32[3,4,64,128]{3,2,1,0:T(8,128)} %vel_ref.5) | copy-start | bytes 1179652
  28.9 6.4 %copy-start.3 = (f32[4,64,128]{2,1,0:T(8,128)S(1)}, f32[4,64,128]{2,1,0:T(8,128)}, u32[]{:S(2)}) copy-start(f32[4,64,128]{2,1,0:T(8,128)} %rho_ref.5) | copy-start | bytes 393220
  28.9 19.5 %all-to-all-start.1 = ((f32[64,8,128]{2,1,0:T(8,128)}), f32[64,8,128]{2,1,0:T(8,128)S(1)}, u32[]{:S(2)}, u32[]{:S(2)}) async-start(f32[64,8,128]{2,1,0:T(8,128)} %bitcast.2), calls=%async_computation.1 | async-start | bytes 524288 | tf_op jit(solution)/shard_map/all_to_all | solution.py:490
  35.3 6.3 %copy-start.12 = (f32[168]{0:T(256)S(1)}, f32[168]{0:T(256)}, u32[]{:S(2)}) copy-start(f32[168]{0:T(256)} %param.19) | copy-start | bytes 2020
  35.3 6.3 %copy-start.13 = (s32[168]{0:T(256)S(1)}, s32[168]{0:T(256)}, u32[]{:S(2)}) copy-start(s32[168]{0:T(256)} %param.20) | copy-start | bytes 2020
  35.4 19.8 %collective-permute-start.2 = (f32[5,2,72,128]{3,2,1,0:T(8,128)S(1)}, f32[5,2,72,128]{3,2,1,0:T(8,128)S(1)}, u32[]{:S(2)}, u32[]{:S(2)}) collective-permute-start(f32[5,2,72,128]{3,2,1,0:T(8,128)S(1)} %get-tuple-element.22), channel_id=1, source_target_pairs={{0,252},{4,8},{8,4},{12,16},{16,12},{20,24},{24,20},{28,32},{32,28... | collective-permute-start | bytes 1105928 | tf_op jit(solution)/shard_map/ppermute | solution.py:500
  37.1 18.1 %collective-permute-start.3 = (f32[5,2,72,128]{3,2,1,0:T(8,128)S(1)}, f32[5,2,72,128]{3,2,1,0:T(8,128)S(1)}, u32[]{:S(2)}, u32[]{:S(2)}) collective-permute-start(f32[5,2,72,128]{3,2,1,0:T(8,128)S(1)} %get-tuple-element.23), channel_id=1, source_target_pairs={{0,4},{4,0},{8,12},{12,8},{16,20},{20,16},{24,28},{28,24},{32,36},... | collective-permute-start | bytes 1105928 | tf_op jit(solution)/shard_map/ppermute | solution.py:501
  41.6 0.7 %copy-start.11 = (f32[168]{0:T(256)S(1)}, f32[168]{0:T(256)}, u32[]{:S(2)}) copy-start(f32[168]{0:T(256)} %param.18) | copy-start | bytes 2020
  50.3 15.0 %all-to-all-start.2 = ((f32[64,2,128]{2,1,0:T(2,128)}), f32[64,2,128]{2,1,0:T(2,128)S(1)}, u32[]{:S(2)}, u32[]{:S(2)}) async-start(f32[64,2,128]{2,1,0:T(2,128)} %get-tuple-element.27), calls=%async_computation.2 | async-start | bytes 131072 | tf_op jit(solution)/shard_map/all_to_all | solution.py:506

commit v2 on v1

--- a/solution.py
+++ b/solution.py
@@ -14,29 +14,30 @@
 TABLE = 64
 DECK = 72
 EDGES = 88
+PER = 7
+VALUES = 64
 NT = (((1,), (1,)), ((), ()))
 NN = (((1,), (0,)), ((), ()))
 
 
-def vmem(count):
-    return [pl.BlockSpec(memory_space=pltpu.VMEM)] * count
-
-
-def local_call(kernel, shapes, name, args, scratch=(), flops=1_000_000, smem=()):
-    single = not isinstance(shapes, list)
-    outs = [s if isinstance(s, jax.ShapeDtypeStruct) else jax.ShapeDtypeStruct(s, jnp.float32) for s in ([shapes] if single else shapes)]
-    specs = [pl.BlockSpec(memory_space=pltpu.SMEM if i in smem else pltpu.VMEM) for i in range(len(args))]
-    result = pl.pallas_call(
+def local_call(kernel, shapes, name, args, scratch=(), flops=1_000_000, smem=(), hbm=(), out_hbm=(), free=False):
+    outs = [jax.ShapeDtypeStruct(*s) if free else pltpu.HBM(*s) if i in out_hbm else pltpu.VMEM(*s) for i, s in enumerate(shapes)]
+    spaces = [pltpu.SMEM if i in smem else pltpu.HBM if i in hbm else pltpu.VMEM for i in range(len(args))]
+    args = [pltpu.with_memory_space_constraint(a, pltpu.HBM) if i in hbm else a for i, a in enumerate(args)]
+    return pl.pallas_call(
         kernel,
         out_shape=outs,
-        in_specs=specs,
-        out_specs=vmem(len(outs)),
+        in_specs=[pl.BlockSpec(memory_space=s) for s in spaces],
+        out_specs=[pl.BlockSpec(memory_space=pltpu.HBM if i in out_hbm else pltpu.VMEM) for i in range(len(outs))],
         scratch_shapes=list(scratch),
         compiler_params=pltpu.CompilerParams(vmem_limit_bytes=32 * 1024 * 1024),
         cost_estimate=pl.CostEstimate(flops=flops, bytes_accessed=1_000_000, transcendentals=0),
         name=name,
     )(*args)
-    return result[0] if single else result
+
+
+def floats(*shape):
+    return shape, jnp.float32
 
 
 def iota(shape, axis):
@@ -103,32 +104,50 @@
     return out
 
 
-def prep_kernel(rho_ref, vel_ref, pre_ref, w_ref, u_ref, ext_ref, cor_ref, own_ref, edge_ref):
+def prep_kernel(rho_hbm, vel_hbm, pre_hbm, w_hbm, u_hbm, raw_ref, wu_ref, ext_ref, cor_ref, own_ref, sems):
     core = lax.axis_index("fluid") % 2
+    pairs = [
+        (rho_hbm, raw_ref.at[0]),
+        (vel_hbm, raw_ref.at[pl.ds(1, 3)]),
+        (pre_hbm, raw_ref.at[4]),
+        (w_hbm, wu_ref.at[0]),
+        (u_hbm, wu_ref.at[1]),
+    ]
+    copies = [pltpu.make_async_copy(a, b, sems.at[i]) for i, (a, b) in enumerate(pairs)]
+    for copy in copies:
+        copy.start()
     chooser = iota((16, 128), 0) == iota((16, 128), 1)
-    raw = [rho_ref, vel_ref.at[0], vel_ref.at[1], vel_ref.at[2], pre_ref]
     own_ref[15:16, :] = jnp.zeros((1, 256), jnp.float32)
+    ext_ref[22:24, :] = jnp.zeros((2, 128), jnp.float32)
+    cor_ref[22:24, :] = jnp.zeros((2, 128), jnp.float32)
+    for copy in copies:
+        copy.wait()
     for c in range(5):
-        own_ref[3 * c : 3 * c + 3, :] = pick(chooser, raw[c][...].reshape(256, 128), NT)[0:3]
-        for side, y in ((0, 0), (1, 62)):
-            for i in range(4):
-                edge_ref[pl.ds(40 * side + 8 * c + 2 * i, 2), :] = raw[c][i, pl.ds(y, 2), :]
+        own_ref[3 * c : 3 * c + 3, :] = pick(chooser, raw_ref[c].reshape(256, 128), NT)[0:3]
     first, last = own_ref[:, 0:128], own_ref[:, 128:256]
     even = core == 0
     ext_ref[0:16, :] = jnp.where(even, first, last)
     cor_ref[0:16, :] = jnp.where(even, last, first)
-    wf, wl, uf, ul = w_ref[0:4, :], w_ref[60:64, :], u_ref[0:2, :], u_ref[62:64, :]
+    wf, wl, uf, ul = wu_ref[0, 0:4, :], wu_ref[0, 60:64, :], wu_ref[1, 0:2, :], wu_ref[1, 62:64, :]
     ext_ref[16:20, :] = jnp.where(even, wf, wl)
     cor_ref[16:20, :] = jnp.where(even, wl, wf)
     ext_ref[20:22, :] = jnp.where(even, uf, ul)
     cor_ref[20:22, :] = jnp.where(even, ul, uf)
-    ext_ref[22:24, :] = jnp.zeros((2, 128), jnp.float32)
-    cor_ref[22:24, :] = jnp.zeros((2, 128), jnp.float32)
-
-
-def table_kernel(cells_ref, owner_ref, row_ref, count_ref, tab_ref, pos_ref, place_ref):
-    owner = jnp.broadcast_to(owner_ref[...].astype(jnp.float32), (128, 128))
-    owner_row = owner.T
+
+
+def table_kernel(cells_hbm, owner_hbm, row_hbm, raw_ref, count_ref, tab_ref, pos_ref, place_ref, cells_ref, edge_ref, slots_ref, sems):
+    pairs = [(cells_hbm, cells_ref), (owner_hbm, slots_ref.at[pl.ds(0, 1)]), (row_hbm, slots_ref.at[pl.ds(8, 1)])]
+    copies = [pltpu.make_async_copy(a, b, sems.at[i]) for i, (a, b) in enumerate(pairs)]
+    for copy in copies:
+        copy.start()
+    for c in range(5):
+        for side, y in ((0, 0), (1, 62)):
+            for i in range(4):
+                edge_ref[pl.ds(40 * side + 8 * c + 2 * i, 2), :] = raw_ref[c, i, pl.ds(y, 2), :]
+    for copy in copies:
+        copy.wait()
+    owner_row = jnp.broadcast_to(slots_ref[0:1, :].astype(jnp.float32), (128, 128))
+    owner = owner_row.T
     same = owner == owner_row
     down, along = iota((128, 128), 0), iota((128, 128), 1)
     within = jnp.sum(jnp.where(same & (along < down), 1.0, 0.0), axis=1, keepdims=True)
@@ -142,12 +161,12 @@
     cells = cells_ref[...].astype(jnp.float32).astype(jnp.bfloat16)
     picked = lax.dot_general(columns, cells, NT, preferred_element_type=jnp.float32)
     live = iota((1, 128), 1) < count_ref[0]
-    code = jnp.where(live, row_ref[...] + 128, 0).astype(jnp.float32)
+    code = jnp.where(live, slots_ref[8:9, :] + 128, 0).astype(jnp.float32)
     stacked = jnp.where(r == 4, jnp.broadcast_to(code, (16, 128)), picked).astype(jnp.bfloat16)
     tab_ref[...] = lax.dot_general(stacked, place, NN, preferred_element_type=jnp.float32)[0:8]
 
 
-def middle_kernel(ext_ref, cor_ref, own_ref, w_ref, u_ref, tab_ref, edge_ref, out_ref, deck_ref, wide):
+def middle_kernel(ext_ref, cor_ref, own_ref, wu_ref, tab_ref, edge_ref, out_ref, deck_ref, wide):
     fluid, sect = lax.axis_index("fluid"), lax.axis_index("sect")
     even = fluid % 2 == 0
     ext, cor = ext_ref[...], cor_ref[...]
@@ -155,13 +174,13 @@
     low_deck = jnp.where(fluid == 0, 0.0, low[16:24])
     high_deck = jnp.where(fluid == 63, 0.0, high[16:24])
     wide[...] = jnp.zeros((2, 128, 128), jnp.float32)
-    wide[0, 0:4, :] = low_deck[0:4]
-    wide[0, 4:68, :] = w_ref[...]
-    wide[0, 68:72, :] = high_deck[0:4]
-    wide[1, 2:4, :] = low_deck[4:6]
-    wide[1, 4:68, :] = u_ref[...]
-    wide[1, 68:70, :] = high_deck[4:6]
-    deck_ref[...] = wide[:, 0:72, :]
+    wide[0, 4:8, :] = low_deck[0:4]
+    wide[0, 8:72, :] = wu_ref[0]
+    wide[0, 72:76, :] = high_deck[0:4]
+    wide[1, 6:8, :] = low_deck[4:6]
+    wide[1, 8:72, :] = wu_ref[1]
+    wide[1, 72:74, :] = high_deck[4:6]
+    deck_ref[...] = wide[:, 0:80, :]
     w_columns, u_columns = wide[0].T, wide[1].T
     pieces = [low[0:16], own_ref[:, 0:128], own_ref[:, 128:256], high[0:16], tab_ref[...], w_columns[0:4], w_columns[124:128], u_columns[0:2], u_columns[126:128], jnp.zeros((4, 128), jnp.float32)]
     block = jnp.concatenate(pieces, axis=0)
@@ -228,6 +247,11 @@
     return [euler_prims(*final[i])[3] for i in range(2)]
 
 
+def by_seven(k):
+    whole = (k * 9363) >> 16
+    return whole, k - PER * whole
+
+
 def gather_lanes(tables, cells):
     index = cells & 127
     low = jnp.take_along_axis(jnp.broadcast_to(tables[0], cells.shape), index, axis=1, mode="promise_in_bounds")
@@ -235,8 +259,8 @@
     return jnp.where(cells < 128, low, high) - AMBIENT
 
 
-def facet_kernel(around_ref, cells_ref, tab_ref, pos_ref, out_ref, press):
-    fluid, sect = lax.axis_index("fluid"), lax.axis_index("sect")
+def facet_kernel(around_ref, cells_ref, tab_ref, pos_ref, out_hbm, press, out_ref, sems):
+    sect = lax.axis_index("sect")
     left, right = side_rows()
     first, second = wall_press(around_ref)
     press[0:8, :] = first
@@ -245,36 +269,51 @@
     def tables(s):
         return press[pl.ds(s, 1), :], press[pl.ds(s + 8, 1), :]
 
-    values = gather_lanes(tables(sect), cells_ref[...])
-    r = iota((512, 128), 0)
-    wanted = 2 * (r >> 3) + (r & 7) - 2
-    chooser = (pos_ref[0:1, :].astype(jnp.int32) == wanted) & ((r & 7) < 6)
-    out_ref[...] = pick(chooser, values)
     left_tab = around_ref[pl.ds(left + TABLE, 8), :]
     right_tab = around_ref[pl.ds(right + TABLE, 8), :]
     left_values = gather_lanes(tables(lax.rem(sect + 3, 4)), left_tab.astype(jnp.int32))
     right_values = gather_lanes(tables(lax.rem(sect + 1, 4)), right_tab.astype(jnp.int32))
     left_code = jnp.where(sect == 0, 0.0, left_tab[4:5])
     right_code = jnp.where(sect == 3, 0.0, right_tab[4:5])
-    rows = [tab_ref[4:5, :], left_code, left_values[2:3], left_values[3:4], right_code, right_values[0:1], right_values[1:2]]
-    spread = jnp.concatenate([jnp.broadcast_to(x, (8, 128)) for x in rows] + [jnp.zeros((72, 128), jnp.float32)], axis=0)
-    place = iota((128, 128), 0) & 7
-    weights = jnp.concatenate([jnp.where(place == 2, spread, 0.0), jnp.where(place == 3, spread, 0.0)], axis=1)
+    codes = jnp.concatenate([jnp.broadcast_to(x, (8, 128)) for x in (tab_ref[4:5, :], left_code, right_code)], axis=0)
+    four = jnp.concatenate([left_values[2:4], right_values[0:2]], axis=0)
+    eight = jnp.concatenate([four, four], axis=0)
+
+    def weights(i):
+        here = jnp.where((iota((24, 128), 0) & 7) == 2 + i, codes, 0.0)
+        there = jnp.where((iota((8, 128), 0) >> 2) == i, eight, 0.0)
+        return jnp.concatenate([here, jnp.zeros((48, 128), jnp.float32), there, jnp.zeros((48, 128), jnp.float32)], axis=0)
+
     o, p = iota((64, 256), 0), iota((64, 256), 1)
-    base = pick(2 * o + (p >> 7) == (p & 127), weights, NT)
-    owner = iota((64, 128), 0)
+    base = pick(2 * o + (p >> 7) == (p & 127), jnp.concatenate([weights(0), weights(1)], axis=1), NT)
+    owner, in_codes = iota((64, 128), 0), iota((64, 128), 1) < VALUES
     before = jnp.where(owner == 0, 0.0, pltpu.roll(base, 1, 0))
     after = jnp.where(owner == 63, 0.0, pltpu.roll(base, 63, 0))
-    meta = base + pltpu.roll(before, 126, 1) + pltpu.roll(after, 2, 1)
-    out_ref[pl.ds(7, 64, stride=8), :] = meta
-
-
-def bending_of(w):
-    def laplace(x):
-        rows, lanes = x.shape
-        return pltpu.roll(x, 1, 0) + pltpu.roll(x, rows - 1, 0) + pltpu.roll(x, 1, 1) + pltpu.roll(x, lanes - 1, 1) - 4.0 * x
-
-    return laplace(laplace(w))
+    meta = base + jnp.where(in_codes, pltpu.roll(before, 126, 1), pltpu.roll(before, 120, 1))
+    meta = meta + jnp.where(in_codes, pltpu.roll(after, 2, 1), pltpu.roll(after, 8, 1))
+    parts = split3(gather_lanes(tables(sect), cells_ref[...]))
+    copies = []
+    size = 16 * PER
+    for i in range(4):
+        r = iota((size, 128), 0) + size * i
+        whole, place = by_seven(r)
+        chooser = (pos_ref[0:1, :].astype(jnp.int32) == 2 * whole + place - 2) & (place < 6)
+        chooser = chooser.astype(jnp.float32).astype(jnp.bfloat16)
+        total = None
+        for part in parts:
+            term = lax.dot_general(chooser, part, NN, preferred_element_type=jnp.float32)
+            total = term if total is None else total + term
+        out_ref[pl.ds(size * i, size), :] = total
+        out_ref[pl.ds(size * i + 6, 16, stride=PER), :] = meta[16 * i : 16 * i + 16]
+        copies.append(pltpu.make_async_copy(out_ref.at[pl.ds(size * i, size)], out_hbm.at[pl.ds(size * i, size)], sems.at[i]))
+        copies[-1].start()
+    for copy in copies:
+        copy.wait()
+
+
+def spread_sides(x):
+    lanes = x.shape[1]
+    return pltpu.roll(x, 1, 1) + pltpu.roll(x, lanes - 1, 1)
 
 
 def early_kernel(around_ref, deck_ref, stiff_ref, tension_ref, anchor_ref, failed_ref, out_ref, turn):
@@ -285,76 +324,96 @@
     turn[0, 124:128, :] = jnp.where(sect == 0, 0.0, around_ref[pl.ds(left + DECK + 4, 4), :])
     turn[1, 0:2, :] = jnp.where(sect == 3, 0.0, around_ref[pl.ds(right + DECK + 8, 2), :])
     turn[1, 126:128, :] = jnp.where(sect == 0, 0.0, around_ref[pl.ds(left + DECK + 10, 2), :])
-    w = jnp.concatenate([deck_ref[0], turn[0].T[0:72]], axis=1)
-    u = jnp.concatenate([deck_ref[1], turn[1].T[0:72]], axis=1)
+    w = jnp.concatenate([deck_ref[0], turn[0].T[0:80]], axis=1)
+    u = jnp.concatenate([deck_ref[1], turn[1].T[0:80]], axis=1)
     anchor = anchor_ref[...]
     count = anchor.shape[1]
     alive = iota((1, count), 1) != failed_ref[0]
-    row = (anchor >> 9) - 64 * fluid + 4
+    row = (anchor >> 9) - 64 * fluid + 8
     column = (anchor & 511) - 128 * sect
     lane = jnp.where((column >= -4) & (column < 132) & alive, column & 255, -1)
-    rows = iota((72, count), 0) == row
+    rows = iota((80, count), 0) == row
     columns = iota((256, count), 0) == lane
     alpha = pick(rows, jnp.where(columns, stiff_ref[...], 0.0), NT)
     beta = pick(rows, jnp.where(columns, tension_ref[...], 0.0), NT)
-    first = 2.0 * w - u + STEP_DECK * (beta - alpha * w - bending_of(w))
-    r, c = iota((72, 256), 0) - 4 + 64 * fluid, iota((72, 256), 1)
-    c = jnp.where(c < 132, c, c - 256) + 128 * sect
-    inside = (r >= 0) & (r < 4096) & (c >= 0) & (c < 512) & (c >= 128 * sect - 4)
+
+    def laplace(x):
+        return pltpu.roll(x, 1, 0) + pltpu.roll(x, 79, 0) + spread_sides(x) - 4.0 * x
+
+    first = 2.0 * w - u + STEP_DECK * (beta - alpha * w - laplace(laplace(w)))
+    r, c = iota((80, 256), 0) - 8, iota((80, 256), 1)
+    c = jnp.where(c < 132, c, c - 256)
+    g, h = r + 64 * fluid, c + 128 * sect
+    inside = (g >= 0) & (g < 4096) & (h >= 0) & (h < 512) & (c >= -2) & (c < 130) & (r >= -2) & (r < 66)
     out_ref[0] = w
     out_ref[1] = jnp.where(inside, first, 0.0)
     out_ref[2] = alpha
     out_ref[3] = beta
 
 
-def deck_kernel(got_ref, early_ref, deck_ref, ret_ref, spread):
-    meta = got_ref[pl.ds(7, 64, stride=8), :]
-    for j in range(8):
-        spread[pl.ds(j, 64, stride=8), :] = meta
-    r, c = iota((512, 128), 0), iota((512, 128), 1)
-    own = jnp.where((c & 7) == (r & 7), spread[...], 0.0)
-    kinds = pick((iota((16, 128), 1) >> 3) == iota((16, 128), 0), own, NT)
-    k = iota((1, 512), 1)
-    offset = 64 * ((k & 7) >> 1) - 64 + 4 - 128
-
-    def rows_of(kind):
-        code = kinds[kind : kind + 1].astype(jnp.int32)
-        local = jnp.where((code > 0) & ((k & 7) < 6), code + offset, -1)
-        return iota((72, 512), 0) == local
+def deck_kernel(got_ref, early_ref, deck_ref, ret_ref, spread, sides_ref, turn):
+    count = 64 * PER
+    meta = got_ref[pl.ds(6, 64, stride=PER), :]
+    lane = iota((64, 128), 1)
+    outer = (lane < 2) | (lane >= 126)
+    for j in range(PER):
+        spread[pl.ds(j, 64, stride=PER), :] = meta if j < 6 else jnp.zeros((64, 128), jnp.float32)
+        turned = pltpu.roll(meta, (126 - VALUES - 4 * j) % 128, 1) if j < 6 else meta
+        sides_ref[pl.ds(j, 64, stride=PER), :] = jnp.where(outer, turned, 0.0) if j < 6 else jnp.zeros((64, 128), jnp.float32)
+    c = iota((count, 128), 1)
+    own = jnp.where(((c & 7) == by_seven(iota((count, 128), 0))[1]) & (c < 24), spread[...], 0.0).astype(jnp.bfloat16)
+    chooser = ((iota((16, 128), 1) >> 3) == iota((16, 128), 0)).astype(jnp.float32).astype(jnp.bfloat16)
+    codes = lax.dot_general(chooser, own, NT, preferred_element_type=jnp.float32).astype(jnp.int32)
+    place = by_seven(iota((1, count), 1))[1]
+    offset = 64 * (place >> 1) - 64 + 8 - 128
+
+    def rows_of(which):
+        code = codes[which : which + 1]
+        local = jnp.where(code > 0, code + offset, -1)
+        return iota((80, count), 0) == local
 
     centre = pick(rows_of(0), got_ref[...])
-    lanes = iota((128, 512), 0)
-    from_left = jnp.where(lanes == 126, kinds[2:3], jnp.where(lanes == 127, kinds[3:4], 0.0))
-    from_right = jnp.where(lanes == 0, kinds[5:6], jnp.where(lanes == 1, kinds[6:7], 0.0))
-    sides = pick(rows_of(1), from_left, NT) + pick(rows_of(4), from_right, NT)
+    sides = pick(jnp.concatenate([rows_of(1), rows_of(2)], axis=0), sides_ref[...])
+    edge = iota((80, 128), 1)
+    sides = jnp.where(edge >= 126, sides[0:80], jnp.where(edge < 2, sides[80:160], 0.0))
     load = jnp.concatenate([centre, sides], axis=1)
     first = early_ref[1] + STEP_DECK * load
-    second = 2.0 * first - early_ref[0] + STEP_DECK * (load + early_ref[3] - early_ref[2] * first - bending_of(first))
-    tile = second[4:68, 0:128]
+    turn[8:88, :] = first
+    bend = turn[7:87, :] + turn[9:89, :] + spread_sides(first) - 4.0 * first
+    turn[8:88, :] = bend
+    bend = bend[8:72]
+    around = spread_sides(bend)[:, 0:128]
+    bend = turn[15:79, 0:128] + turn[17:81, 0:128] + around - 4.0 * bend[:, 0:128]
+    own_rows = slice(8, 72)
+    here = first[own_rows, 0:128]
+    force = centre[own_rows] + early_ref[3, own_rows, 0:128] - early_ref[2, own_rows, 0:128] * here
+    tile = 2.0 * here - early_ref[0, own_rows, 0:128] + STEP_DECK * (force - bend)
     deck_ref[...] = tile
+    row = jnp.concatenate([meta[:, 2:3], meta[:, 3:4]], axis=0).astype(jnp.int32) - 128
+    answer = pick(iota((128, 64), 1) == row, tile)
     for i in range(2):
-        row = meta[:, 2 + i : 3 + i].astype(jnp.int32) - 128
-        ret_ref[:, i, :] = pick(iota((64, 64), 1) == row, tile)
+        ret_ref[:, i, :] = answer[64 * i : 64 * i + 64]
 
 
 def final_kernel(got_ref, place_ref, out_ref):
     out_ref[...] = pick(place_ref[...], got_ref[...])
 
 
-def pack_kernel(rho_ref, vel_ref, pre_ref, around_ref, ext_ref, cor_ref):
+def pack_kernel(raw_ref, around_ref, ext_ref, cor_ref):
     core = lax.axis_index("fluid") % 2
     left, right = side_rows()
-    raw = [rho_ref, vel_ref.at[0], vel_ref.at[1], vel_ref.at[2], pre_ref]
     for ref, start in ((ext_ref, 2 * core), (cor_ref, 2 - 2 * core)):
         for c in range(5):
             for i in range(2):
-                ref[c, i, 0:64, :] = raw[c][start + i]
+                ref[c, i, 0:64, :] = raw_ref[c, start + i]
                 ref[c, i, 64:66, :] = around_ref[pl.ds(right + EDGES + 8 * c + 2 * (start + i), 2), :]
                 ref[c, i, 66:68, :] = around_ref[pl.ds(left + EDGES + 8 * c + 2 * (start + i), 2), :]
                 ref[c, i, 68:72, :] = jnp.ones((4, 128), jnp.float32)
 
 
-def bulk_kernel(rho_ref, vel_ref, pre_ref, ext_ref, cor_ref, around_ref, out_ref, ua, pa, ub, pb):
+def bulk_kernel(raw_ref, ext_ref, cor_ref, around_ref, tile_ref, out_hbm, deck_hbm, ua, pa, ub, pb, result, sems):
+    deck_copy = pltpu.make_async_copy(tile_ref, deck_hbm, sems.at[4])
+    deck_copy.start()
     core = lax.axis_index("fluid") % 2
     left, right = side_rows()
     lane = lax.broadcasted_iota(jnp.int32, (8, 128), 1)
@@ -369,7 +428,7 @@
     def own(i, _):
         for r in range(0, 64, 8):
             rows = pl.ds(r, 8)
-            put(i + 2, pl.ds(r + YOFF, 8), (rho_ref[i, rows, :], vel_ref[0, i, rows, :], vel_ref[1, i, rows, :], vel_ref[2, i, rows, :], pre_ref[i, rows, :]))
+            put(i + 2, pl.ds(r + YOFF, 8), [raw_ref[c, i, rows, :] for c in range(5)])
         put(i + 2, pl.ds(YOFF - 2, 2), [around_ref[pl.ds(left + EDGES + 8 * c + 2 * i, 2), :] for c in range(5)])
         put(i + 2, pl.ds(YOFF + 64, 2), [around_ref[pl.ds(right + EDGES + 8 * c + 2 * i, 2), :] for c in range(5)])
         return 0
@@ -429,20 +488,28 @@
         for r in range(0, 64, 8):
             new = update(ub, pb, i + 2, r + YOFF, 8)
             for c in range(5):
-                out_ref[c, i, pl.ds(r, 8), :] = new[c]
+                result[c, i, pl.ds(r, 8), :] = new[c]
         return 0
 
-    lax.fori_loop(0, 4, step_two, 0)
-
-
-def bulk_euler(density, velocity, pressure, ext, cor, around):
+    copies = []
+    for i in range(4):
+        step_two(i, 0)
+        copies.append(pltpu.make_async_copy(result.at[:, i], out_hbm.at[:, i], sems.at[i]))
+        copies[-1].start()
+    for copy in copies:
+        copy.wait()
+    deck_copy.wait()
+
+
+def bulk_euler(raw, ext, cor, around, tile):
     return local_call(
         bulk_kernel,
-        (5, 4, 64, 128),
+        [floats(5, 4, 64, 128), floats(64, 128)],
         "bulk_euler",
-        (density, velocity, pressure, ext, cor, around),
-        scratch=[pltpu.VMEM((5, 8, YROWS, 128), jnp.float32)] * 4,
+        (raw, ext, cor, around, tile),
+        scratch=[pltpu.VMEM((5, 8, YROWS, 128), jnp.float32)] * 4 + [pltpu.VMEM((5, 4, 64, 128), jnp.float32), pltpu.SemaphoreType.DMA((5,))],
         flops=60_000_000,
+        out_hbm=(0, 1),
     )
 
 
@@ -464,47 +531,65 @@
     count = lax.axis_size("fluid")
     outward = [(i, (i + 1) % count if i % 2 else (i - 1) % count) for i in range(count)]
     inward = [(i, i ^ 1) for i in range(count)]
-    ext, cor, own, edge = local_call(
-        prep_kernel, [(24, 128), (24, 128), (16, 256), (80, 128)], "prep", (density, velocity, pressure, deck_disp, deck_prev)
+    raw, wu, ext, cor, own = local_call(
+        prep_kernel,
+        [floats(5, 4, 64, 128), floats(2, 64, 128), floats(24, 128), floats(24, 128), floats(16, 256)],
+        "prep",
+        (density, velocity, pressure, deck_disp, deck_prev),
+        scratch=[pltpu.SemaphoreType.DMA((5,))],
+        hbm=range(5),
     )
     ext = lax.ppermute(ext, "fluid", outward)
     cor = lax.ppermute(cor, "fluid", inward)
-    tab, pos, place = local_call(
+    tab, pos, place, cells, edge = local_call(
         table_kernel,
-        [(8, 128), (8, 128), jax.ShapeDtypeStruct((128, 128), jnp.bfloat16)],
+        [floats(8, 128), floats(8, 128), ((128, 128), jnp.bfloat16), ((128, 128), jnp.int32), floats(80, 128)],
         "tables",
-        (facet_cells, facet_owner, facet_row.reshape(1, -1), facet_count),
-        smem=(3,),
+        (facet_cells, facet_owner.reshape(1, -1), facet_row.reshape(1, -1), raw, facet_count),
+        scratch=[pltpu.VMEM((16, 128), jnp.int32), pltpu.SemaphoreType.DMA((3,))],
+        hbm=range(3),
+        smem=(4,),
     )
     block, deck = local_call(
         middle_kernel,
-        [(4, 128, 128), (2, 72, 128)],
+        [floats(4, 128, 128), floats(2, 80, 128)],
         "middle",
-        (ext, cor, own, deck_disp, deck_prev, tab, edge),
+        (ext, cor, own, wu, tab, edge),
         scratch=[pltpu.VMEM((2, 128, 128), jnp.float32)],
     )
     around = lax.all_to_all(block, "sect", split_axis=0, concat_axis=0, tiled=True).reshape(512, 128)
-    facets = local_call(
-        facet_kernel, (512, 128), "facets", (around, facet_cells, tab, pos), scratch=[pltpu.VMEM((16, 128), jnp.float32)], flops=4_000_000
-    )
-    got = lax.all_to_all(facets.reshape(64, 8, 128), "fluid", split_axis=0, concat_axis=0, tiled=True).reshape(512, 128)
-    early = local_call(
+    (facets,) = local_call(
+        facet_kernel,
+        [floats(64 * PER, 128)],
+        "facets",
+        (around, cells, tab, pos),
+        scratch=[pltpu.VMEM((16, 128), jnp.float32), pltpu.VMEM((64 * PER, 128), jnp.float32), pltpu.SemaphoreType.DMA((4,))],
+        flops=4_000_000,
+        out_hbm=(0,),
+    )
+    got = lax.all_to_all(facets.reshape(64, 1, PER * 128), "fluid", split_axis=0, concat_axis=0, tiled=True).reshape(64 * PER, 128)
+    (early,) = local_call(
         early_kernel,
-        (4, 72, 256),
+        [floats(4, 80, 256)],
         "early_deck",
         (around, deck, stay_stiff.reshape(1, -1), stay_tension.reshape(1, -1), anchor_node.reshape(1, -1), failed_stay),
         scratch=[pltpu.VMEM((2, 128, 128), jnp.float32)],
         smem=(5,),
     )
-    ext_planes, cor_planes = local_call(pack_kernel, [(5, 2, 72, 128), (5, 2, 72, 128)], "pack", (density, velocity, pressure, around))
+    ext_planes, cor_planes = local_call(pack_kernel, [floats(5, 2, 72, 128), floats(5, 2, 72, 128)], "pack", (raw, around))
     ext_planes = lax.ppermute(ext_planes, "fluid", outward)
     cor_planes = lax.ppermute(cor_planes, "fluid", inward)
-    fields = bulk_euler(density, velocity, pressure, ext_planes, cor_planes, around)
-    deck_next, back = local_call(
-        deck_kernel, [(64, 128), (64, 2, 128)], "deck", (got, early), scratch=[pltpu.VMEM((512, 128), jnp.float32)], flops=4_000_000
+    tile, back = local_call(
+        deck_kernel,
+        [floats(64, 128), floats(64, 2, 128)],
+        "deck",
+        (got, early),
+        scratch=[pltpu.VMEM((64 * PER, 128), jnp.float32)] * 2 + [pltpu.VMEM((96, 256), jnp.float32)],
+        flops=4_000_000,
     )
     back = lax.all_to_all(back, "fluid", split_axis=0, concat_axis=0, tiled=True)
-    facet_disp = local_call(final_kernel, (128, 128), "final", (back.reshape(128, 128), place))
+    fields, deck_next = bulk_euler(raw, ext_planes, cor_planes, around, tile)
+    (facet_disp,) = local_call(final_kernel, [floats(128, 128)], "final", (back.reshape(128, 128), place), free=True)
     return (fields, deck_next, facet_disp)
 
 

time: 66.7 us -> 62.1 us (0.931)
  local copies, waits for them, and re-layouts: 6.09 us -> 0.67 us
  Pallas kernels: 10.1 us -> 11.6 us
    unnamed x33 -> x6, local copies, waits for them, and re-layouts: 6.09 us -> 0.67 us
    pallas_call x9, Pallas kernels: 10.1 us -> 11.6 us  [local_call(): pl.pallas_call(kernel, out_shape=outs, in_specs=[pl.BlockSpec(memory_spac...]
  transfers between devices with their start and end apart: 6 -> 6, of which waited for: 2 -> 2; matrix products, arithmetic and copies ran while one was open for 0% -> 0% of each run, Pallas kernels for 11% -> 12%
where the time goes in v2:
time: 62.1 us; the launch traced here: 61.7 us
  starting transfers between devices  25.8 us (42%)
  Pallas kernels  11.6 us (19%)
  waiting for transfers between devices  11 us (18%)
  blocking collectives  10.5 us (17%)
  between operations  2.08 us (3%)
  local copies, waits for them, and re-layouts  0.67 us (1%)
    pallas_call x9, Pallas kernels, local_call(): pl.pallas_call(kernel, out_shape=outs, in_specs=[pl.BlockSpec(memory_spac...  11.6 us
    all_to_all x1, blocking collectives, body(): lax.all_to_all(block, 'sect', split_axis=0, concat_axis=0, tiled=True)  10.5 us
    all_to_all x1, starting transfers between devices, body(): lax.all_to_all(facets.reshape(64, 1, PER * 128), 'fluid', split_axis=0, c...  6.5 us
    ppermute x1, starting transfers between devices, body(): cor = lax.ppermute(cor, 'fluid', inward)  6.39 us
    all_to_all x1, waiting for transfers between devices, body(): lax.all_to_all(back, 'fluid', split_axis=0, concat_axis=0, tiled=True)  5.87 us
    all_to_all x1, waiting for transfers between devices, body(): lax.all_to_all(facets.reshape(64, 1, PER * 128), 'fluid', split_axis=0, c...  5.16 us
    all_to_all x1, starting transfers between devices, body(): lax.all_to_all(back, 'fluid', split_axis=0, concat_axis=0, tiled=True)  4.75 us
    ppermute x1, starting transfers between devices, body(): cor_planes = lax.ppermute(cor_planes, 'fluid', inward)  3.77 us
  transfers between devices with their start and end apart: 6, of which 2 were waited for; matrix products, arithmetic and copies ran while one was open for 0% of the time, Pallas kernels for 12%

profile of v2, /device:TPU:1, one launch (start us, length us, event | category | flops | bytes accessed | tf_op | source)
XLA Modules:
  0.0 61.7 jit_solution(4883558092293159354)
XLA Ops:
  0.6 1.5 %prep.1 = (f32[5,4,64,128]{3,2,1,0:T(8,128)S(1)}, f32[2,64,128]{2,1,0:T(8,128)S(1)}, f32[24,128]{1,0:T(8,128)S(1)}, f32[24,128]{1,0:T(8,128)S(1)}, f32[16,256]{1,0:T(8,128)S(1)}) custom-call(f32[4,64,128]{2,1,0:T(8,128)} %rho_hbm.1, f32[3,4,64,128]{3,2,1,0:T(8,128)} %vel_hbm.1, f32[4,64,128]{2,1,0:T(8,128)} %pre_hbm.1, f32[64,128]{1,0:T(8,128)} %w_hbm.1, ...), custom_call_target="tpu_custom_call" | custom-call | flops 1000000 | bytes 1000000 | tf_op jit(solution)/shard_map/prep/pallas_call | solution.py:27
  2.2 2.7 %collective-permute-start = (f32[24,128]{1,0:T(8,128)S(1)}, f32[24,128]{1,0:T(8,128)S(1)}, u32[]{:S(2)}, u32[]{:S(2)}) collective-permute-start(f32[24,128]{1,0:T(8,128)S(1)} %get-tuple-element.22), channel_id=1, source_target_pairs={{0,252},{4,8},{8,4},{12,16},{16,12},{20,24},{24,20},{28,32},{32,28... | collective-permute-start | bytes 36872 | tf_op jit(solution)/shard_map/ppermute | solution.py:542
  4.9 6.4 %collective-permute-start.1 = (f32[24,128]{1,0:T(8,128)S(1)}, f32[24,128]{1,0:T(8,128)S(1)}, u32[]{:S(2)}, u32[]{:S(2)}) collective-permute-start(f32[24,128]{1,0:T(8,128)S(1)} %get-tuple-element.23), channel_id=1, source_target_pairs={{0,4},{4,0},{8,12},{12,8},{16,20},{20,16},{24,28},{28,24},{32,36},... | collective-permute-start | bytes 36872 | tf_op jit(solution)/shard_map/ppermute | solution.py:543
  11.9 1.2 %tables.1 = (f32[8,128]{1,0:T(8,128)S(1)}, f32[8,128]{1,0:T(8,128)S(1)}, bf16[128,128]{1,0:T(8,128)(2,1)S(1)}, s32[128,128]{1,0:T(8,128)S(1)}, f32[80,128]{1,0:T(8,128)S(1)}) custom-call(s32[128,128]{1,0:T(8,128)} %cells_hbm.1, s32[1,128]{1,0:T(1,128)} %bitcast.19, s32[1,128]{1,0:T(1,128)} %bitcast.20, f32[5,4,64,128]{3,2,1,0:T(8,128)S(1)} %get-tuple-element.21.raw_ref, ...), custom_call_target="tpu_custom_call" | custom-call | flops 1000000 | bytes 1000000 | tf_op jit(solution)/shard_map/tables/pallas_call | solution.py:27
  13.2 0.0 collective-permute-done.ext_ref
  13.2 0.0 collective-permute-done.1.cor_ref
  13.2 0.1 middle.1
  13.3 10.5 %all_to_all.15 = f32[4,128,128]{2,1,0:T(8,128)S(1)} all-to-all(f32[4,128,128]{2,1,0:T(8,128)S(1)} %get-tuple-element.28), channel_id=1, replica_groups=mesh['fluid'=64,'sect'=4] {'sect'}, dimensions={0} | all-to-all | bytes 524288 | tf_op jit(solution)/shard_map/all_to_all | solution.py:560
  23.8 1.6 %facets.1 = f32[448,128]{1,0:T(8,128)} custom-call(f32[512,128]{1,0:T(8,128)S(1)} %bitcast.9, s32[128,128]{1,0:T(8,128)S(1)} %get-tuple-element.31.cells_ref, f32[8,128]{1,0:T(8,128)S(1)} %get-tuple-element.26.tab_ref, f32[8,128]{1,0:T(8,128)S(1)} %get-tuple-element.32.pos_ref), custom_call_target="tpu_custom_call" | custom-call | flops 4000000 | bytes 1000000 | tf_op jit(solution)/shard_map/facets/pallas_call | solution.py:27
  25.5 6.5 %all-to-all-start.1 = ((f32[64,1,896]{2,1,0:T(1,128)}), f32[64,1,896]{2,1,0:T(1,128)S(1)}, u32[]{:S(2)}, u32[]{:S(2)}) async-start(f32[64,1,896]{2,1,0:T(1,128)} %bitcast.18), calls=%async_computation.1 | async-start | bytes 458752 | tf_op jit(solution)/shard_map/all_to_all | solution.py:570
  32.0 0.0 copy-start.1
  32.0 0.0 copy-start.2
  32.0 0.1 pack.1
  32.1 1.7 %collective-permute-start.2 = (f32[5,2,72,128]{3,2,1,0:T(8,128)S(1)}, f32[5,2,72,128]{3,2,1,0:T(8,128)S(1)}, u32[]{:S(2)}, u32[]{:S(2)}) collective-permute-start(f32[5,2,72,128]{3,2,1,0:T(8,128)S(1)} %get-tuple-element.29), channel_id=1, source_target_pairs={{0,252},{4,8},{8,4},{12,16},{16,12},{20,24},{24,20},{28,32},{32,28... | collective-permute-start | bytes 1105928 | tf_op jit(solution)/shard_map/ppermute | solution.py:580
  33.8 3.8 %collective-permute-start.3 = (f32[5,2,72,128]{3,2,1,0:T(8,128)S(1)}, f32[5,2,72,128]{3,2,1,0:T(8,128)S(1)}, u32[]{:S(2)}, u32[]{:S(2)}) collective-permute-start(f32[5,2,72,128]{3,2,1,0:T(8,128)S(1)} %get-tuple-element.30), channel_id=1, source_target_pairs={{0,4},{4,0},{8,12},{12,8},{16,20},{20,16},{24,28},{28,24},{32,36},... | collective-permute-start | bytes 1105928 | tf_op jit(solution)/shard_map/ppermute | solution.py:581
  38.2 0.0 copy-start
  38.2 0.0 copy-done.1
  38.2 0.0 copy-done.2
  38.2 0.7 %copy-done = f32[168]{0:T(256)S(1)} copy-done((f32[168]{0:T(256)S(1)}, f32[168]{0:T(256)}, u32[]{:S(2)}) %copy-start) | copy-done | bytes 696
  38.9 0.5 early_deck.1.early_ref
  39.4 5.2 %all-to-all-done.1 = f32[64,1,896]{2,1,0:T(1,128)S(1)} async-done(((f32[64,1,896]{2,1,0:T(1,128)}), f32[64,1,896]{2,1,0:T(1,128)S(1)}, u32[]{:S(2)}, u32[]{:S(2)}) %all-to-all-start.1) | async-done | bytes 229408 | tf_op jit(solution)/shard_map/all_to_all | solution.py:570
  44.5 1.6 %deck.1 = (f32[64,128]{1,0:T(8,128)S(1)}, f32[64,2,128]{2,1,0:T(2,128)}) custom-call(f32[448,128]{1,0:T(8,128)S(1)} %bitcast.13, f32[4,80,256]{2,1,0:T(8,128)S(1)} %early_deck.1.early_ref), custom_call_target="tpu_custom_call" | custom-call | flops 4000000 | bytes 1000000 | tf_op jit(solution)/shard_map/deck/pallas_call | solution.py:27
  46.1 4.7 %all-to-all-start.2 = ((f32[64,2,128]{2,1,0:T(2,128)}), f32[64,2,128]{2,1,0:T(2,128)S(1)}, u32[]{:S(2)}, u32[]{:S(2)}) async-start(f32[64,2,128]{2,1,0:T(2,128)} %get-tuple-element.37), calls=%async_computation.2 | async-start | bytes 131072 | tf_op jit(solution)/shard_map/all_to_all | solution.py:590
  50.8 0.0 collective-permute-done.2.ext_ref
  50.8 0.0 collective-permute-done.3.cor_ref
  50.9 4.2 %bulk_euler.1 = (f32[5,4,64,128]{3,2,1,0:T(8,128)}, f32[64,128]{1,0:T(8,128)}) custom-call(f32[5,4,64,128]{3,2,1,0:T(8,128)S(1)} %get-tuple-element.21.raw_ref, f32[5,2,72,128]{3,2,1,0:T(8,128)S(1)} %collective-permute-done.2.ext_ref, f32[5,2,72,128]{3,2,1,0:T(8,128)S(1)} %collective-permute-done.3.cor_ref, f32[512,128]{1,0:T(8,128)S(1)} %bitcast.12, ...), custom_call_target="tpu_custom_call" | custom-call | flops 60000000 | bytes 1000000 | tf_op jit(solution)/shard_map/bulk_euler/pallas_call | solution.py:27
  55.1 5.9 %all-to-all-done.2 = f32[64,2,128]{2,1,0:T(2,128)S(1)} async-done(((f32[64,2,128]{2,1,0:T(2,128)}), f32[64,2,128]{2,1,0:T(2,128)S(1)}, u32[]{:S(2)}, u32[]{:S(2)}) %all-to-all-start.2) | async-done | bytes 65568 | tf_op jit(solution)/shard_map/all_to_all | solution.py:590
  60.9 0.8 %final.1 = f32[128,128]{1,0:T(8,128)} custom-call(f32[128,128]{1,0:T(8,128)S(1)} %bitcast.14, bf16[128,128]{1,0:T(8,128)(2,1)S(1)} %get-tuple-element.38.place_ref), custom_call_target="tpu_custom_call" | custom-call | flops 1000000 | bytes 1000000 | tf_op jit(solution)/shard_map/final/pallas_call | solution.py:27
Async XLA Ops:
  2.2 11.0 %collective-permute-start = (f32[24,128]{1,0:T(8,128)S(1)}, f32[24,128]{1,0:T(8,128)S(1)}, u32[]{:S(2)}, u32[]{:S(2)}) collective-permute-start(f32[24,128]{1,0:T(8,128)S(1)} %get-tuple-element.22), channel_id=1, source_target_pairs={{0,252},{4,8},{8,4},{12,16},{16,12},{20,24},{24,20},{28,32},{32,28... | collective-permute-start | bytes 36872 | tf_op jit(solution)/shard_map/ppermute | solution.py:542
  4.9 8.3 %collective-permute-start.1 = (f32[24,128]{1,0:T(8,128)S(1)}, f32[24,128]{1,0:T(8,128)S(1)}, u32[]{:S(2)}, u32[]{:S(2)}) collective-permute-start(f32[24,128]{1,0:T(8,128)S(1)} %get-tuple-element.23), channel_id=1, source_target_pairs={{0,4},{4,0},{8,12},{12,8},{16,20},{20,16},{24,28},{28,24},{32,36},... | collective-permute-start | bytes 36872 | tf_op jit(solution)/shard_map/ppermute | solution.py:543
  25.5 19.1 %all-to-all-start.1 = ((f32[64,1,896]{2,1,0:T(1,128)}), f32[64,1,896]{2,1,0:T(1,128)S(1)}, u32[]{:S(2)}, u32[]{:S(2)}) async-start(f32[64,1,896]{2,1,0:T(1,128)} %bitcast.18), calls=%async_computation.1 | async-start | bytes 458752 | tf_op jit(solution)/shard_map/all_to_all | solution.py:570
  32.0 6.3 %copy-start.1 = (f32[168]{0:T(256)S(1)}, f32[168]{0:T(256)}, u32[]{:S(2)}) copy-start(f32[168]{0:T(256)} %param.19) | copy-start | bytes 2020
  32.0 6.3 %copy-start.2 = (s32[168]{0:T(256)S(1)}, s32[168]{0:T(256)}, u32[]{:S(2)}) copy-start(s32[168]{0:T(256)} %param.20) | copy-start | bytes 2020
  32.1 18.8 %collective-permute-start.2 = (f32[5,2,72,128]{3,2,1,0:T(8,128)S(1)}, f32[5,2,72,128]{3,2,1,0:T(8,128)S(1)}, u32[]{:S(2)}, u32[]{:S(2)}) collective-permute-start(f32[5,2,72,128]{3,2,1,0:T(8,128)S(1)} %get-tuple-element.29), channel_id=1, source_target_pairs={{0,252},{4,8},{8,4},{12,16},{16,12},{20,24},{24,20},{28,32},{32,28... | collective-permute-start | bytes 1105928 | tf_op jit(solution)/shard_map/ppermute | solution.py:580
  33.8 17.1 %collective-permute-start.3 = (f32[5,2,72,128]{3,2,1,0:T(8,128)S(1)}, f32[5,2,72,128]{3,2,1,0:T(8,128)S(1)}, u32[]{:S(2)}, u32[]{:S(2)}) collective-permute-start(f32[5,2,72,128]{3,2,1,0:T(8,128)S(1)} %get-tuple-element.30), channel_id=1, source_target_pairs={{0,4},{4,0},{8,12},{12,8},{16,20},{20,16},{24,28},{28,24},{32,36},... | collective-permute-start | bytes 1105928 | tf_op jit(solution)/shard_map/ppermute | solution.py:581
  38.2 0.7 %copy-start = (f32[168]{0:T(256)S(1)}, f32[168]{0:T(256)}, u32[]{:S(2)}) copy-start(f32[168]{0:T(256)} %param.18) | copy-start | bytes 2020
  46.1 14.8 %all-to-all-start.2 = ((f32[64,2,128]{2,1,0:T(2,128)}), f32[64,2,128]{2,1,0:T(2,128)S(1)}, u32[]{:S(2)}, u32[]{:S(2)}) async-start(f32[64,2,128]{2,1,0:T(2,128)} %get-tuple-element.37), calls=%async_computation.2 | async-start | bytes 131072 | tf_op jit(solution)/shard_map/all_to_all | solution.py:590

commit v3 on v2

--- a/solution.py
+++ b/solution.py
@@ -10,10 +10,10 @@
 GAMMA_LESS = 0.4
 AMBIENT = 1.0
 
-THIN = 0
 TABLE = 64
 DECK = 72
-EDGES = 88
+EDGES = 80
+BLOCK = 120
 PER = 7
 VALUES = 64
 NT = (((1,), (1,)), ((), ()))
@@ -61,12 +61,6 @@
     return total
 
 
-def side_rows():
-    sect = lax.axis_index("sect")
-    left, right = lax.rem(sect + 3, 4), lax.rem(sect + 1, 4)
-    return pl.multiple_of(left * 128, 128), pl.multiple_of(right * 128, 128)
-
-
 YOFF = 8
 YROWS = 80
 KFL = 0.5 * STEP_FLUID
@@ -104,7 +98,7 @@
     return out
 
 
-def prep_kernel(rho_hbm, vel_hbm, pre_hbm, w_hbm, u_hbm, raw_ref, wu_ref, ext_ref, cor_ref, own_ref, sems):
+def prep_kernel(rho_hbm, vel_hbm, pre_hbm, w_hbm, u_hbm, cells_hbm, owner_hbm, row_hbm, raw_ref, wu_ref, ext_ref, cor_ref, own_ref, cells_ref, slots_ref, sems):
     core = lax.axis_index("fluid") % 2
     pairs = [
         (rho_hbm, raw_ref.at[0]),
@@ -112,6 +106,9 @@
         (pre_hbm, raw_ref.at[4]),
         (w_hbm, wu_ref.at[0]),
         (u_hbm, wu_ref.at[1]),
+        (cells_hbm, cells_ref),
+        (owner_hbm, slots_ref.at[pl.ds(0, 1)]),
+        (row_hbm, slots_ref.at[pl.ds(8, 1)]),
     ]
     copies = [pltpu.make_async_copy(a, b, sems.at[i]) for i, (a, b) in enumerate(pairs)]
     for copy in copies:
@@ -120,7 +117,7 @@
     own_ref[15:16, :] = jnp.zeros((1, 256), jnp.float32)
     ext_ref[22:24, :] = jnp.zeros((2, 128), jnp.float32)
     cor_ref[22:24, :] = jnp.zeros((2, 128), jnp.float32)
-    for copy in copies:
+    for copy in copies[:5]:
         copy.wait()
     for c in range(5):
         own_ref[3 * c : 3 * c + 3, :] = pick(chooser, raw_ref[c].reshape(256, 128), NT)[0:3]
@@ -133,19 +130,15 @@
     cor_ref[16:20, :] = jnp.where(even, wl, wf)
     ext_ref[20:22, :] = jnp.where(even, uf, ul)
     cor_ref[20:22, :] = jnp.where(even, ul, uf)
-
-
-def table_kernel(cells_hbm, owner_hbm, row_hbm, raw_ref, count_ref, tab_ref, pos_ref, place_ref, cells_ref, edge_ref, slots_ref, sems):
-    pairs = [(cells_hbm, cells_ref), (owner_hbm, slots_ref.at[pl.ds(0, 1)]), (row_hbm, slots_ref.at[pl.ds(8, 1)])]
-    copies = [pltpu.make_async_copy(a, b, sems.at[i]) for i, (a, b) in enumerate(pairs)]
-    for copy in copies:
-        copy.start()
+    for copy in copies[5:]:
+        copy.wait()
+
+
+def table_kernel(cells_ref, slots_ref, raw_ref, count_ref, tab_ref, pos_ref, place_ref, edge_ref):
     for c in range(5):
         for side, y in ((0, 0), (1, 62)):
             for i in range(4):
-                edge_ref[pl.ds(40 * side + 8 * c + 2 * i, 2), :] = raw_ref[c, i, pl.ds(y, 2), :]
-    for copy in copies:
-        copy.wait()
+                edge_ref[side, pl.ds(8 * c + 2 * i, 2), :] = raw_ref[c, i, pl.ds(y, 2), :]
     owner_row = jnp.broadcast_to(slots_ref[0:1, :].astype(jnp.float32), (128, 128))
     owner = owner_row.T
     same = owner == owner_row
@@ -160,14 +153,14 @@
     columns = jnp.where(((r < 2) & (c == r)) | ((r >= 2) & (r < 4) & (c == r + 124)), 1.0, 0.0).astype(jnp.bfloat16)
     cells = cells_ref[...].astype(jnp.float32).astype(jnp.bfloat16)
     picked = lax.dot_general(columns, cells, NT, preferred_element_type=jnp.float32)
-    live = iota((1, 128), 1) < count_ref[0]
+    live = iota((1, 128), 1) < count_ref[...]
     code = jnp.where(live, slots_ref[8:9, :] + 128, 0).astype(jnp.float32)
     stacked = jnp.where(r == 4, jnp.broadcast_to(code, (16, 128)), picked).astype(jnp.bfloat16)
     tab_ref[...] = lax.dot_general(stacked, place, NN, preferred_element_type=jnp.float32)[0:8]
 
 
-def middle_kernel(ext_ref, cor_ref, own_ref, wu_ref, tab_ref, edge_ref, out_ref, deck_ref, wide):
-    fluid, sect = lax.axis_index("fluid"), lax.axis_index("sect")
+def middle_kernel(ext_ref, cor_ref, own_ref, wu_ref, tab_ref, edge_ref, up_ref, down_ref, far_ref, deck_ref, wide):
+    fluid = lax.axis_index("fluid")
     even = fluid % 2 == 0
     ext, cor = ext_ref[...], cor_ref[...]
     low, high = jnp.where(even, ext, cor), jnp.where(even, cor, ext)
@@ -182,20 +175,22 @@
     wide[1, 72:74, :] = high_deck[4:6]
     deck_ref[...] = wide[:, 0:80, :]
     w_columns, u_columns = wide[0].T, wide[1].T
-    pieces = [low[0:16], own_ref[:, 0:128], own_ref[:, 128:256], high[0:16], tab_ref[...], w_columns[0:4], w_columns[124:128], u_columns[0:2], u_columns[126:128], jnp.zeros((4, 128), jnp.float32)]
-    block = jnp.concatenate(pieces, axis=0)
-    for t in range(4):
-        out_ref[t, 0:EDGES, :] = block
-        out_ref[t, EDGES:128, :] = edge_ref[0:40, :]
-    out_ref[lax.rem(sect + 1, 4), EDGES:128, :] = edge_ref[40:80, :]
-
-
-def wall_press(around_ref):
+    tiles = [low[0:16], own_ref[:, 0:128], own_ref[:, 128:256], high[0:16]]
+    pad = jnp.zeros((2, 128), jnp.float32)
+    for ref, side, w_part, u_part in ((up_ref, 1, w_columns[124:128], u_columns[126:128]), (down_ref, 0, w_columns[0:4], u_columns[0:2])):
+        ref[0:80, :] = jnp.concatenate(tiles + [tab_ref[...], w_part, u_part, pad], axis=0)
+        ref[EDGES:BLOCK, :] = edge_ref[side]
+    y = iota((16, 128), 1) & 63
+    rim = (y < 2) | (y >= 62)
+    far_ref[...] = sum(pltpu.roll(jnp.where(rim, x, 0.0), 4 * i, 1) if i else jnp.where(rim, x, 0.0) for i, x in enumerate(tiles))
+
+
+def wall_press(thin):
     lane = iota((8, 128), 1)
     low_half, y = lane < 64, lane & 63
 
     def get(t, c, z):
-        part = around_ref[pl.ds(THIN + 16 * t + 3 * c + z, 4, stride=128), :]
+        part = thin[pl.ds(16 * t + 3 * c + z, 4, stride=64), :]
         return jnp.concatenate([part, part], axis=0)
 
     def x_around(tiles):
@@ -259,20 +254,23 @@
     return jnp.where(cells < 128, low, high) - AMBIENT
 
 
-def facet_kernel(around_ref, cells_ref, tab_ref, pos_ref, out_hbm, press, out_ref, sems):
+def facet_kernel(up_ref, left_ref, right_ref, far_ref, cells_ref, tab_ref, pos_ref, out_hbm, thin, press, out_ref, sems):
     sect = lax.axis_index("sect")
-    left, right = side_rows()
-    first, second = wall_press(around_ref)
+    for i, ref in ((0, up_ref), (1, right_ref), (3, left_ref)):
+        thin[64 * i : 64 * i + 64, :] = ref[0:64, :]
+    far = far_ref[...]
+    for i in range(4):
+        thin[128 + 16 * i : 144 + 16 * i, :] = pltpu.roll(far, 128 - 4 * i, 1) if i else far
+    first, second = wall_press(thin)
     press[0:8, :] = first
     press[8:16, :] = second
 
     def tables(s):
-        return press[pl.ds(s, 1), :], press[pl.ds(s + 8, 1), :]
-
-    left_tab = around_ref[pl.ds(left + TABLE, 8), :]
-    right_tab = around_ref[pl.ds(right + TABLE, 8), :]
-    left_values = gather_lanes(tables(lax.rem(sect + 3, 4)), left_tab.astype(jnp.int32))
-    right_values = gather_lanes(tables(lax.rem(sect + 1, 4)), right_tab.astype(jnp.int32))
+        return press[s : s + 1, :], press[s + 8 : s + 9, :]
+
+    left_tab, right_tab = left_ref[TABLE : TABLE + 8, :], right_ref[TABLE : TABLE + 8, :]
+    left_values = gather_lanes(tables(3), left_tab.astype(jnp.int32))
+    right_values = gather_lanes(tables(1), right_tab.astype(jnp.int32))
     left_code = jnp.where(sect == 0, 0.0, left_tab[4:5])
     right_code = jnp.where(sect == 3, 0.0, right_tab[4:5])
     codes = jnp.concatenate([jnp.broadcast_to(x, (8, 128)) for x in (tab_ref[4:5, :], left_code, right_code)], axis=0)
@@ -291,7 +289,7 @@
     after = jnp.where(owner == 63, 0.0, pltpu.roll(base, 63, 0))
     meta = base + jnp.where(in_codes, pltpu.roll(before, 126, 1), pltpu.roll(before, 120, 1))
     meta = meta + jnp.where(in_codes, pltpu.roll(after, 2, 1), pltpu.roll(after, 8, 1))
-    parts = split3(gather_lanes(tables(sect), cells_ref[...]))
+    parts = split3(gather_lanes(tables(0), cells_ref[...]))
     copies = []
     size = 16 * PER
     for i in range(4):
@@ -316,14 +314,15 @@
     return pltpu.roll(x, 1, 1) + pltpu.roll(x, lanes - 1, 1)
 
 
-def early_kernel(around_ref, deck_ref, stiff_ref, tension_ref, anchor_ref, failed_ref, out_ref, turn):
+def early_kernel(left_ref, right_ref, deck_ref, stiff_ref, tension_ref, anchor_ref, failed_ref, out_ref, turn):
     fluid, sect = lax.axis_index("fluid"), lax.axis_index("sect")
-    left, right = side_rows()
     turn[...] = jnp.zeros((2, 128, 128), jnp.float32)
-    turn[0, 0:4, :] = jnp.where(sect == 3, 0.0, around_ref[pl.ds(right + DECK, 4), :])
-    turn[0, 124:128, :] = jnp.where(sect == 0, 0.0, around_ref[pl.ds(left + DECK + 4, 4), :])
-    turn[1, 0:2, :] = jnp.where(sect == 3, 0.0, around_ref[pl.ds(right + DECK + 8, 2), :])
-    turn[1, 126:128, :] = jnp.where(sect == 0, 0.0, around_ref[pl.ds(left + DECK + 10, 2), :])
+    from_left = jnp.where(sect == 0, 0.0, left_ref[DECK : DECK + 8, :])
+    from_right = jnp.where(sect == 3, 0.0, right_ref[DECK : DECK + 8, :])
+    turn[0, 0:4, :] = from_right[0:4]
+    turn[0, 124:128, :] = from_left[0:4]
+    turn[1, 0:2, :] = from_right[4:6]
+    turn[1, 126:128, :] = from_left[4:6]
     w = jnp.concatenate([deck_ref[0], turn[0].T[0:80]], axis=1)
     u = jnp.concatenate([deck_ref[1], turn[1].T[0:80]], axis=1)
     anchor = anchor_ref[...]
@@ -379,13 +378,19 @@
     load = jnp.concatenate([centre, sides], axis=1)
     first = early_ref[1] + STEP_DECK * load
     turn[8:88, :] = first
-    bend = turn[7:87, :] + turn[9:89, :] + spread_sides(first) - 4.0 * first
-    turn[8:88, :] = bend
-    bend = bend[8:72]
-    around = spread_sides(bend)[:, 0:128]
-    bend = turn[15:79, 0:128] + turn[17:81, 0:128] + around - 4.0 * bend[:, 0:128]
+
+    def at(step):
+        return turn[16 + step : 80 + step, :]
+
+    here = at(0)
+    near, two = at(1) + at(-1), at(2) + at(-2)
+    cross = 2.0 * near - 8.0 * here
+    bend = 20.0 * here - 8.0 * near + two
+    for x, step in ((cross, 1), (here, 2)):
+        bend = bend + pltpu.roll(x, step, 1) + pltpu.roll(x, 256 - step, 1)
+    bend = bend[:, 0:128]
     own_rows = slice(8, 72)
-    here = first[own_rows, 0:128]
+    here = here[:, 0:128]
     force = centre[own_rows] + early_ref[3, own_rows, 0:128] - early_ref[2, own_rows, 0:128] * here
     tile = 2.0 * here - early_ref[0, own_rows, 0:128] + STEP_DECK * (force - bend)
     deck_ref[...] = tile
@@ -399,23 +404,21 @@
     out_ref[...] = pick(place_ref[...], got_ref[...])
 
 
-def pack_kernel(raw_ref, around_ref, ext_ref, cor_ref):
+def pack_kernel(raw_ref, left_ref, right_ref, ext_ref, cor_ref):
     core = lax.axis_index("fluid") % 2
-    left, right = side_rows()
     for ref, start in ((ext_ref, 2 * core), (cor_ref, 2 - 2 * core)):
         for c in range(5):
             for i in range(2):
                 ref[c, i, 0:64, :] = raw_ref[c, start + i]
-                ref[c, i, 64:66, :] = around_ref[pl.ds(right + EDGES + 8 * c + 2 * (start + i), 2), :]
-                ref[c, i, 66:68, :] = around_ref[pl.ds(left + EDGES + 8 * c + 2 * (start + i), 2), :]
+                ref[c, i, 64:66, :] = right_ref[pl.ds(EDGES + 8 * c + 2 * (start + i), 2), :]
+                ref[c, i, 66:68, :] = left_ref[pl.ds(EDGES + 8 * c + 2 * (start + i), 2), :]
                 ref[c, i, 68:72, :] = jnp.ones((4, 128), jnp.float32)
 
 
-def bulk_kernel(raw_ref, ext_ref, cor_ref, around_ref, tile_ref, out_hbm, deck_hbm, ua, pa, ub, pb, result, sems):
+def bulk_kernel(raw_ref, ext_ref, cor_ref, left_ref, right_ref, tile_ref, out_hbm, deck_hbm, ua, pa, ub, pb, result, sems):
     deck_copy = pltpu.make_async_copy(tile_ref, deck_hbm, sems.at[4])
     deck_copy.start()
     core = lax.axis_index("fluid") % 2
-    left, right = side_rows()
     lane = lax.broadcasted_iota(jnp.int32, (8, 128), 1)
     first, last = lane == 0, lane == 127
 
@@ -429,8 +432,8 @@
         for r in range(0, 64, 8):
             rows = pl.ds(r, 8)
             put(i + 2, pl.ds(r + YOFF, 8), [raw_ref[c, i, rows, :] for c in range(5)])
-        put(i + 2, pl.ds(YOFF - 2, 2), [around_ref[pl.ds(left + EDGES + 8 * c + 2 * i, 2), :] for c in range(5)])
-        put(i + 2, pl.ds(YOFF + 64, 2), [around_ref[pl.ds(right + EDGES + 8 * c + 2 * i, 2), :] for c in range(5)])
+        put(i + 2, pl.ds(YOFF - 2, 2), [left_ref[pl.ds(EDGES + 8 * c + 2 * i, 2), :] for c in range(5)])
+        put(i + 2, pl.ds(YOFF + 64, 2), [right_ref[pl.ds(EDGES + 8 * c + 2 * i, 2), :] for c in range(5)])
         return 0
 
     lax.fori_loop(0, 4, own, 0)
@@ -501,12 +504,12 @@
     deck_copy.wait()
 
 
-def bulk_euler(raw, ext, cor, around, tile):
+def bulk_euler(raw, ext, cor, left, right, tile):
     return local_call(
         bulk_kernel,
         [floats(5, 4, 64, 128), floats(64, 128)],
         "bulk_euler",
-        (raw, ext, cor, around, tile),
+        (raw, ext, cor, left, right, tile),
         scratch=[pltpu.VMEM((5, 8, YROWS, 128), jnp.float32)] * 4 + [pltpu.VMEM((5, 4, 64, 128), jnp.float32), pltpu.SemaphoreType.DMA((5,))],
         flops=60_000_000,
         out_hbm=(0, 1),
@@ -531,39 +534,38 @@
     count = lax.axis_size("fluid")
     outward = [(i, (i + 1) % count if i % 2 else (i - 1) % count) for i in range(count)]
     inward = [(i, i ^ 1) for i in range(count)]
-    raw, wu, ext, cor, own = local_call(
+    raw, wu, ext, cor, own, cells, slots = local_call(
         prep_kernel,
-        [floats(5, 4, 64, 128), floats(2, 64, 128), floats(24, 128), floats(24, 128), floats(16, 256)],
+        [floats(5, 4, 64, 128), floats(2, 64, 128), floats(24, 128), floats(24, 128), floats(16, 256), ((128, 128), jnp.int32), ((16, 128), jnp.int32)],
         "prep",
-        (density, velocity, pressure, deck_disp, deck_prev),
-        scratch=[pltpu.SemaphoreType.DMA((5,))],
-        hbm=range(5),
+        (density, velocity, pressure, deck_disp, deck_prev, facet_cells, facet_owner.reshape(1, -1), facet_row.reshape(1, -1)),
+        scratch=[pltpu.SemaphoreType.DMA((8,))],
+        hbm=range(8),
     )
     ext = lax.ppermute(ext, "fluid", outward)
     cor = lax.ppermute(cor, "fluid", inward)
-    tab, pos, place, cells, edge = local_call(
-        table_kernel,
-        [floats(8, 128), floats(8, 128), ((128, 128), jnp.bfloat16), ((128, 128), jnp.int32), floats(80, 128)],
-        "tables",
-        (facet_cells, facet_owner.reshape(1, -1), facet_row.reshape(1, -1), raw, facet_count),
-        scratch=[pltpu.VMEM((16, 128), jnp.int32), pltpu.SemaphoreType.DMA((3,))],
-        hbm=range(3),
-        smem=(4,),
-    )
-    block, deck = local_call(
+    tab, pos, place, edge = local_call(
+        table_kernel, [floats(8, 128), floats(8, 128), ((128, 128), jnp.bfloat16), floats(2, 40, 128)], "tables", (cells, slots, raw, facet_count.reshape(1, 1))
+    )
+    up, down, far, deck = local_call(
         middle_kernel,
-        [floats(4, 128, 128), floats(2, 80, 128)],
+        [floats(BLOCK, 128), floats(BLOCK, 128), floats(16, 128), floats(2, 80, 128)],
         "middle",
         (ext, cor, own, wu, tab, edge),
         scratch=[pltpu.VMEM((2, 128, 128), jnp.float32)],
     )
-    around = lax.all_to_all(block, "sect", split_axis=0, concat_axis=0, tiled=True).reshape(512, 128)
+    around = lax.axis_size("sect")
+    forward = [(i, (i + 1) % around) for i in range(around)]
+    backward = [(i, (i - 1) % around) for i in range(around)]
+    far = lax.ppermute(far, "sect", [(i, (i + 2) % around) for i in range(around)])
+    left = lax.ppermute(up, "sect", forward)
+    right = lax.ppermute(down, "sect", backward)
     (facets,) = local_call(
         facet_kernel,
         [floats(64 * PER, 128)],
         "facets",
-        (around, cells, tab, pos),
-        scratch=[pltpu.VMEM((16, 128), jnp.float32), pltpu.VMEM((64 * PER, 128), jnp.float32), pltpu.SemaphoreType.DMA((4,))],
+        (up, left, right, far, cells, tab, pos),
+        scratch=[pltpu.VMEM((256, 128), jnp.float32), pltpu.VMEM((16, 128), jnp.float32), pltpu.VMEM((64 * PER, 128), jnp.float32), pltpu.SemaphoreType.DMA((4,))],
         flops=4_000_000,
         out_hbm=(0,),
     )
@@ -572,11 +574,11 @@
         early_kernel,
         [floats(4, 80, 256)],
         "early_deck",
-        (around, deck, stay_stiff.reshape(1, -1), stay_tension.reshape(1, -1), anchor_node.reshape(1, -1), failed_stay),
+        (left, right, deck, stay_stiff.reshape(1, -1), stay_tension.reshape(1, -1), anchor_node.reshape(1, -1), failed_stay),
         scratch=[pltpu.VMEM((2, 128, 128), jnp.float32)],
-        smem=(5,),
-    )
-    ext_planes, cor_planes = local_call(pack_kernel, [floats(5, 2, 72, 128), floats(5, 2, 72, 128)], "pack", (raw, around))
+        smem=(6,),
+    )
+    ext_planes, cor_planes = local_call(pack_kernel, [floats(5, 2, 72, 128), floats(5, 2, 72, 128)], "pack", (raw, left, right))
     ext_planes = lax.ppermute(ext_planes, "fluid", outward)
     cor_planes = lax.ppermute(cor_planes, "fluid", inward)
     tile, back = local_call(
@@ -588,7 +590,7 @@
         flops=4_000_000,
     )
     back = lax.all_to_all(back, "fluid", split_axis=0, concat_axis=0, tiled=True)
-    fields, deck_next = bulk_euler(raw, ext_planes, cor_planes, around, tile)
+    fields, deck_next = bulk_euler(raw, ext_planes, cor_planes, left, right, tile)
     (facet_disp,) = local_call(final_kernel, [floats(128, 128)], "final", (back.reshape(128, 128), place), free=True)
     return (fields, deck_next, facet_disp)
 

time: 62.1 us -> 59.6 us (0.960)
  blocking collectives: 10.5 us -> 0 us
  starting transfers between devices: 25.8 us -> 32.2 us
  waiting for transfers between devices: 11 us -> 13.8 us
  Pallas kernels: 11.6 us -> 10.7 us
    all_to_all x1 -> x0, blocking collectives: 10.5 us -> none  [body(): lax.all_to_all(block, 'sect', split_axis=0, concat_axis=0, tiled=True)]
    ppermute x0 -> x3, starting transfers between devices: none -> 4.45 us  [the longest x1 2.81 us: body(): right = lax.ppermute(down, 'sect', backward)]
    ppermute x0 -> x3, waiting for transfers between devices: none -> 2.72 us  [the longest x1 2.45 us: body(): lax.ppermute(far, 'sect', [(i, (i + 2) % around) for i in range(around)])]
    all_to_all x1, starting transfers between devices: 6.5 us -> 8.39 us  [body(): lax.all_to_all(facets.reshape(64, 1, PER * 128), 'fluid', split_axis=0, c...]
    pallas_call x9, Pallas kernels: 11.6 us -> 10.7 us  [local_call(): pl.pallas_call(kernel, out_shape=outs, in_specs=[pl.BlockSpec(memory_spac...]
  transfers between devices with their start and end apart: 6 -> 9, of which waited for: 2 -> 4; matrix products, arithmetic and copies ran while one was open for 0% -> 0% of each run, Pallas kernels for 12% -> 11%
where the time goes in v3:
time: 59.6 us; the launch traced here: 59.4 us
  starting transfers between devices  32.2 us (54%)
  waiting for transfers between devices  13.8 us (23%)
  Pallas kernels  10.7 us (18%)
  between operations  2.05 us (3%)
  local copies, waits for them, and re-layouts  0.67 us (1%)
    pallas_call x9, Pallas kernels, local_call(): pl.pallas_call(kernel, out_shape=outs, in_specs=[pl.BlockSpec(memory_spac...  10.7 us
    all_to_all x1, starting transfers between devices, body(): lax.all_to_all(facets.reshape(64, 1, PER * 128), 'fluid', split_axis=0, c...  8.39 us
    ppermute x1, starting transfers between devices, body(): cor = lax.ppermute(cor, 'fluid', inward)  6.39 us
    all_to_all x1, waiting for transfers between devices, body(): lax.all_to_all(back, 'fluid', split_axis=0, concat_axis=0, tiled=True)  5.87 us
    all_to_all x1, waiting for transfers between devices, body(): lax.all_to_all(facets.reshape(64, 1, PER * 128), 'fluid', split_axis=0, c...  5.17 us
    all_to_all x1, starting transfers between devices, body(): lax.all_to_all(back, 'fluid', split_axis=0, concat_axis=0, tiled=True)  4.75 us
    ppermute x1, starting transfers between devices, body(): cor_planes = lax.ppermute(cor_planes, 'fluid', inward)  3.77 us
    ppermute x1, starting transfers between devices, body(): right = lax.ppermute(down, 'sect', backward)  2.81 us
  transfers between devices with their start and end apart: 9, of which 4 were waited for; matrix products, arithmetic and copies ran while one was open for 0% of the time, Pallas kernels for 11%

profile of v3, /device:TPU:1, one launch (start us, length us, event | category | flops | bytes accessed | tf_op | source)
XLA Modules:
  0.0 59.4 jit_solution(10799649645295363900)
XLA Ops:
  0.6 1.6 %prep.1 = (f32[5,4,64,128]{3,2,1,0:T(8,128)S(1)}, f32[2,64,128]{2,1,0:T(8,128)S(1)}, f32[24,128]{1,0:T(8,128)S(1)}, f32[24,128]{1,0:T(8,128)S(1)}, f32[16,256]{1...) custom-call(f32[4,64,128]{2,1,0:T(8,128)} %rho_hbm.1, f32[3,4,64,128]{3,2,1,0:T(8,128)} %vel_hbm.1, ...), custom_call_target="tpu_custom_call" | custom-call | flops 1000000 | bytes 1000000 | tf_op jit(solution)/shard_map/prep/pallas_call | solution.py:27
  2.2 2.7 %collective-permute-start = (f32[24,128]{1,0:T(8,128)S(1)}, f32[24,128]{1,0:T(8,128)S(1)}, u32[]{:S(2)}, u32[]{:S(2)}) collective-permute-start(f32[24,128]{1,0:T(8,128)S(1)} %get-tuple-element.25), channel_id=1, source_target_pairs={{0,252},{4,8},{8,4},{12,16},{16,12},{20,24},{24,20},{28,32},{32,28... | collective-permute-start | bytes 36872 | tf_op jit(solution)/shard_map/ppermute | solution.py:545
  4.9 6.4 %collective-permute-start.1 = (f32[24,128]{1,0:T(8,128)S(1)}, f32[24,128]{1,0:T(8,128)S(1)}, u32[]{:S(2)}, u32[]{:S(2)}) collective-permute-start(f32[24,128]{1,0:T(8,128)S(1)} %get-tuple-element.26), channel_id=1, source_target_pairs={{0,4},{4,0},{8,12},{12,8},{16,20},{20,16},{24,28},{28,24},{32,36},... | collective-permute-start | bytes 36872 | tf_op jit(solution)/shard_map/ppermute | solution.py:546
  11.9 0.4 tables.1
  12.3 0.0 collective-permute-done.ext_ref
  12.3 0.0 collective-permute-done.1.cor_ref
  12.3 0.1 middle.1
  12.5 2.8 %collective-permute-start.3 = (f32[120,128]{1,0:T(8,128)S(1)}, f32[120,128]{1,0:T(8,128)S(1)}, u32[]{:S(2)}, u32[]{:S(2)}) collective-permute-start(f32[120,128]{1,0:T(8,128)S(1)} %get-tuple-element.34), channel_id=1, source_target_pairs={{0,3},{1,0},{2,1},{3,2},{4,7},{5,4},{6,5},{7,6},{8,11},{9,8},{10,9... | collective-permute-start | bytes 184328 | tf_op jit(solution)/shard_map/ppermute | solution.py:562
  15.3 0.0 collective-permute-start.2
  15.3 1.6 %collective-permute-start.6 = (f32[16,128]{1,0:T(8,128)S(1)}, f32[16,128]{1,0:T(8,128)S(1)}, u32[]{:S(2)}, u32[]{:S(2)}) collective-permute-start(f32[16,128]{1,0:T(8,128)S(1)} %get-tuple-element.37), channel_id=1, source_target_pairs={{0,2},{1,3},{2,0},{3,1},{4,6},{5,7},{6,4},{7,5},{8,10},{9,11},{10,... | collective-permute-start | bytes 24584 | tf_op jit(solution)/shard_map/ppermute | solution.py:560
  16.9 2.5 %collective-permute-done.6.far_ref = f32[16,128]{1,0:T(8,128)S(1)} collective-permute-done((f32[16,128]{1,0:T(8,128)S(1)}, f32[16,128]{1,0:T(8,128)S(1)}, u32[]{:S(2)}, u32[]{:S(2)}) %collective-permute-start.6) | collective-permute-done | bytes 8224 | tf_op jit(solution)/shard_map/ppermute | solution.py:560
  19.4 0.0 collective-permute-done.3.right_ref
  19.4 0.3 collective-permute-done.2.left_ref
  19.6 1.7 %facets.1 = f32[448,128]{1,0:T(8,128)} custom-call(f32[120,128]{1,0:T(8,128)S(1)} %get-tuple-element.33.up_ref, f32[120,128]{1,0:T(8,128)S(1)} %collective-permute-done.2.left_ref, f32[120,128]{1,0:T(8,128)S(1)} %collective-permute-done.3.right_ref, f32[16,128]{1,0:T(8,128)S(1)} %collective-permute-done.6.far_ref, ...), custom_call_target="tpu_custom_call" | custom-call | flops 4000000 | bytes 1000000 | tf_op jit(solution)/shard_map/facets/pallas_call | solution.py:27
  21.3 8.4 %all-to-all-start = ((f32[64,1,896]{2,1,0:T(1,128)}), f32[64,1,896]{2,1,0:T(1,128)S(1)}, u32[]{:S(2)}, u32[]{:S(2)}) async-start(f32[64,1,896]{2,1,0:T(1,128)} %bitcast.15), calls=%async_computation | async-start | bytes 458752 | tf_op jit(solution)/shard_map/all_to_all | solution.py:572
  29.7 0.0 copy-start.1
  29.7 0.0 copy-start.2
  29.7 0.1 pack.1
  29.8 1.7 %collective-permute-start.4 = (f32[5,2,72,128]{3,2,1,0:T(8,128)S(1)}, f32[5,2,72,128]{3,2,1,0:T(8,128)S(1)}, u32[]{:S(2)}, u32[]{:S(2)}) collective-permute-start(f32[5,2,72,128]{3,2,1,0:T(8,128)S(1)} %get-tuple-element.35), channel_id=1, source_target_pairs={{0,252},{4,8},{8,4},{12,16},{16,12},{20,24},{24,20},{28,32},{32,28... | collective-permute-start | bytes 1105928 | tf_op jit(solution)/shard_map/ppermute | solution.py:582
  31.5 3.8 %collective-permute-start.5 = (f32[5,2,72,128]{3,2,1,0:T(8,128)S(1)}, f32[5,2,72,128]{3,2,1,0:T(8,128)S(1)}, u32[]{:S(2)}, u32[]{:S(2)}) collective-permute-start(f32[5,2,72,128]{3,2,1,0:T(8,128)S(1)} %get-tuple-element.36), channel_id=1, source_target_pairs={{0,4},{4,0},{8,12},{12,8},{16,20},{20,16},{24,28},{28,24},{32,36},... | collective-permute-start | bytes 1105928 | tf_op jit(solution)/shard_map/ppermute | solution.py:583
  36.0 0.0 copy-start
  36.0 0.0 copy-done.1
  36.0 0.0 copy-done.2
  36.0 0.7 %copy-done = f32[168]{0:T(256)S(1)} copy-done((f32[168]{0:T(256)S(1)}, f32[168]{0:T(256)}, u32[]{:S(2)}) %copy-start) | copy-done | bytes 696
  36.6 0.4 early_deck.1.early_ref
  37.1 5.2 %all-to-all-done = f32[64,1,896]{2,1,0:T(1,128)S(1)} async-done(((f32[64,1,896]{2,1,0:T(1,128)}), f32[64,1,896]{2,1,0:T(1,128)S(1)}, u32[]{:S(2)}, u32[]{:S(2)}) %all-to-all-start) | async-done | bytes 229408 | tf_op jit(solution)/shard_map/all_to_all | solution.py:572
  42.3 1.5 %deck.1 = (f32[64,128]{1,0:T(8,128)S(1)}, f32[64,2,128]{2,1,0:T(2,128)}) custom-call(f32[448,128]{1,0:T(8,128)S(1)} %bitcast.10, f32[4,80,256]{2,1,0:T(8,128)S(1)} %early_deck.1.early_ref), custom_call_target="tpu_custom_call" | custom-call | flops 4000000 | bytes 1000000 | tf_op jit(solution)/shard_map/deck/pallas_call | solution.py:27
  43.7 4.7 %all-to-all-start.1 = ((f32[64,2,128]{2,1,0:T(2,128)}), f32[64,2,128]{2,1,0:T(2,128)S(1)}, u32[]{:S(2)}, u32[]{:S(2)}) async-start(f32[64,2,128]{2,1,0:T(2,128)} %get-tuple-element.43), calls=%async_computation.1 | async-start | bytes 131072 | tf_op jit(solution)/shard_map/all_to_all | solution.py:592
  48.5 0.0 collective-permute-done.4.ext_ref
  48.5 0.0 collective-permute-done.5.cor_ref
  48.5 4.2 %bulk_euler.1 = (f32[5,4,64,128]{3,2,1,0:T(8,128)}, f32[64,128]{1,0:T(8,128)}) custom-call(f32[5,4,64,128]{3,2,1,0:T(8,128)S(1)} %get-tuple-element.24.raw_ref, f32[5,2,72,128]{3,2,1,0:T(8,128)S(1)} %collective-permute-done.4.ext_ref, f32[5,2,72,128]{3,2,1,0:T(8,128)S(1)} %collective-permute-done.5.cor_ref, f32[120,128]{1,0:T(8,128)S(1)} %collective-permute-done.2.left_ref, ...), custom_call_target="tpu_custom_call" | custom-call | flops 60000000 | bytes 1000000 | tf_op jit(solution)/shard_map/bulk_euler/pallas_call | solution.py:27
  52.7 5.9 %all-to-all-done.1 = f32[64,2,128]{2,1,0:T(2,128)S(1)} async-done(((f32[64,2,128]{2,1,0:T(2,128)}), f32[64,2,128]{2,1,0:T(2,128)S(1)}, u32[]{:S(2)}, u32[]{:S(2)}) %all-to-all-start.1) | async-done | bytes 65568 | tf_op jit(solution)/shard_map/all_to_all | solution.py:592
  58.6 0.8 %final.1 = f32[128,128]{1,0:T(8,128)} custom-call(f32[128,128]{1,0:T(8,128)S(1)} %bitcast.11, bf16[128,128]{1,0:T(8,128)(2,1)S(1)} %get-tuple-element.44.place_ref), custom_call_target="tpu_custom_call" | custom-call | flops 1000000 | bytes 1000000 | tf_op jit(solution)/shard_map/final/pallas_call | solution.py:27
Async XLA Ops:
  2.2 10.1 %collective-permute-start = (f32[24,128]{1,0:T(8,128)S(1)}, f32[24,128]{1,0:T(8,128)S(1)}, u32[]{:S(2)}, u32[]{:S(2)}) collective-permute-start(f32[24,128]{1,0:T(8,128)S(1)} %get-tuple-element.25), channel_id=1, source_target_pairs={{0,252},{4,8},{8,4},{12,16},{16,12},{20,24},{24,20},{28,32},{32,28... | collective-permute-start | bytes 36872 | tf_op jit(solution)/shard_map/ppermute | solution.py:545
  4.9 7.4 %collective-permute-start.1 = (f32[24,128]{1,0:T(8,128)S(1)}, f32[24,128]{1,0:T(8,128)S(1)}, u32[]{:S(2)}, u32[]{:S(2)}) collective-permute-start(f32[24,128]{1,0:T(8,128)S(1)} %get-tuple-element.26), channel_id=1, source_target_pairs={{0,4},{4,0},{8,12},{12,8},{16,20},{20,16},{24,28},{28,24},{32,36},... | collective-permute-start | bytes 36872 | tf_op jit(solution)/shard_map/ppermute | solution.py:546
  12.5 6.9 %collective-permute-start.3 = (f32[120,128]{1,0:T(8,128)S(1)}, f32[120,128]{1,0:T(8,128)S(1)}, u32[]{:S(2)}, u32[]{:S(2)}) collective-permute-start(f32[120,128]{1,0:T(8,128)S(1)} %get-tuple-element.34), channel_id=1, source_target_pairs={{0,3},{1,0},{2,1},{3,2},{4,7},{5,4},{6,5},{7,6},{8,11},{9,8},{10,9... | collective-permute-start | bytes 184328 | tf_op jit(solution)/shard_map/ppermute | solution.py:562
  15.3 4.4 %collective-permute-start.2 = (f32[120,128]{1,0:T(8,128)S(1)}, f32[120,128]{1,0:T(8,128)S(1)}, u32[]{:S(2)}, u32[]{:S(2)}) collective-permute-start(f32[120,128]{1,0:T(8,128)S(1)} %get-tuple-element.33.up_ref), channel_id=1, source_target_pairs={{0,1},{1,2},{2,3},{3,0},{4,5},{5,6},{6,7},{7,4},{8,9},{9,10},{10,1... | collective-permute-start | bytes 184328 | tf_op jit(solution)/shard_map/ppermute | solution.py:561
  15.3 4.1 %collective-permute-start.6 = (f32[16,128]{1,0:T(8,128)S(1)}, f32[16,128]{1,0:T(8,128)S(1)}, u32[]{:S(2)}, u32[]{:S(2)}) collective-permute-start(f32[16,128]{1,0:T(8,128)S(1)} %get-tuple-element.37), channel_id=1, source_target_pairs={{0,2},{1,3},{2,0},{3,1},{4,6},{5,7},{6,4},{7,5},{8,10},{9,11},{10,... | collective-permute-start | bytes 24584 | tf_op jit(solution)/shard_map/ppermute | solution.py:560
  21.3 20.9 %all-to-all-start = ((f32[64,1,896]{2,1,0:T(1,128)}), f32[64,1,896]{2,1,0:T(1,128)S(1)}, u32[]{:S(2)}, u32[]{:S(2)}) async-start(f32[64,1,896]{2,1,0:T(1,128)} %bitcast.15), calls=%async_computation | async-start | bytes 458752 | tf_op jit(solution)/shard_map/all_to_all | solution.py:572
  29.7 6.3 %copy-start.1 = (f32[168]{0:T(256)S(1)}, f32[168]{0:T(256)}, u32[]{:S(2)}) copy-start(f32[168]{0:T(256)} %param.19) | copy-start | bytes 2020
  29.7 6.3 %copy-start.2 = (s32[168]{0:T(256)S(1)}, s32[168]{0:T(256)}, u32[]{:S(2)}) copy-start(s32[168]{0:T(256)} %param.20) | copy-start | bytes 2020
  29.8 18.7 %collective-permute-start.4 = (f32[5,2,72,128]{3,2,1,0:T(8,128)S(1)}, f32[5,2,72,128]{3,2,1,0:T(8,128)S(1)}, u32[]{:S(2)}, u32[]{:S(2)}) collective-permute-start(f32[5,2,72,128]{3,2,1,0:T(8,128)S(1)} %get-tuple-element.35), channel_id=1, source_target_pairs={{0,252},{4,8},{8,4},{12,16},{16,12},{20,24},{24,20},{28,32},{32,28... | collective-permute-start | bytes 1105928 | tf_op jit(solution)/shard_map/ppermute | solution.py:582
  31.5 17.0 %collective-permute-start.5 = (f32[5,2,72,128]{3,2,1,0:T(8,128)S(1)}, f32[5,2,72,128]{3,2,1,0:T(8,128)S(1)}, u32[]{:S(2)}, u32[]{:S(2)}) collective-permute-start(f32[5,2,72,128]{3,2,1,0:T(8,128)S(1)} %get-tuple-element.36), channel_id=1, source_target_pairs={{0,4},{4,0},{8,12},{12,8},{16,20},{20,16},{24,28},{28,24},{32,36},... | collective-permute-start | bytes 1105928 | tf_op jit(solution)/shard_map/ppermute | solution.py:583
  36.0 0.7 %copy-start = (f32[168]{0:T(256)S(1)}, f32[168]{0:T(256)}, u32[]{:S(2)}) copy-start(f32[168]{0:T(256)} %param.18) | copy-start | bytes 2020
  43.7 14.8 %all-to-all-start.1 = ((f32[64,2,128]{2,1,0:T(2,128)}), f32[64,2,128]{2,1,0:T(2,128)S(1)}, u32[]{:S(2)}, u32[]{:S(2)}) async-start(f32[64,2,128]{2,1,0:T(2,128)} %get-tuple-element.43), calls=%async_computation.1 | async-start | bytes 131072 | tf_op jit(solution)/shard_map/all_to_all | solution.py:592

commit v4 on v3

--- a/solution.py
+++ b/solution.py
@@ -119,8 +119,9 @@
     cor_ref[22:24, :] = jnp.zeros((2, 128), jnp.float32)
     for copy in copies[:5]:
         copy.wait()
+    thin = pick(chooser, raw_ref[...].reshape(1280, 128), NT)
     for c in range(5):
-        own_ref[3 * c : 3 * c + 3, :] = pick(chooser, raw_ref[c].reshape(256, 128), NT)[0:3]
+        own_ref[3 * c : 3 * c + 3, :] = thin[0:3, 256 * c : 256 * c + 256]
     first, last = own_ref[:, 0:128], own_ref[:, 128:256]
     even = core == 0
     ext_ref[0:16, :] = jnp.where(even, first, last)
@@ -134,7 +135,7 @@
         copy.wait()
 
 
-def table_kernel(cells_ref, slots_ref, raw_ref, count_ref, tab_ref, pos_ref, place_ref, edge_ref):
+def table_kernel(cells_ref, slots_ref, raw_ref, count_ref, tab_ref, choose_ref, place_ref, edge_ref):
     for c in range(5):
         for side, y in ((0, 0), (1, 62)):
             for i in range(4):
@@ -146,7 +147,10 @@
     within = jnp.sum(jnp.where(same & (along < down), 1.0, 0.0), axis=1, keepdims=True)
     within_row = jnp.sum(jnp.where(same & (down < along), 1.0, 0.0), axis=0, keepdims=True)
     position = (2.0 * owner[:, 0:1] + within).astype(jnp.int32)
-    pos_ref[...] = jnp.broadcast_to(2.0 * owner_row[0:1, :] + within_row, (8, 128))
+    whole, spot = by_seven(iota((64 * PER, 128), 0))
+    position_row = (2.0 * owner_row[0:1, :] + within_row).astype(jnp.int32)
+    choose = (position_row == 2 * whole + spot - 2) & (spot < 6)
+    choose_ref[...] = choose.astype(jnp.float32).astype(jnp.bfloat16)
     place = jnp.where(position == along, 1.0, 0.0).astype(jnp.bfloat16)
     place_ref[...] = place
     r, c = iota((16, 128), 0), iota((16, 128), 1)
@@ -254,7 +258,7 @@
     return jnp.where(cells < 128, low, high) - AMBIENT
 
 
-def facet_kernel(up_ref, left_ref, right_ref, far_ref, cells_ref, tab_ref, pos_ref, out_hbm, thin, press, out_ref, sems):
+def facet_kernel(up_ref, left_ref, right_ref, far_ref, cells_ref, tab_ref, choose_ref, out_hbm, thin, press, out_ref, sems):
     sect = lax.axis_index("sect")
     for i, ref in ((0, up_ref), (1, right_ref), (3, left_ref)):
         thin[64 * i : 64 * i + 64, :] = ref[0:64, :]
@@ -293,10 +297,7 @@
     copies = []
     size = 16 * PER
     for i in range(4):
-        r = iota((size, 128), 0) + size * i
-        whole, place = by_seven(r)
-        chooser = (pos_ref[0:1, :].astype(jnp.int32) == 2 * whole + place - 2) & (place < 6)
-        chooser = chooser.astype(jnp.float32).astype(jnp.bfloat16)
+        chooser = choose_ref[pl.ds(size * i, size), :]
         total = None
         for part in parts:
             term = lax.dot_general(chooser, part, NN, preferred_element_type=jnp.float32)
@@ -544,8 +545,8 @@
     )
     ext = lax.ppermute(ext, "fluid", outward)
     cor = lax.ppermute(cor, "fluid", inward)
-    tab, pos, place, edge = local_call(
-        table_kernel, [floats(8, 128), floats(8, 128), ((128, 128), jnp.bfloat16), floats(2, 40, 128)], "tables", (cells, slots, raw, facet_count.reshape(1, 1))
+    tab, choose, place, edge = local_call(
+        table_kernel, [floats(8, 128), ((64 * PER, 128), jnp.bfloat16), ((128, 128), jnp.bfloat16), floats(2, 40, 128)], "tables", (cells, slots, raw, facet_count.reshape(1, 1))
     )
     up, down, far, deck = local_call(
         middle_kernel,
@@ -564,7 +565,7 @@
         facet_kernel,
         [floats(64 * PER, 128)],
         "facets",
-        (up, left, right, far, cells, tab, pos),
+        (up, left, right, far, cells, tab, choose),
         scratch=[pltpu.VMEM((256, 128), jnp.float32), pltpu.VMEM((16, 128), jnp.float32), pltpu.VMEM((64 * PER, 128), jnp.float32), pltpu.SemaphoreType.DMA((4,))],
         flops=4_000_000,
         out_hbm=(0,),

time: 59.6 us -> 59.6 us (level)
  no operation moved by 1% of the time
where the time goes in v4:
time: 59.6 us; the launch traced here: 59.4 us
  starting transfers between devices  32.1 us (54%)
  waiting for transfers between devices  13.8 us (23%)
  Pallas kernels  10.8 us (18%)
  between operations  2.05 us (3%)
  local copies, waits for them, and re-layouts  0.67 us (1%)
    pallas_call x9, Pallas kernels, local_call(): pl.pallas_call(kernel, out_shape=outs, in_specs=[pl.BlockSpec(memory_spac...  10.8 us
    all_to_all x1, starting transfers between devices, body(): lax.all_to_all(facets.reshape(64, 1, PER * 128), 'fluid', split_axis=0, c...  8.34 us
    ppermute x1, starting transfers between devices, body(): cor = lax.ppermute(cor, 'fluid', inward)  6.39 us
    all_to_all x1, waiting for transfers between devices, body(): lax.all_to_all(back, 'fluid', split_axis=0, concat_axis=0, tiled=True)  5.87 us
    all_to_all x1, waiting for transfers between devices, body(): lax.all_to_all(facets.reshape(64, 1, PER * 128), 'fluid', split_axis=0, c...  5.17 us
    all_to_all x1, starting transfers between devices, body(): lax.all_to_all(back, 'fluid', split_axis=0, concat_axis=0, tiled=True)  4.75 us
    ppermute x1, starting transfers between devices, body(): cor_planes = lax.ppermute(cor_planes, 'fluid', inward)  3.77 us
    ppermute x1, starting transfers between devices, body(): right = lax.ppermute(down, 'sect', backward)  2.81 us
  transfers between devices with their start and end apart: 9, of which 4 were waited for; matrix products, arithmetic and copies ran while one was open for 0% of the time, Pallas kernels for 11%

profile of v4, /device:TPU:1, one launch (start us, length us, event | category | flops | bytes accessed | tf_op | source)
XLA Modules:
  0.0 59.4 jit_solution(14213833266084787096)
XLA Ops:
  0.6 1.6 %prep.1 = (f32[5,4,64,128]{3,2,1,0:T(8,128)S(1)}, f32[2,64,128]{2,1,0:T(8,128)S(1)}, f32[24,128]{1,0:T(8,128)S(1)}, f32[24,128]{1,0:T(8,128)S(1)}, f32[16,256]{1...) custom-call(f32[4,64,128]{2,1,0:T(8,128)} %rho_hbm.1, f32[3,4,64,128]{3,2,1,0:T(8,128)} %vel_hbm.1, ...), custom_call_target="tpu_custom_call" | custom-call | flops 1000000 | bytes 1000000 | tf_op jit(solution)/shard_map/prep/pallas_call | solution.py:27
  2.2 2.7 %collective-permute-start = (f32[24,128]{1,0:T(8,128)S(1)}, f32[24,128]{1,0:T(8,128)S(1)}, u32[]{:S(2)}, u32[]{:S(2)}) collective-permute-start(f32[24,128]{1,0:T(8,128)S(1)} %get-tuple-element.25), channel_id=1, source_target_pairs={{0,252},{4,8},{8,4},{12,16},{16,12},{20,24},{24,20},{28,32},{32,28... | collective-permute-start | bytes 36872 | tf_op jit(solution)/shard_map/ppermute | solution.py:546
  4.9 6.4 %collective-permute-start.1 = (f32[24,128]{1,0:T(8,128)S(1)}, f32[24,128]{1,0:T(8,128)S(1)}, u32[]{:S(2)}, u32[]{:S(2)}) collective-permute-start(f32[24,128]{1,0:T(8,128)S(1)} %get-tuple-element.26), channel_id=1, source_target_pairs={{0,4},{4,0},{8,12},{12,8},{16,20},{20,16},{24,28},{28,24},{32,36},... | collective-permute-start | bytes 36872 | tf_op jit(solution)/shard_map/ppermute | solution.py:547
  11.9 0.4 tables.1
  12.4 0.0 collective-permute-done.ext_ref
  12.4 0.0 collective-permute-done.1.cor_ref
  12.4 0.1 middle.1
  12.5 2.8 %collective-permute-start.3 = (f32[120,128]{1,0:T(8,128)S(1)}, f32[120,128]{1,0:T(8,128)S(1)}, u32[]{:S(2)}, u32[]{:S(2)}) collective-permute-start(f32[120,128]{1,0:T(8,128)S(1)} %get-tuple-element.34), channel_id=1, source_target_pairs={{0,3},{1,0},{2,1},{3,2},{4,7},{5,4},{6,5},{7,6},{8,11},{9,8},{10,9... | collective-permute-start | bytes 184328 | tf_op jit(solution)/shard_map/ppermute | solution.py:563
  15.3 0.0 collective-permute-start.2
  15.3 1.6 %collective-permute-start.6 = (f32[16,128]{1,0:T(8,128)S(1)}, f32[16,128]{1,0:T(8,128)S(1)}, u32[]{:S(2)}, u32[]{:S(2)}) collective-permute-start(f32[16,128]{1,0:T(8,128)S(1)} %get-tuple-element.37), channel_id=1, source_target_pairs={{0,2},{1,3},{2,0},{3,1},{4,6},{5,7},{6,4},{7,5},{8,10},{9,11},{10,... | collective-permute-start | bytes 24584 | tf_op jit(solution)/shard_map/ppermute | solution.py:561
  17.0 2.4 %collective-permute-done.6.far_ref = f32[16,128]{1,0:T(8,128)S(1)} collective-permute-done((f32[16,128]{1,0:T(8,128)S(1)}, f32[16,128]{1,0:T(8,128)S(1)}, u32[]{:S(2)}, u32[]{:S(2)}) %collective-permute-start.6) | collective-permute-done | bytes 8224 | tf_op jit(solution)/shard_map/ppermute | solution.py:561
  19.4 0.0 collective-permute-done.3.right_ref
  19.4 0.3 collective-permute-done.2.left_ref
  19.7 1.7 %facets.1 = f32[448,128]{1,0:T(8,128)} custom-call(f32[120,128]{1,0:T(8,128)S(1)} %get-tuple-element.33.up_ref, f32[120,128]{1,0:T(8,128)S(1)} %collective-permute-done.2.left_ref, f32[120,128]{1,0:T(8,128)S(1)} %collective-permute-done.3.right_ref, f32[16,128]{1,0:T(8,128)S(1)} %collective-permute-done.6.far_ref, ...), custom_call_target="tpu_custom_call" | custom-call | flops 4000000 | bytes 1000000 | tf_op jit(solution)/shard_map/facets/pallas_call | solution.py:27
  21.4 8.3 %all-to-all-start = ((f32[64,1,896]{2,1,0:T(1,128)}), f32[64,1,896]{2,1,0:T(1,128)S(1)}, u32[]{:S(2)}, u32[]{:S(2)}) async-start(f32[64,1,896]{2,1,0:T(1,128)} %bitcast.15), calls=%async_computation | async-start | bytes 458752 | tf_op jit(solution)/shard_map/all_to_all | solution.py:573
  29.7 0.0 copy-start.1
  29.7 0.0 copy-start.2
  29.7 0.1 pack.1
  29.8 1.7 %collective-permute-start.4 = (f32[5,2,72,128]{3,2,1,0:T(8,128)S(1)}, f32[5,2,72,128]{3,2,1,0:T(8,128)S(1)}, u32[]{:S(2)}, u32[]{:S(2)}) collective-permute-start(f32[5,2,72,128]{3,2,1,0:T(8,128)S(1)} %get-tuple-element.35), channel_id=1, source_target_pairs={{0,252},{4,8},{8,4},{12,16},{16,12},{20,24},{24,20},{28,32},{32,28... | collective-permute-start | bytes 1105928 | tf_op jit(solution)/shard_map/ppermute | solution.py:583
  31.5 3.8 %collective-permute-start.5 = (f32[5,2,72,128]{3,2,1,0:T(8,128)S(1)}, f32[5,2,72,128]{3,2,1,0:T(8,128)S(1)}, u32[]{:S(2)}, u32[]{:S(2)}) collective-permute-start(f32[5,2,72,128]{3,2,1,0:T(8,128)S(1)} %get-tuple-element.36), channel_id=1, source_target_pairs={{0,4},{4,0},{8,12},{12,8},{16,20},{20,16},{24,28},{28,24},{32,36},... | collective-permute-start | bytes 1105928 | tf_op jit(solution)/shard_map/ppermute | solution.py:584
  36.0 0.0 copy-start
  36.0 0.0 copy-done.1
  36.0 0.0 copy-done.2
  36.0 0.7 %copy-done = f32[168]{0:T(256)S(1)} copy-done((f32[168]{0:T(256)S(1)}, f32[168]{0:T(256)}, u32[]{:S(2)}) %copy-start) | copy-done | bytes 696
  36.6 0.4 early_deck.1.early_ref
  37.1 5.2 %all-to-all-done = f32[64,1,896]{2,1,0:T(1,128)S(1)} async-done(((f32[64,1,896]{2,1,0:T(1,128)}), f32[64,1,896]{2,1,0:T(1,128)S(1)}, u32[]{:S(2)}, u32[]{:S(2)}) %all-to-all-start) | async-done | bytes 229408 | tf_op jit(solution)/shard_map/all_to_all | solution.py:573
  42.3 1.5 %deck.1 = (f32[64,128]{1,0:T(8,128)S(1)}, f32[64,2,128]{2,1,0:T(2,128)}) custom-call(f32[448,128]{1,0:T(8,128)S(1)} %bitcast.10, f32[4,80,256]{2,1,0:T(8,128)S(1)} %early_deck.1.early_ref), custom_call_target="tpu_custom_call" | custom-call | flops 4000000 | bytes 1000000 | tf_op jit(solution)/shard_map/deck/pallas_call | solution.py:27
  43.7 4.7 %all-to-all-start.1 = ((f32[64,2,128]{2,1,0:T(2,128)}), f32[64,2,128]{2,1,0:T(2,128)S(1)}, u32[]{:S(2)}, u32[]{:S(2)}) async-start(f32[64,2,128]{2,1,0:T(2,128)} %get-tuple-element.43), calls=%async_computation.1 | async-start | bytes 131072 | tf_op jit(solution)/shard_map/all_to_all | solution.py:593
  48.5 0.0 collective-permute-done.4.ext_ref
  48.5 0.0 collective-permute-done.5.cor_ref
  48.5 4.2 %bulk_euler.1 = (f32[5,4,64,128]{3,2,1,0:T(8,128)}, f32[64,128]{1,0:T(8,128)}) custom-call(f32[5,4,64,128]{3,2,1,0:T(8,128)S(1)} %get-tuple-element.24.raw_ref, f32[5,2,72,128]{3,2,1,0:T(8,128)S(1)} %collective-permute-done.4.ext_ref, f32[5,2,72,128]{3,2,1,0:T(8,128)S(1)} %collective-permute-done.5.cor_ref, f32[120,128]{1,0:T(8,128)S(1)} %collective-permute-done.2.left_ref, ...), custom_call_target="tpu_custom_call" | custom-call | flops 60000000 | bytes 1000000 | tf_op jit(solution)/shard_map/bulk_euler/pallas_call | solution.py:27
  52.7 5.9 %all-to-all-done.1 = f32[64,2,128]{2,1,0:T(2,128)S(1)} async-done(((f32[64,2,128]{2,1,0:T(2,128)}), f32[64,2,128]{2,1,0:T(2,128)S(1)}, u32[]{:S(2)}, u32[]{:S(2)}) %all-to-all-start.1) | async-done | bytes 65568 | tf_op jit(solution)/shard_map/all_to_all | solution.py:593
  58.6 0.8 %final.1 = f32[128,128]{1,0:T(8,128)} custom-call(f32[128,128]{1,0:T(8,128)S(1)} %bitcast.11, bf16[128,128]{1,0:T(8,128)(2,1)S(1)} %get-tuple-element.44.place_ref), custom_call_target="tpu_custom_call" | custom-call | flops 1000000 | bytes 1000000 | tf_op jit(solution)/shard_map/final/pallas_call | solution.py:27
Async XLA Ops:
  2.2 10.1 %collective-permute-start = (f32[24,128]{1,0:T(8,128)S(1)}, f32[24,128]{1,0:T(8,128)S(1)}, u32[]{:S(2)}, u32[]{:S(2)}) collective-permute-start(f32[24,128]{1,0:T(8,128)S(1)} %get-tuple-element.25), channel_id=1, source_target_pairs={{0,252},{4,8},{8,4},{12,16},{16,12},{20,24},{24,20},{28,32},{32,28... | collective-permute-start | bytes 36872 | tf_op jit(solution)/shard_map/ppermute | solution.py:546
  4.9 7.5 %collective-permute-start.1 = (f32[24,128]{1,0:T(8,128)S(1)}, f32[24,128]{1,0:T(8,128)S(1)}, u32[]{:S(2)}, u32[]{:S(2)}) collective-permute-start(f32[24,128]{1,0:T(8,128)S(1)} %get-tuple-element.26), channel_id=1, source_target_pairs={{0,4},{4,0},{8,12},{12,8},{16,20},{20,16},{24,28},{28,24},{32,36},... | collective-permute-start | bytes 36872 | tf_op jit(solution)/shard_map/ppermute | solution.py:547
  12.5 6.9 %collective-permute-start.3 = (f32[120,128]{1,0:T(8,128)S(1)}, f32[120,128]{1,0:T(8,128)S(1)}, u32[]{:S(2)}, u32[]{:S(2)}) collective-permute-start(f32[120,128]{1,0:T(8,128)S(1)} %get-tuple-element.34), channel_id=1, source_target_pairs={{0,3},{1,0},{2,1},{3,2},{4,7},{5,4},{6,5},{7,6},{8,11},{9,8},{10,9... | collective-permute-start | bytes 184328 | tf_op jit(solution)/shard_map/ppermute | solution.py:563
  15.3 4.4 %collective-permute-start.2 = (f32[120,128]{1,0:T(8,128)S(1)}, f32[120,128]{1,0:T(8,128)S(1)}, u32[]{:S(2)}, u32[]{:S(2)}) collective-permute-start(f32[120,128]{1,0:T(8,128)S(1)} %get-tuple-element.33.up_ref), channel_id=1, source_target_pairs={{0,1},{1,2},{2,3},{3,0},{4,5},{5,6},{6,7},{7,4},{8,9},{9,10},{10,1... | collective-permute-start | bytes 184328 | tf_op jit(solution)/shard_map/ppermute | solution.py:562
  15.3 4.1 %collective-permute-start.6 = (f32[16,128]{1,0:T(8,128)S(1)}, f32[16,128]{1,0:T(8,128)S(1)}, u32[]{:S(2)}, u32[]{:S(2)}) collective-permute-start(f32[16,128]{1,0:T(8,128)S(1)} %get-tuple-element.37), channel_id=1, source_target_pairs={{0,2},{1,3},{2,0},{3,1},{4,6},{5,7},{6,4},{7,5},{8,10},{9,11},{10,... | collective-permute-start | bytes 24584 | tf_op jit(solution)/shard_map/ppermute | solution.py:561
  21.4 20.9 %all-to-all-start = ((f32[64,1,896]{2,1,0:T(1,128)}), f32[64,1,896]{2,1,0:T(1,128)S(1)}, u32[]{:S(2)}, u32[]{:S(2)}) async-start(f32[64,1,896]{2,1,0:T(1,128)} %bitcast.15), calls=%async_computation | async-start | bytes 458752 | tf_op jit(solution)/shard_map/all_to_all | solution.py:573
  29.7 6.3 %copy-start.1 = (f32[168]{0:T(256)S(1)}, f32[168]{0:T(256)}, u32[]{:S(2)}) copy-start(f32[168]{0:T(256)} %param.19) | copy-start | bytes 2020
  29.7 6.3 %copy-start.2 = (s32[168]{0:T(256)S(1)}, s32[168]{0:T(256)}, u32[]{:S(2)}) copy-start(s32[168]{0:T(256)} %param.20) | copy-start | bytes 2020
  29.8 18.7 %collective-permute-start.4 = (f32[5,2,72,128]{3,2,1,0:T(8,128)S(1)}, f32[5,2,72,128]{3,2,1,0:T(8,128)S(1)}, u32[]{:S(2)}, u32[]{:S(2)}) collective-permute-start(f32[5,2,72,128]{3,2,1,0:T(8,128)S(1)} %get-tuple-element.35), channel_id=1, source_target_pairs={{0,252},{4,8},{8,4},{12,16},{16,12},{20,24},{24,20},{28,32},{32,28... | collective-permute-start | bytes 1105928 | tf_op jit(solution)/shard_map/ppermute | solution.py:583
  31.5 17.0 %collective-permute-start.5 = (f32[5,2,72,128]{3,2,1,0:T(8,128)S(1)}, f32[5,2,72,128]{3,2,1,0:T(8,128)S(1)}, u32[]{:S(2)}, u32[]{:S(2)}) collective-permute-start(f32[5,2,72,128]{3,2,1,0:T(8,128)S(1)} %get-tuple-element.36), channel_id=1, source_target_pairs={{0,4},{4,0},{8,12},{12,8},{16,20},{20,16},{24,28},{28,24},{32,36},... | collective-permute-start | bytes 1105928 | tf_op jit(solution)/shard_map/ppermute | solution.py:584
  36.0 0.7 %copy-start = (f32[168]{0:T(256)S(1)}, f32[168]{0:T(256)}, u32[]{:S(2)}) copy-start(f32[168]{0:T(256)} %param.18) | copy-start | bytes 2020
  43.7 14.8 %all-to-all-start.1 = ((f32[64,2,128]{2,1,0:T(2,128)}), f32[64,2,128]{2,1,0:T(2,128)S(1)}, u32[]{:S(2)}, u32[]{:S(2)}) async-start(f32[64,2,128]{2,1,0:T(2,128)} %get-tuple-element.43), calls=%async_computation.1 | async-start | bytes 131072 | tf_op jit(solution)/shard_map/all_to_all | solution.py:593
